TPU v7x, 32 devices: a whole 2x2x4 slice. The times are simulated.
32 devices in a mesh: pipe: 4 (over y, x), dp: 8 (over z, core).
Axes of the slice: x: 2, y: 2, z: 4, core: 2. Of those that a mesh axis runs over, the one named last changes fastest.
Arguments:
- x_big: bfloat16 [4, 8, 14, 14, 1024], P(None, 'dp'), may hold values from -6 to 6
- x_small: bfloat16 [4, 16, 6, 6, 1024], P(None, 'dp'), may hold values from -6 to 6
- cot_big: bfloat16 [4, 8, 7, 7, 2048], P(None, 'dp'), may hold values from -6 to 6
- cot_small: bfloat16 [4, 16, 3, 3, 2048], P(None, 'dp'), may hold values from -6 to 6
- section_weights: bfloat16 [4, 4456448], P('pipe'), may hold values from -0.1875 to 0.1875
- section_norms: float32 [4, 4, 4096], P('pipe'), may hold values from 0.5 to 1.5
- gate_big: int32 [4, 8], P(None, 'dp'), may hold values 0 or 1
- gate_small: int32 [4, 16], P(None, 'dp'), may hold values 0 or 1
- width_step: int32 [4], replicated, may hold values from 1 to 4
Outputs:
- out_big: bfloat16 [4, 8, 7, 7, 2048], P('pipe', 'dp')
- out_small: bfloat16 [4, 16, 3, 3, 2048], P('pipe', 'dp')
- grad_big: bfloat16 [4, 8, 14, 14, 1024], P('pipe', 'dp')
- grad_small: bfloat16 [4, 16, 6, 6, 1024], P('pipe', 'dp')
- weight_grads: float32 [4, 4456448], P('pipe', 'dp')
- norm_grads: float32 [4, 4, 4096], P('pipe')
Inputs may be any that keep to these rules, and one draw needn't show every extreme that they name: `gate_big`: 1 keeps the crop's identity-block branch, 0 skips it. `gate_small`: 1 keeps the crop's identity-block branch, 0 skips it. The 96-pixel crops of micro-batch m use the first 512 * width_step[m] / 4 bottleneck channels.
All inputs are finite; a program needn't handle non-finite values.
Results may differ from a plain program's by a relative error of at most 0.017.
Values may be sent and summed in bfloat16 or wider, within the bound.
A program may use at most 576 MiB of HBM per device.

v0:
```python
from functools import partial

import jax
import jax.numpy as jnp
from jax import lax
from jax.sharding import PartitionSpec as P

C_IN = 1024
C_MID = 512
C_OUT = 2048


EPS = 1e-05


def for_sending(array):
    return jax.tree.map(lambda a: a.astype(jnp.bfloat16) if a.dtype == jnp.float32 else a, array)


def from_behind(value, axis, steps):
    count = lax.axis_size(axis)
    first, last = (max(0, -steps), min(count, count - steps))
    return lax.ppermute(value, axis, [(source, source + steps) for source in range(first, last)])


def silu_slope(values):
    sigmoid_v = jax.nn.sigmoid(values)
    return sigmoid_v * (1.0 + values * (1.0 - sigmoid_v))


def pointwise(inputs, weight):
    return jnp.einsum("nhwc,cd->nhwd", inputs, weight, preferred_element_type=jnp.float32)


def pointwise_back(inputs, upstream, weight):
    w_grad = jnp.einsum("nhwc,nhwd->cd", inputs, upstream, preferred_element_type=jnp.float32)
    in_grad = jnp.einsum("nhwd,cd->nhwc", upstream, weight, preferred_element_type=jnp.float32)
    return (w_grad, in_grad)


def stacked_taps(inputs, stride):
    extent = inputs.shape[1]
    span_len = stride * ((extent - 1) // stride) + 1
    padded = jnp.pad(inputs, ((0, 0), (1, 1), (1, 1), (0, 0)))
    return jnp.stack(
        [
            padded[
                :, tap_row : tap_row + span_len : stride, tap_col : tap_col + span_len : stride, :
            ]
            for tap_row in range(3)
            for tap_col in range(3)
        ]
    )


def spatial(windows, weight):
    return jnp.einsum("knhwc,kcd->nhwd", windows, weight, preferred_element_type=jnp.float32)


def spatial_back(windows, upstream, weight, extent, stride):
    w_grad = jnp.einsum("knhwc,nhwd->kcd", windows, upstream, preferred_element_type=jnp.float32)
    tap_grads = jnp.einsum("nhwd,kcd->knhwc", upstream, weight, preferred_element_type=jnp.float32)
    span_len = stride * (upstream.shape[1] - 1) + 1
    summed = jnp.zeros((upstream.shape[0], extent + 2, extent + 2, weight.shape[1]), jnp.float32)
    for tap_row in range(3):
        for tap_col in range(3):
            config = (
                (0, 0, 0),
                (tap_row, extent + 2 - tap_row - span_len, stride - 1),
                (tap_col, extent + 2 - tap_col - span_len, stride - 1),
                (0, 0, 0),
            )
            summed = summed + lax.pad(tap_grads[tap_row * 3 + tap_col], jnp.float32(0.0), config)
    return (w_grad, summed[:, 1:-1, 1:-1, :])


def place_at(paired, offset, width_all):
    return jnp.pad(paired, ((0, 0), (offset, width_all - offset - paired.shape[1])))


def moments_of(values, offset, width_all):
    paired = jnp.stack([jnp.sum(values, axis=(0, 1, 2)), jnp.sum(values * values, axis=(0, 1, 2))])
    return place_at(paired, offset, width_all)


def grad_moments(upstream, centered, offset, width_all):
    paired = jnp.stack(
        [jnp.sum(upstream, axis=(0, 1, 2)), jnp.sum(upstream * centered, axis=(0, 1, 2))]
    )
    return place_at(paired, offset, width_all)


def norm_apply(values, totals, norm_table, gain_row, offset, members):
    width = values.shape[-1]
    mean_v = totals[0, offset : offset + width] / members
    var_v = totals[1, offset : offset + width] / members - mean_v * mean_v
    rstd_v = lax.rsqrt(var_v + EPS)
    centered = (values - mean_v) * rstd_v
    gain_v = norm_table[gain_row, offset : offset + width]
    normed = centered * gain_v + norm_table[gain_row + 1, offset : offset + width]
    return (normed, centered, rstd_v * gain_v)


def norm_back(upstream, centered, factor, backs, offset, members):
    width = upstream.shape[-1]
    return factor * (
        upstream
        - backs[0, offset : offset + width] / members
        - centered * (backs[1, offset : offset + width] / members)
    )


def section_mats(weight_row, section_id):
    if section_id == 0:
        return (weight_row[: C_IN * C_MID].reshape(C_IN, C_MID),)
    if section_id == 1:
        return (weight_row[: 9 * C_MID * C_MID].reshape(9, C_MID, C_MID),)
    if section_id == 2:
        split_at = C_MID * C_OUT
        return (
            weight_row[:split_at].reshape(C_MID, C_OUT),
            weight_row[split_at : split_at + C_IN * C_OUT].reshape(C_IN, C_OUT),
        )
    begin_b = C_OUT * C_MID
    begin_c = begin_b + 9 * C_MID * C_MID
    return (
        weight_row[:begin_b].reshape(C_OUT, C_MID),
        weight_row[begin_b:begin_c].reshape(9, C_MID, C_MID),
        weight_row[begin_c : begin_c + C_MID * C_OUT].reshape(C_MID, C_OUT),
    )


def add_into(accum, w_grad, offset):
    flat_grad = w_grad.reshape(-1)
    current = accum[offset : offset + flat_grad.shape[0]]
    return lax.dynamic_update_slice_in_dim(accum, current + flat_grad, offset, 0)


def fill_to(values, width):
    return jnp.pad(values, ((0, 0), (0, width - values.shape[1])))


def store_at(store, values, index_m, valid):
    previous = lax.dynamic_index_in_dim(store, index_m, 0, keepdims=False)
    return lax.dynamic_update_index_in_dim(store, jnp.where(valid, values, previous), index_m, 0)


def pack_parts(parts):
    return jnp.concatenate([part.reshape(-1) for part in parts])


def unpack_parts(packed, shapes):
    pieces, start = ([], 0)
    for shape_v in shapes:
        length = shape_v[0] * shape_v[1]
        pieces.append(packed[start : start + length].reshape(shape_v))
        start = start + length
    return tuple(pieces)


def make_contexts(images_all, width_step, index_m, replicas):
    steps_now = lax.dynamic_index_in_dim(width_step, index_m, 0, keepdims=False)
    keep_small = (jnp.arange(C_MID) < C_MID * steps_now // 4).astype(jnp.float32)
    keeps = (jnp.ones((C_MID,), jnp.float32), keep_small)
    return tuple(
        (
            (
                images.shape[2],
                images.shape[2] // 2,
                keeps[part_id],
                2 * part_id,
                images.shape[1] * replicas,
            )
            for part_id, images in enumerate(images_all)
        )
    )


def forward_group(
    section_id, phase_id, weight_row, norm_table, context, holding, incoming, images, gate_v, totals
):
    s_in, s_out, keep_mask, gain_row, members = context
    buf_one, buf_two, outgoing, result = holding
    samples = images.shape[0]
    flat_len = buf_one.shape[1]
    inner_len = s_out * s_out * C_MID
    area_in = members * s_in * s_in
    area_out = members * s_out * s_out
    width_all = norm_table.shape[1]
    moments = jnp.zeros((2, width_all), jnp.float32)
    matrices = section_mats(weight_row, section_id)
    grid_in = (samples, s_in, s_in)
    grid_out = (samples, s_out, s_out)
    if section_id == 0 and phase_id == 0:
        pre_one = pointwise(images, matrices[0])
        buf_one = pre_one.reshape(samples, flat_len)
        moments = moments_of(pre_one, 0, width_all)
    elif section_id == 0 and phase_id == 1:
        normed = norm_apply(
            buf_one.reshape(grid_in + (C_MID,)), totals[0], norm_table, gain_row, 0, area_in
        )[0]
        outgoing = (jax.nn.silu(normed) * keep_mask).astype(jnp.bfloat16).reshape(samples, flat_len)
    elif section_id == 1 and phase_id == 0:
        inputs = incoming.reshape(grid_in + (C_MID,))
        pre_two = spatial(stacked_taps(inputs, 2), matrices[0])
        buf_one = fill_to(pre_two.reshape(samples, inner_len), flat_len)
        moments = moments_of(pre_two, 0, width_all)
    elif section_id == 1 and phase_id == 1:
        pre_two = buf_one[:, :inner_len].reshape(grid_out + (C_MID,))
        normed = norm_apply(pre_two, totals[0], norm_table, gain_row, 0, area_out)[0]
        acts_two = (jax.nn.silu(normed) * keep_mask).astype(jnp.bfloat16)
        outgoing = fill_to(acts_two.reshape(samples, inner_len), flat_len)
    elif section_id == 2 and phase_id == 0:
        inputs = incoming[:, :inner_len].reshape(grid_out + (C_MID,))
        main_pre = pointwise(inputs, matrices[0])
        short_pre = pointwise(images[:, ::2, ::2, :], matrices[1])
        buf_one = main_pre.reshape(samples, flat_len)
        buf_two = short_pre.reshape(samples, flat_len)
        moments = moments_of(main_pre, 0, width_all) + moments_of(short_pre, C_OUT, width_all)
    elif section_id == 2 and phase_id == 1:
        main_pre = buf_one.reshape(grid_out + (C_OUT,))
        short_pre = buf_two.reshape(grid_out + (C_OUT,))
        joined = (
            norm_apply(main_pre, totals[0], norm_table, gain_row, 0, area_out)[0]
            + norm_apply(short_pre, totals[0], norm_table, gain_row, C_OUT, area_out)[0]
        )
        outgoing = jax.nn.silu(joined).astype(jnp.bfloat16).reshape(samples, flat_len)
    elif section_id == 3 and phase_id == 0:
        inputs = incoming.reshape(grid_out + (C_OUT,))
        pre_a = pointwise(inputs, matrices[0])
        buf_one = fill_to(pre_a.reshape(samples, inner_len), flat_len)
        moments = moments_of(pre_a, 0, width_all)
    elif section_id == 3 and phase_id == 1:
        pre_a = buf_one[:, :inner_len].reshape(grid_out + (C_MID,))
        normed = norm_apply(pre_a, totals[0], norm_table, gain_row, 0, area_out)[0]
        hidden = (jax.nn.silu(normed) * keep_mask).astype(jnp.bfloat16)
        pre_b = spatial(stacked_taps(hidden, 1), matrices[1])
        buf_one = fill_to(pre_b.reshape(samples, inner_len), flat_len)
        moments = moments_of(pre_b, C_MID, width_all)
    elif section_id == 3 and phase_id == 2:
        pre_b = buf_one[:, :inner_len].reshape(grid_out + (C_MID,))
        normed = norm_apply(pre_b, totals[1], norm_table, gain_row, C_MID, area_out)[0]
        hidden = (jax.nn.silu(normed) * keep_mask).astype(jnp.bfloat16)
        pre_c = pointwise(hidden, matrices[2])
        buf_one = pre_c.reshape(samples, flat_len)
        moments = moments_of(pre_c, 2 * C_MID, width_all)
    elif section_id == 3 and phase_id == 3:
        pre_c = buf_one.reshape(grid_out + (C_OUT,))
        branch = norm_apply(pre_c, totals[2], norm_table, gain_row, 2 * C_MID, area_out)[0]
        inputs = incoming.reshape(grid_out + (C_OUT,)).astype(jnp.float32)
        result = jax.nn.silu(inputs + gate_v[:, None, None, None] * branch)
    return ((buf_one, buf_two, outgoing, result), moments)


def forward_branch(section_id, phase_id, weight_row, norm_table, contexts, operand):
    holding, received, images_now, gates_now, totals = operand
    new_holding, all_moments = ([], [])
    for context, state_v, incoming, images, gate_v, sums in zip(
        contexts, holding, received, images_now, gates_now, totals
    ):
        state_v, moments = forward_group(
            section_id,
            phase_id,
            weight_row,
            norm_table,
            context,
            state_v,
            incoming,
            images,
            gate_v,
            sums,
        )
        new_holding.append(state_v)
        all_moments.append(moments)
    return (tuple(new_holding), tuple(all_moments))


def spare_forward(width_all, operand):
    holding = operand[0]
    return (holding, tuple((jnp.zeros((2, width_all), jnp.float32) for state_v in holding)))


def backward_group(
    section_id,
    phase_id,
    weight_row,
    norm_table,
    context,
    holding,
    accum,
    stored,
    images,
    gate_v,
    upstream,
    totals,
    backs,
):
    s_in, s_out, keep_mask, gain_row, members = context
    buf_one, buf_two, buf_three, outgoing, in_grads = holding
    samples = images.shape[0]
    flat_len = buf_one.shape[1]
    inner_len = s_out * s_out * C_MID
    area_in = members * s_in * s_in
    area_out = members * s_out * s_out
    width_all = norm_table.shape[1]
    moments = jnp.zeros((2, width_all), jnp.float32)
    matrices = section_mats(weight_row, section_id)
    grid_in = (samples, s_in, s_in)
    grid_out = (samples, s_out, s_out)
    if section_id == 0 and phase_id < 2:
        if phase_id == 0:
            pre_one = pointwise(images, matrices[0])
        else:
            pre_one = buf_one.reshape(grid_in + (C_MID,))
        normed, centered, factor = norm_apply(pre_one, totals[0], norm_table, gain_row, 0, area_in)
        if phase_id == 0:
            slope = (
                upstream.reshape(grid_in + (C_MID,)).astype(jnp.float32)
                * keep_mask
                * silu_slope(normed)
            )
            buf_one = pre_one.reshape(samples, flat_len)
            buf_two = slope.reshape(samples, flat_len)
            moments = grad_moments(slope, centered, 0, width_all)
        else:
            slope = buf_two.reshape(grid_in + (C_MID,))
            pre_grad = norm_back(slope, centered, factor, backs[0], 0, area_in).astype(jnp.bfloat16)
            w_grad, x_grad = pointwise_back(images, pre_grad, matrices[0])
            accum = add_into(accum, w_grad, 0)
            in_grads = in_grads + x_grad
    elif section_id == 1 and phase_id < 2:
        windows = stacked_taps(stored.reshape(grid_in + (C_MID,)), 2)
        if phase_id == 0:
            pre_two = spatial(windows, matrices[0])
        else:
            pre_two = buf_one[:, :inner_len].reshape(grid_out + (C_MID,))
        normed, centered, factor = norm_apply(pre_two, totals[0], norm_table, gain_row, 0, area_out)
        if phase_id == 0:
            slope = (
                upstream[:, :inner_len].reshape(grid_out + (C_MID,)).astype(jnp.float32)
                * keep_mask
                * silu_slope(normed)
            )
            buf_one = fill_to(pre_two.reshape(samples, inner_len), flat_len)
            buf_two = fill_to(slope.reshape(samples, inner_len), flat_len)
            moments = grad_moments(slope, centered, 0, width_all)
        else:
            slope = buf_two[:, :inner_len].reshape(grid_out + (C_MID,))
            pre_grad = norm_back(slope, centered, factor, backs[0], 0, area_out).astype(
                jnp.bfloat16
            )
            w_grad, act_grad = spatial_back(windows, pre_grad, matrices[0], s_in, 2)
            accum = add_into(accum, w_grad, 0)
            outgoing = act_grad.astype(jnp.bfloat16).reshape(samples, flat_len)
    elif section_id == 2 and phase_id < 2:
        inputs = stored[:, :inner_len].reshape(grid_out + (C_MID,))
        subsampled = images[:, ::2, ::2, :]
        if phase_id == 0:
            main_pre = pointwise(inputs, matrices[0])
            short_pre = pointwise(subsampled, matrices[1])
        else:
            main_pre = buf_one.reshape(grid_out + (C_OUT,))
            short_pre = buf_two.reshape(grid_out + (C_OUT,))
        main_n, main_c, main_f = norm_apply(main_pre, totals[0], norm_table, gain_row, 0, area_out)
        short_n, short_c, short_f = norm_apply(
            short_pre, totals[0], norm_table, gain_row, C_OUT, area_out
        )
        if phase_id == 0:
            slope = upstream.reshape(grid_out + (C_OUT,)).astype(jnp.float32) * silu_slope(
                main_n + short_n
            )
            buf_one = main_pre.reshape(samples, flat_len)
            buf_two = short_pre.reshape(samples, flat_len)
            buf_three = slope.reshape(samples, flat_len)
            moments = grad_moments(slope, main_c, 0, width_all) + grad_moments(
                slope, short_c, C_OUT, width_all
            )
        else:
            slope = buf_three.reshape(grid_out + (C_OUT,))
            main_grad = norm_back(slope, main_c, main_f, backs[0], 0, area_out).astype(jnp.bfloat16)
            short_grad = norm_back(slope, short_c, short_f, backs[0], C_OUT, area_out).astype(
                jnp.bfloat16
            )
            w_main, act_grad = pointwise_back(inputs, main_grad, matrices[0])
            w_short, sub_grad = pointwise_back(subsampled, short_grad, matrices[1])
            accum = add_into(accum, w_main, 0)
            accum = add_into(accum, w_short, C_MID * C_OUT)
            outgoing = fill_to(act_grad.astype(jnp.bfloat16).reshape(samples, inner_len), flat_len)
            in_grads = in_grads + lax.pad(
                sub_grad, jnp.float32(0.0), ((0, 0, 0), (0, 1, 1), (0, 1, 1), (0, 0, 0))
            )
    elif section_id == 3:
        inputs = stored.reshape(grid_out + (C_OUT,))
        gate_four = gate_v[:, None, None, None]
        begin_b = C_OUT * C_MID
        begin_c = begin_b + 9 * C_MID * C_MID
        if phase_id == 0:
            pre_a = pointwise(inputs, matrices[0])
            norm_a = norm_apply(pre_a, totals[0], norm_table, gain_row, 0, area_out)[0]
            hidden_a = (jax.nn.silu(norm_a) * keep_mask).astype(jnp.bfloat16)
            pre_b = spatial(stacked_taps(hidden_a, 1), matrices[1])
            norm_b = norm_apply(pre_b, totals[1], norm_table, gain_row, C_MID, area_out)[0]
            hidden_b = (jax.nn.silu(norm_b) * keep_mask).astype(jnp.bfloat16)
            pre_c = pointwise(hidden_b, matrices[2])
            norm_c, cent_c, fac_c = norm_apply(
                pre_c, totals[2], norm_table, gain_row, 2 * C_MID, area_out
            )
            slope = upstream.reshape(grid_out + (C_OUT,)).astype(jnp.float32) * silu_slope(
                inputs.astype(jnp.float32) + gate_four * norm_c
            )
            buf_one = pre_c.reshape(samples, flat_len)
            buf_two = slope.reshape(samples, flat_len)
            buf_three = fill_to(
                jnp.concatenate(
                    [pre_a.reshape(samples, inner_len), pre_b.reshape(samples, inner_len)], axis=1
                ),
                flat_len,
            )
            moments = grad_moments(gate_four * slope, cent_c, 2 * C_MID, width_all)
        else:
            pre_a = buf_three[:, :inner_len].reshape(grid_out + (C_MID,))
            pre_b = buf_three[:, inner_len : 2 * inner_len].reshape(grid_out + (C_MID,))
            middle = buf_three[:, 2 * inner_len : 3 * inner_len].reshape(grid_out + (C_MID,))
            if phase_id == 1:
                slope = buf_two.reshape(grid_out + (C_OUT,))
                norm_c, cent_c, fac_c = norm_apply(
                    buf_one.reshape(grid_out + (C_OUT,)),
                    totals[2],
                    norm_table,
                    gain_row,
                    2 * C_MID,
                    area_out,
                )
                norm_b, cent_b, fac_b = norm_apply(
                    pre_b, totals[1], norm_table, gain_row, C_MID, area_out
                )
                hidden_b = (jax.nn.silu(norm_b) * keep_mask).astype(jnp.bfloat16)
                grad_c = norm_back(
                    gate_four * slope, cent_c, fac_c, backs[0], 2 * C_MID, area_out
                ).astype(jnp.bfloat16)
                w_widen, hid_grad = pointwise_back(hidden_b, grad_c, matrices[2])
                middle = hid_grad * keep_mask * silu_slope(norm_b)
                buf_three = lax.dynamic_update_slice_in_dim(
                    buf_three, middle.reshape(samples, inner_len), 2 * inner_len, 1
                )
                moments = grad_moments(middle, cent_b, C_MID, width_all)
                accum = add_into(accum, w_widen, begin_c)
            elif phase_id == 2:
                norm_b, cent_b, fac_b = norm_apply(
                    pre_b, totals[1], norm_table, gain_row, C_MID, area_out
                )
                grad_b = norm_back(middle, cent_b, fac_b, backs[1], C_MID, area_out).astype(
                    jnp.bfloat16
                )
                norm_a, cent_a, fac_a = norm_apply(
                    pre_a, totals[0], norm_table, gain_row, 0, area_out
                )
                hidden_a = (jax.nn.silu(norm_a) * keep_mask).astype(jnp.bfloat16)
                w_spatial, hid_grad = spatial_back(
                    stacked_taps(hidden_a, 1), grad_b, matrices[1], s_out, 1
                )
                middle = hid_grad * keep_mask * silu_slope(norm_a)
                buf_three = lax.dynamic_update_slice_in_dim(
                    buf_three, middle.reshape(samples, inner_len), 2 * inner_len, 1
                )
                moments = grad_moments(middle, cent_a, 0, width_all)
                accum = add_into(accum, w_spatial, begin_b)
            else:
                norm_a, cent_a, fac_a = norm_apply(
                    pre_a, totals[0], norm_table, gain_row, 0, area_out
                )
                grad_a = norm_back(middle, cent_a, fac_a, backs[2], 0, area_out).astype(
                    jnp.bfloat16
                )
                w_narrow, y_grad = pointwise_back(inputs, grad_a, matrices[0])
                y_grad = y_grad + buf_two.reshape(grid_out + (C_OUT,))
                outgoing = y_grad.astype(jnp.bfloat16).reshape(samples, flat_len)
                accum = add_into(accum, w_narrow, 0)
    return ((buf_one, buf_two, buf_three, outgoing, in_grads), accum, moments)


def backward_branch(section_id, phase_id, weight_row, norm_table, contexts, operand):
    holding, accum, stored_now, images_now, gates_now, upstream_now, totals, backs = operand
    new_holding, all_moments = ([], [])
    for context, state_v, stored, images, gate_v, upstream, sums, back_sums in zip(
        contexts, holding, stored_now, images_now, gates_now, upstream_now, totals, backs
    ):
        state_v, accum, moments = backward_group(
            section_id,
            phase_id,
            weight_row,
            norm_table,
            context,
            state_v,
            accum,
            stored,
            images,
            gate_v,
            upstream,
            sums,
            back_sums,
        )
        new_holding.append(state_v)
        all_moments.append(moments)
    return (tuple(new_holding), accum, tuple(all_moments))


def spare_backward(width_all, operand):
    holding, accum = (operand[0], operand[1])
    return (holding, accum, tuple((jnp.zeros((2, width_all), jnp.float32) for state_v in holding)))


def on_device(
    x_big,
    x_small,
    cot_big,
    cot_small,
    section_weights,
    section_norms,
    gate_big,
    gate_small,
    width_step,
):
    micro = x_big.shape[0]
    sections = lax.axis_size("pipe")
    replicas = lax.axis_size("dp")
    section_id = lax.axis_index("pipe")
    weight_row = section_weights[0]
    norm_table = section_norms[0]
    width_all = norm_table.shape[1]
    images_all = (x_big, x_small)
    cotangents = (cot_big, cot_small)
    gates_all = (gate_big.astype(jnp.float32), gate_small.astype(jnp.float32))
    shapes = tuple(
        ((images.shape[1], images.shape[2] * images.shape[2] * C_MID) for images in images_all)
    )
    ticks = micro + sections - 1
    received = tuple((jnp.zeros(shape_v, jnp.bfloat16) for shape_v in shapes))
    kept_inputs = tuple((jnp.zeros((micro,) + shape_v, jnp.bfloat16) for shape_v in shapes))
    kept_totals = tuple((jnp.zeros((micro, 3, 2, width_all), jnp.float32) for shape_v in shapes))
    finals = tuple(
        (
            jnp.zeros(
                (micro, images.shape[1], images.shape[2] // 2, images.shape[2] // 2, C_OUT),
                jnp.float32,
            )
            for images in images_all
        )
    )
    for tick in range(ticks):
        position = tick - section_id
        valid = (position >= 0) & (position < micro)
        index_m = jnp.clip(position, 0, micro - 1)
        chooser = jnp.where(valid, section_id, sections)
        contexts = make_contexts(images_all, width_step, index_m, replicas)
        forward_fns = [
            [
                partial(forward_branch, sid, phase_id, weight_row, norm_table, contexts)
                for sid in range(4)
            ]
            + [partial(spare_forward, width_all)]
            for phase_id in range(4)
        ]
        images_now = tuple(
            (lax.dynamic_index_in_dim(images, index_m, 0, keepdims=False) for images in images_all)
        )
        gates_now = tuple(
            (lax.dynamic_index_in_dim(gates, index_m, 0, keepdims=False) for gates in gates_all)
        )
        kept_inputs = tuple(
            (
                store_at(store, incoming, index_m, valid)
                for store, incoming in zip(kept_inputs, received)
            )
        )
        holding = tuple(
            (
                (
                    jnp.zeros(shape_v, jnp.float32),
                    jnp.zeros(shape_v, jnp.float32),
                    jnp.zeros(shape_v, jnp.bfloat16),
                    jnp.zeros(store.shape[1:], jnp.float32),
                )
                for shape_v, store in zip(shapes, finals)
            )
        )
        totals = tuple(
            (
                tuple((jnp.zeros((2, width_all), jnp.float32) for slot in range(3)))
                for shape_v in shapes
            )
        )
        for phase_id in range(4):
            holding, moments = lax.switch(
                chooser, forward_fns[phase_id], (holding, received, images_now, gates_now, totals)
            )
            if phase_id < 3:
                summed = lax.psum(moments, "dp")
                totals = tuple(
                    (
                        tuple(
                            (
                                summed[part_id] if slot == phase_id else sums[slot]
                                for slot in range(3)
                            )
                        )
                        for part_id, sums in enumerate(totals)
                    )
                )
        kept_totals = tuple(
            (
                store_at(store, jnp.stack(sums), index_m, valid)
                for store, sums in zip(kept_totals, totals)
            )
        )
        finals = tuple(
            (store_at(store, state_v[3], index_m, valid) for store, state_v in zip(finals, holding))
        )
        moved = from_behind(for_sending(pack_parts([state_v[2] for state_v in holding])), "pipe", 1)
        received = unpack_parts(moved, shapes)
    grads_in = tuple((jnp.zeros(shape_v, jnp.bfloat16) for shape_v in shapes))
    accum = jnp.zeros(weight_row.shape, jnp.float32)
    norm_sum = jnp.zeros((4, width_all), jnp.float32)
    input_grads = tuple(
        (
            jnp.zeros(images.shape[:2] + images.shape[2:4] + (C_IN,), jnp.float32)
            for images in images_all
        )
    )
    for tick in range(ticks):
        position = tick - (sections - 1 - section_id)
        valid = (position >= 0) & (position < micro)
        index_m = jnp.clip(position, 0, micro - 1)
        chooser = jnp.where(valid, section_id, sections)
        contexts = make_contexts(images_all, width_step, index_m, replicas)
        backward_fns = [
            [
                partial(backward_branch, sid, phase_id, weight_row, norm_table, contexts)
                for sid in range(4)
            ]
            + [partial(spare_backward, width_all)]
            for phase_id in range(4)
        ]
        images_now = tuple(
            (lax.dynamic_index_in_dim(images, index_m, 0, keepdims=False) for images in images_all)
        )
        gates_now = tuple(
            (lax.dynamic_index_in_dim(gates, index_m, 0, keepdims=False) for gates in gates_all)
        )
        stored_now = tuple(
            (lax.dynamic_index_in_dim(store, index_m, 0, keepdims=False) for store in kept_inputs)
        )
        totals = tuple(
            (
                tuple(
                    (
                        lax.dynamic_index_in_dim(store, index_m, 0, keepdims=False)[slot]
                        for slot in range(3)
                    )
                )
                for store in kept_totals
            )
        )
        upstream_now = tuple(
            (
                jnp.where(
                    section_id == sections - 1,
                    lax.dynamic_index_in_dim(cot, index_m, 0, keepdims=False).reshape(shape_v),
                    grad_v,
                )
                for cot, shape_v, grad_v in zip(cotangents, shapes, grads_in)
            )
        )
        holding = tuple(
            (
                (
                    jnp.zeros(shape_v, jnp.float32),
                    jnp.zeros(shape_v, jnp.float32),
                    jnp.zeros(shape_v, jnp.float32),
                    jnp.zeros(shape_v, jnp.bfloat16),
                    jnp.zeros(store.shape[1:], jnp.float32),
                )
                for shape_v, store in zip(shapes, input_grads)
            )
        )
        backs = tuple(
            (
                tuple((jnp.zeros((2, width_all), jnp.float32) for slot in range(3)))
                for shape_v in shapes
            )
        )
        for phase_id in range(4):
            holding, accum, moments = lax.switch(
                chooser,
                backward_fns[phase_id],
                (holding, accum, stored_now, images_now, gates_now, upstream_now, totals, backs),
            )
            if phase_id < 3:
                summed = lax.psum(moments, "dp")
                backs = tuple(
                    (
                        tuple(
                            (
                                summed[part_id] if slot == phase_id else sums[slot]
                                for slot in range(3)
                            )
                        )
                        for part_id, sums in enumerate(backs)
                    )
                )
                norm_sum = norm_sum + jnp.stack(
                    [summed[0][1], summed[0][0], summed[1][1], summed[1][0]]
                )
        input_grads = tuple(
            (
                store_at(store, state_v[4], index_m, valid)
                for store, state_v in zip(input_grads, holding)
            )
        )
        moved = from_behind(
            for_sending(pack_parts([state_v[3] for state_v in holding])), "pipe", -1
        )
        grads_in = unpack_parts(moved, shapes)
    weight_part = lax.psum_scatter(accum, "dp", scatter_dimension=0, tiled=True)
    returned = (
        lax.psum_scatter(
            input_grads[0].astype(jnp.bfloat16), "pipe", scatter_dimension=0, tiled=True
        ).astype(jnp.float32),
        lax.psum_scatter(
            input_grads[1].astype(jnp.bfloat16), "pipe", scatter_dimension=0, tiled=True
        ).astype(jnp.float32),
        lax.psum_scatter(
            finals[0].astype(jnp.bfloat16), "pipe", scatter_dimension=0, tiled=True
        ).astype(jnp.float32),
        lax.psum_scatter(
            finals[1].astype(jnp.bfloat16), "pipe", scatter_dimension=0, tiled=True
        ).astype(jnp.float32),
    )
    return (
        returned[2].astype(jnp.bfloat16),
        returned[3].astype(jnp.bfloat16),
        returned[0].astype(jnp.bfloat16),
        returned[1].astype(jnp.bfloat16),
        weight_part[None],
        norm_sum[None],
    )


def solution(mesh):
    placed = (
        P(None, "dp", None, None, None),
        P(None, "dp", None, None, None),
        P(None, "dp", None, None, None),
        P(None, "dp", None, None, None),
        P("pipe", None),
        P("pipe", None, None),
        P(None, "dp"),
        P(None, "dp"),
        P(),
    )
    return jax.shard_map(
        on_device,
        mesh=mesh,
        in_specs=placed,
        out_specs=(
            P("pipe", "dp", None, None, None),
            P("pipe", "dp", None, None, None),
            P("pipe", "dp", None, None, None),
            P("pipe", "dp", None, None, None),
            P("pipe", "dp"),
            P("pipe", None, None),
        ),
        check_vma=False,
    )
```

profile of v0, /device:TPU:0, one launch (start us, length us, event | category | flops | bytes accessed | tf_op | source)
XLA Modules:
  0.0 5490.6 jit_solution(2139420625093624486)
XLA Ops:
  7.2 189.4 %reduce.643 = bf16[4456448]{0:T(1024)(128)(2,1)} reduce(bf16[1,4456448]{1,0:T(2,128)(2,1)} %param.293, bf16[]{:T(256)} %constant.5476), dimensions={0}, to_apply=%param.293.reduce_sub_computation | reduce | bytes 17825794 | tf_op args[4]
  273.5 29.7 conditional.57
  338.8 63.7 %all-reduce.768.cloned.1.call-done = (f32[2,4096]{1,0:T(2,128)}, f32[2,4096]{1,0:T(2,128)}) async-done(((f32[2,4096]{1,0:T(2,128)}, f32[2,4096]{1,0:T(2,128)}), (f32[2,4096]{1,0:T(2,128)}, f32[2,4096]{1,0:T(2,128)})) %all-reduce.768.cloned.1.call-update) | async-done | bytes 65552 | tf_op jit(solution)/shard_map/psum | solution.py:598
  444.1 80.0 %all-reduce.766.cloned.1.call-done = (f32[2,4096]{1,0:T(2,128)}, f32[2,4096]{1,0:T(2,128)}) async-done(((f32[2,4096]{1,0:T(2,128)}, f32[2,4096]{1,0:T(2,128)}), (f32[2,4096]{1,0:T(2,128)}, f32[2,4096]{1,0:T(2,128)})) %all-reduce.766.cloned.1.call-update) | async-done | bytes 65552 | tf_op jit(solution)/shard_map/psum | solution.py:598
  565.7 96.7 %all-reduce.764.cloned.1.call-done = (f32[2,4096]{1,0:T(2,128)}, f32[2,4096]{1,0:T(2,128)}) async-done(((f32[2,4096]{1,0:T(2,128)}, f32[2,4096]{1,0:T(2,128)}), (f32[2,4096]{1,0:T(2,128)}, f32[2,4096]{1,0:T(2,128)})) %all-reduce.764.cloned.1.call-update) | async-done | bytes 65552 | tf_op jit(solution)/shard_map/psum | solution.py:598
  693.0 113.4 %all-reduce.762.cloned.1.call-done = (f32[2,4096]{1,0:T(2,128)}, f32[2,4096]{1,0:T(2,128)}) async-done(((f32[2,4096]{1,0:T(2,128)}, f32[2,4096]{1,0:T(2,128)}), (f32[2,4096]{1,0:T(2,128)}, f32[2,4096]{1,0:T(2,128)})) %all-reduce.762.cloned.1.call-update) | async-done | bytes 65552 | tf_op jit(solution)/shard_map/psum | solution.py:598
  835.2 117.0 %all-reduce.760.cloned.1.call-done = (f32[2,4096]{1,0:T(2,128)}, f32[2,4096]{1,0:T(2,128)}) async-done(((f32[2,4096]{1,0:T(2,128)}, f32[2,4096]{1,0:T(2,128)}), (f32[2,4096]{1,0:T(2,128)}, f32[2,4096]{1,0:T(2,128)})) %all-reduce.760.cloned.1.call-update) | async-done | bytes 65552 | tf_op jit(solution)/shard_map/psum | solution.py:598
  979.8 86.2 %all-reduce.758.cloned.1.call-done = (f32[2,4096]{1,0:T(2,128)}, f32[2,4096]{1,0:T(2,128)}) async-done(((f32[2,4096]{1,0:T(2,128)}, f32[2,4096]{1,0:T(2,128)}), (f32[2,4096]{1,0:T(2,128)}, f32[2,4096]{1,0:T(2,128)})) %all-reduce.758.cloned.1.call-update) | async-done | bytes 65552 | tf_op jit(solution)/shard_map/psum | solution.py:598
  1067.1 89.8 %all-reduce.756.cloned.1.call-done = (f32[2,4096]{1,0:T(2,128)}, f32[2,4096]{1,0:T(2,128)}, f32[2,4096]{1,0:T(2,128)}, f32[2,4096]{1,0:T(2,128)}, f32[2,4096]{1,...) async-done(((f32[2,4096]{1,0:T(2,128)}, f32[2,4096]{1,0:T(2,128)}, ...) | async-done | bytes 458768 | tf_op jit(solution)/shard_map/psum | solution.py:598
  1178.7 116.9 %all-reduce.754.cloned.1.call-done = (f32[2,4096]{1,0:T(2,128)}, f32[2,4096]{1,0:T(2,128)}, f32[2,4096]{1,0:T(2,128)}, f32[2,4096]{1,0:T(2,128)}, f32[2,4096]{1,...) async-done(((f32[2,4096]{1,0:T(2,128)}, f32[2,4096]{1,0:T(2,128)}, ...) | async-done | bytes 458768 | tf_op jit(solution)/shard_map/psum | solution.py:598
  1305.8 22.5 conditional.84
  1329.0 133.3 %all-reduce.752.cloned.1.call-done = (f32[2,4096]{1,0:T(2,128)}, f32[2,4096]{1,0:T(2,128)}) async-done(((f32[2,4096]{1,0:T(2,128)}, f32[2,4096]{1,0:T(2,128)}), (f32[2,4096]{1,0:T(2,128)}, f32[2,4096]{1,0:T(2,128)})) %all-reduce.752.cloned.1.call-update) | async-done | bytes 65552 | tf_op jit(solution)/shard_map/psum | solution.py:699
  1462.4 40.4 conditional.85
  1502.9 99.7 %all-reduce.750.cloned.1.call-done = (f32[2,4096]{1,0:T(2,128)}, f32[2,4096]{1,0:T(2,128)}) async-done(((f32[2,4096]{1,0:T(2,128)}, f32[2,4096]{1,0:T(2,128)}), (f32[2,4096]{1,0:T(2,128)}, f32[2,4096]{1,0:T(2,128)})) %all-reduce.750.cloned.1.call-update) | async-done | bytes 65552 | tf_op jit(solution)/shard_map/psum | solution.py:699
  1611.3 154.6 %all-reduce.748.cloned.1.call-done = (f32[2,4096]{1,0:T(2,128)}, f32[2,4096]{1,0:T(2,128)}) async-done(((f32[2,4096]{1,0:T(2,128)}, f32[2,4096]{1,0:T(2,128)}), (f32[2,4096]{1,0:T(2,128)}, f32[2,4096]{1,0:T(2,128)})) %all-reduce.748.cloned.1.call-update) | async-done | bytes 65552 | tf_op jit(solution)/shard_map/psum | solution.py:699
  1782.5 22.7 conditional.88
  1805.9 201.7 %all-reduce.746.cloned.1.call-done = (f32[2,4096]{1,0:T(2,128)}, f32[2,4096]{1,0:T(2,128)}) async-done(((f32[2,4096]{1,0:T(2,128)}, f32[2,4096]{1,0:T(2,128)}), (f32[2,4096]{1,0:T(2,128)}, f32[2,4096]{1,0:T(2,128)})) %all-reduce.746.cloned.1.call-update) | async-done | bytes 65552 | tf_op jit(solution)/shard_map/psum | solution.py:699
  2007.6 47.3 conditional.89
  2055.0 211.6 %all-reduce.744.cloned.1.call-done = (f32[2,4096]{1,0:T(2,128)}, f32[2,4096]{1,0:T(2,128)}) async-done(((f32[2,4096]{1,0:T(2,128)}, f32[2,4096]{1,0:T(2,128)}), (f32[2,4096]{1,0:T(2,128)}, f32[2,4096]{1,0:T(2,128)})) %all-reduce.744.cloned.1.call-update) | async-done | bytes 65552 | tf_op jit(solution)/shard_map/psum | solution.py:699
  2275.4 154.6 %all-reduce.742.cloned.1.call-done = (f32[2,4096]{1,0:T(2,128)}, f32[2,4096]{1,0:T(2,128)}) async-done(((f32[2,4096]{1,0:T(2,128)}, f32[2,4096]{1,0:T(2,128)}), (f32[2,4096]{1,0:T(2,128)}, f32[2,4096]{1,0:T(2,128)})) %all-reduce.742.cloned.1.call-update) | async-done | bytes 65552 | tf_op jit(solution)/shard_map/psum | solution.py:699
  2446.4 22.7 conditional.92
  2469.8 201.6 %all-reduce.740.cloned.1.call-done = (f32[2,4096]{1,0:T(2,128)}, f32[2,4096]{1,0:T(2,128)}) async-done(((f32[2,4096]{1,0:T(2,128)}, f32[2,4096]{1,0:T(2,128)}), (f32[2,4096]{1,0:T(2,128)}, f32[2,4096]{1,0:T(2,128)})) %all-reduce.740.cloned.1.call-update) | async-done | bytes 65552 | tf_op jit(solution)/shard_map/psum | solution.py:699
  2671.5 47.6 conditional.93
  2719.1 211.3 %all-reduce.738.cloned.1.call-done = (f32[2,4096]{1,0:T(2,128)}, f32[2,4096]{1,0:T(2,128)}) async-done(((f32[2,4096]{1,0:T(2,128)}, f32[2,4096]{1,0:T(2,128)}), (f32[2,4096]{1,0:T(2,128)}, f32[2,4096]{1,0:T(2,128)})) %all-reduce.738.cloned.1.call-update) | async-done | bytes 65552 | tf_op jit(solution)/shard_map/psum | solution.py:699
  2938.8 154.4 %all-reduce.736.cloned.1.call-done = (f32[2,4096]{1,0:T(2,128)}, f32[2,4096]{1,0:T(2,128)}) async-done(((f32[2,4096]{1,0:T(2,128)}, f32[2,4096]{1,0:T(2,128)}), (f32[2,4096]{1,0:T(2,128)}, f32[2,4096]{1,0:T(2,128)})) %all-reduce.736.cloned.1.call-update) | async-done | bytes 65552 | tf_op jit(solution)/shard_map/psum | solution.py:699
  3110.4 34.4 conditional.96
  3146.7 189.7 %all-reduce.734.cloned.1.call-done = (f32[2,4096]{1,0:T(2,128)}, f32[2,4096]{1,0:T(2,128)}) async-done(((f32[2,4096]{1,0:T(2,128)}, f32[2,4096]{1,0:T(2,128)}), (f32[2,4096]{1,0:T(2,128)}, f32[2,4096]{1,0:T(2,128)})) %all-reduce.734.cloned.1.call-update) | async-done | bytes 65552 | tf_op jit(solution)/shard_map/psum | solution.py:699
  3336.5 85.0 %conditional.97 = (f32[1,100352]{1,0:T(1,128)S(1)}, bf16[1,100352]{1,0:T(2,128)(2,1)S(1)}, bf16[1,14,14,1024]{3,2,1,0:T(8,128)(2,1)S(1)}, f32[2,18432]{1,0:T(2,1...) conditional(s32[]{:T(128)} %clamp.38, (f32[2,4096]{1,0:T(2,128)}, ...), branch_computations={%region_561.562_spmd, %region_562.563_spmd, %region_563.564_spmd, ... | conditional | flops 852772352 | bytes 338122432 | solution.py:693
  3422.2 166.2 %all-reduce.732.cloned.1.call-done = (f32[2,4096]{1,0:T(2,128)}, f32[2,4096]{1,0:T(2,128)}) async-done(((f32[2,4096]{1,0:T(2,128)}, f32[2,4096]{1,0:T(2,128)}), (f32[2,4096]{1,0:T(2,128)}, f32[2,4096]{1,0:T(2,128)})) %all-reduce.732.cloned.1.call-update) | async-done | bytes 65552 | tf_op jit(solution)/shard_map/psum | solution.py:699
  3611.6 138.5 %all-reduce.730.cloned.1.call-done = (f32[2,4096]{1,0:T(2,128)}, f32[2,4096]{1,0:T(2,128)}) async-done(((f32[2,4096]{1,0:T(2,128)}, f32[2,4096]{1,0:T(2,128)}), (f32[2,4096]{1,0:T(2,128)}, f32[2,4096]{1,0:T(2,128)})) %all-reduce.730.cloned.1.call-update) | async-done | bytes 65552 | tf_op jit(solution)/shard_map/psum | solution.py:699
  3767.4 37.6 conditional.100
  3808.0 151.7 %all-reduce.728.cloned.1.call-done = (f32[2,4096]{1,0:T(2,128)}, f32[2,4096]{1,0:T(2,128)}) async-done(((f32[2,4096]{1,0:T(2,128)}, f32[2,4096]{1,0:T(2,128)}), (f32[2,4096]{1,0:T(2,128)}, f32[2,4096]{1,0:T(2,128)})) %all-reduce.728.cloned.1.call-update) | async-done | bytes 65552 | tf_op jit(solution)/shard_map/psum | solution.py:699
  3959.7 82.5 %conditional.101 = (f32[1,100352]{1,0:T(1,128)}, bf16[1,100352]{1,0:T(2,128)(2,1)S(1)}, bf16[1,14,14,1024]{3,2,1,0:T(8,128)(2,1)S(1)}, f32[2,18432]{1,0:T(2,128)...) conditional(s32[]{:T(128)} %clamp.39, (f32[2,4096]{1,0:T(2,128)}, ...), branch_computations={%region_613.614_spmd, %region_614.615_spmd, %region_615.616_spmd, ... | conditional | flops 852772352 | bytes 339552064 | solution.py:693
  4044.1 165.2 %all-reduce.726.cloned.1.call-done = (f32[2,4096]{1,0:T(2,128)}, f32[2,4096]{1,0:T(2,128)}) async-done(((f32[2,4096]{1,0:T(2,128)}, f32[2,4096]{1,0:T(2,128)}), (f32[2,4096]{1,0:T(2,128)}, f32[2,4096]{1,0:T(2,128)})) %all-reduce.726.cloned.1.call-update) | async-done | bytes 65552 | tf_op jit(solution)/shard_map/psum | solution.py:699
  4220.9 51.2 all-reduce.724.cloned.1.call-done
  4318.7 76.0 %all-reduce.722.cloned.1.call-done = (f32[2,4096]{1,0:T(2,128)}, f32[2,4096]{1,0:T(2,128)}) async-done(((f32[2,4096]{1,0:T(2,128)}, f32[2,4096]{1,0:T(2,128)}), (f32[2,4096]{1,0:T(2,128)}, f32[2,4096]{1,0:T(2,128)})) %all-reduce.722.cloned.1.call-update) | async-done | bytes 65552 | tf_op jit(solution)/shard_map/psum | solution.py:699
  4394.7 84.1 %conditional.105 = (f32[1,100352]{1,0:T(1,128)}, bf16[1,100352]{1,0:T(2,128)(2,1)S(1)}, bf16[1,14,14,1024]{3,2,1,0:T(8,128)(2,1)}, f32[2,18432]{1,0:T(2,128)}, b...) conditional(s32[]{:T(128)} %clamp.40, (f32[2,4096]{1,0:T(2,128)}, ...), branch_computations={%region_665.666_spmd, %region_666.667_spmd, %region_667.668_spmd, ... | conditional | flops 852772352 | bytes 341452672 | solution.py:693
  4480.5 142.6 %all-reduce.720.cloned.1.call-done = (f32[2,4096]{1,0:T(2,128)}, f32[2,4096]{1,0:T(2,128)}) async-done(((f32[2,4096]{1,0:T(2,128)}, f32[2,4096]{1,0:T(2,128)}), (f32[2,4096]{1,0:T(2,128)}, f32[2,4096]{1,0:T(2,128)})) %all-reduce.720.cloned.1.call-update) | async-done | bytes 65552 | tf_op jit(solution)/shard_map/psum | solution.py:699
  4634.8 51.7 all-reduce.718.cloned.1.call-done
  4705.6 32.6 conditional.108
  4739.8 50.4 all-reduce.716.cloned.1.call-done
  4790.2 81.2 %conditional.109 = (f32[1,100352]{1,0:T(1,128)}, bf16[1,14,14,1024]{3,2,1,0:T(8,128)(2,1)}, f32[2,18432]{1,0:T(2,128)}, bf16[2,6,6,1024]{3,2,1,0:T(8,128)(2,1)S(...) conditional(s32[]{:T(128)} %clamp.41, (f32[2,4096]{1,0:T(2,128)}, ...), branch_computations={%region_717.718_spmd, %region_718.719_spmd, %region_719.720_spmd, ... | conditional | flops 711526400 | bytes 316208576 | solution.py:693
  4872.7 49.9 all-reduce.714.cloned.1.call-done
  4935.3 50.5 all-reduce.712.cloned.1.call-done
  4997.1 34.0 all-reduce.708.cloned.1.call-done
  5062.7 353.3 %all-reduce.710.cloned.1.call-done = f32[4456448]{0:T(1024)} async-done(((f32[4456448]{0:T(1024)}), f32[4456448]{0:T(1024)}) %all-reduce.710.cloned.1.call-update) | async-done | bytes 17825808
  5419.1 27.7 reduce-scatter.10.cloned.1.call-done
  5446.8 37.0 reduce-scatter.12.cloned.1.call-done
  (1598 shorter events, 1017.4 us)
Async XLA Ops:
  7.2 266.3 %all-reduce.770.cloned.1.call-start = ((), (), s32[]{:S(2)}) async-start(), calls=%async_computation.37 | async-start | bytes 131072 | tf_op jit(solution)/shard_map/psum | solution.py:598
  218.6 183.8 %all-reduce.768.cloned.1.call-start = ((), (), s32[]{:S(2)}) async-start(), calls=%async_computation.36 | async-start | bytes 131072 | tf_op jit(solution)/shard_map/psum | solution.py:598
  244.5 279.6 %copy-start.487 = (f32[512]{0:T(512)}, f32[512]{0:T(512)S(1)}, u32[]{:S(2)}) copy-start(f32[512]{0:T(512)S(1)} %fusion.2051) | copy-start | bytes 6148
  304.4 9.9 collective-permute-start
  337.5 186.6 %all-reduce.766.cloned.1.call-start = ((), (), s32[]{:S(2)}) async-start(), calls=%async_computation.35 | async-start | bytes 131072 | tf_op jit(solution)/shard_map/psum | solution.py:598
  415.1 5.8 collective-permute-start.1
  442.2 220.2 %all-reduce.764.cloned.1.call-start = ((), (), s32[]{:S(2)}) async-start(), calls=%async_computation.34 | async-start | bytes 131072 | tf_op jit(solution)/shard_map/psum | solution.py:598
  536.7 5.8 collective-permute-start.2
  563.7 242.7 %all-reduce.762.cloned.1.call-start = ((), (), s32[]{:S(2)}) async-start(), calls=%async_computation.33 | async-start | bytes 131072 | tf_op jit(solution)/shard_map/psum | solution.py:598
  674.9 5.8 collective-permute-start.3
  691.1 261.1 %all-reduce.760.cloned.1.call-start = ((), (), s32[]{:S(2)}) async-start(), calls=%async_computation.32 | async-start | bytes 131072 | tf_op jit(solution)/shard_map/psum | solution.py:598
  812.9 10.0 collective-permute-start.4
  833.3 232.7 %all-reduce.758.cloned.1.call-start = ((), (), s32[]{:S(2)}) async-start(), calls=%async_computation.31 | async-start | bytes 131072 | tf_op jit(solution)/shard_map/psum | solution.py:598
  958.5 7.6 collective-permute-start.5
  975.6 181.4 %all-reduce.756.cloned.1.call-start = ((), (), s32[]{:S(2)}) async-start(), calls=%async_computation.30 | async-start | bytes 917504 | tf_op jit(solution)/shard_map/psum | solution.py:598
  1066.7 229.0 %all-reduce.754.cloned.1.call-start = ((), (), s32[]{:S(2)}) async-start(), calls=%async_computation.29 | async-start | bytes 917504 | tf_op jit(solution)/shard_map/psum | solution.py:598
  1177.6 284.8 %all-reduce.752.cloned.1.call-start = ((), (), s32[]{:S(2)}) async-start(), calls=%async_computation.28 | async-start | bytes 131072 | tf_op jit(solution)/shard_map/psum | solution.py:699
  1329.0 273.6 %all-reduce.750.cloned.1.call-start = ((), (), s32[]{:S(2)}) async-start(), calls=%async_computation.27 | async-start | bytes 131072 | tf_op jit(solution)/shard_map/psum | solution.py:699
  1502.8 263.1 %all-reduce.748.cloned.1.call-start = ((), (), s32[]{:S(2)}) async-start(), calls=%async_computation.26 | async-start | bytes 131072 | tf_op jit(solution)/shard_map/psum | solution.py:699
  1611.3 396.3 %all-reduce.746.cloned.1.call-start = ((), (), s32[]{:S(2)}) async-start(), calls=%async_computation.25 | async-start | bytes 131072 | tf_op jit(solution)/shard_map/psum | solution.py:699
  1773.4 8.6 collective-permute-start.6
  1805.8 460.7 %all-reduce.744.cloned.1.call-start = ((), (), s32[]{:S(2)}) async-start(), calls=%async_computation.24 | async-start | bytes 131072 | tf_op jit(solution)/shard_map/psum | solution.py:699
  2054.9 375.0 %all-reduce.742.cloned.1.call-start = ((), (), s32[]{:S(2)}) async-start(), calls=%async_computation.23 | async-start | bytes 131072 | tf_op jit(solution)/shard_map/psum | solution.py:699
  2275.3 396.1 %all-reduce.740.cloned.1.call-start = ((), (), s32[]{:S(2)}) async-start(), calls=%async_computation.22 | async-start | bytes 131072 | tf_op jit(solution)/shard_map/psum | solution.py:699
  2437.4 8.6 collective-permute-start.7
  2469.8 460.6 %all-reduce.738.cloned.1.call-start = ((), (), s32[]{:S(2)}) async-start(), calls=%async_computation.21 | async-start | bytes 131072 | tf_op jit(solution)/shard_map/psum | solution.py:699
  2719.1 374.1 %all-reduce.736.cloned.1.call-start = ((), (), s32[]{:S(2)}) async-start(), calls=%async_computation.20 | async-start | bytes 131072 | tf_op jit(solution)/shard_map/psum | solution.py:699
  2938.7 397.7 %all-reduce.734.cloned.1.call-start = ((), (), s32[]{:S(2)}) async-start(), calls=%async_computation.19 | async-start | bytes 131072 | tf_op jit(solution)/shard_map/psum | solution.py:699
  3100.9 9.1 collective-permute-start.8
  3145.5 442.9 %all-reduce.732.cloned.1.call-start = ((), (), s32[]{:S(2)}) async-start(), calls=%async_computation.18 | async-start | bytes 131072 | tf_op jit(solution)/shard_map/psum | solution.py:699
  3421.5 328.6 %all-reduce.730.cloned.1.call-start = ((), (), s32[]{:S(2)}) async-start(), calls=%async_computation.17 | async-start | bytes 131072 | tf_op jit(solution)/shard_map/psum | solution.py:699
  3595.0 364.7 %all-reduce.728.cloned.1.call-start = ((), (), s32[]{:S(2)}) async-start(), calls=%async_computation.16 | async-start | bytes 131072 | tf_op jit(solution)/shard_map/psum | solution.py:699
  3758.3 8.6 collective-permute-start.9
  3805.0 404.3 %all-reduce.726.cloned.1.call-start = ((), (), s32[]{:S(2)}) async-start(), calls=%async_computation.15 | async-start | bytes 131072 | tf_op jit(solution)/shard_map/psum | solution.py:699
  4042.2 229.9 %all-reduce.724.cloned.1.call-start = ((), (), s32[]{:S(2)}) async-start(), calls=%async_computation.14 | async-start | bytes 131072 | tf_op jit(solution)/shard_map/psum | solution.py:699
  4219.1 175.6 %all-reduce.722.cloned.1.call-start = ((), (), s32[]{:S(2)}) async-start(), calls=%async_computation.13 | async-start | bytes 131072 | tf_op jit(solution)/shard_map/psum | solution.py:699
  4284.4 8.6 collective-permute-start.10
  4315.7 307.5 %all-reduce.720.cloned.1.call-start = ((), (), s32[]{:S(2)}) async-start(), calls=%async_computation.12 | async-start | bytes 131072 | tf_op jit(solution)/shard_map/psum | solution.py:699
  4478.8 207.7 %all-reduce.718.cloned.1.call-start = ((), (), s32[]{:S(2)}) async-start(), calls=%async_computation.11 | async-start | bytes 131072 | tf_op jit(solution)/shard_map/psum | solution.py:699
  4633.0 157.2 %all-reduce.716.cloned.1.call-start = ((), (), s32[]{:S(2)}) async-start(), calls=%async_computation.10 | async-start | bytes 131072 | tf_op jit(solution)/shard_map/psum | solution.py:699
  4696.2 8.9 collective-permute-start.11
  4738.2 184.5 %all-reduce.714.cloned.1.call-start = ((), (), s32[]{:S(2)}) async-start(), calls=%async_computation.9 | async-start | bytes 131072 | tf_op jit(solution)/shard_map/psum | solution.py:699
  4871.5 114.3 %all-reduce.712.cloned.1.call-start = ((), (), s32[]{:S(2)}) async-start(), calls=%async_computation.8 | async-start | bytes 131072 | tf_op jit(solution)/shard_map/psum | solution.py:699
  4931.7 99.4 %all-reduce.708.cloned.1.call-start = ((), (), s32[]{:S(2)}) async-start(), calls=%async_computation.3 | async-start | bytes 589824
  4932.6 128.4 %reduce-scatter.14.cloned.1.call-start = ((), (), s32[]{:S(2)}) async-start(), calls=%async_computation.7 | async-start | bytes 983040
  4935.2 480.8 %all-reduce.710.cloned.1.call-start = ((), (), s32[]{:S(2)}) async-start(), calls=%async_computation.4 | async-start | bytes 35651584
  4985.9 461.0 %reduce-scatter.10.cloned.1.call-start = ((), (), s32[]{:S(2)}) async-start(), calls=%async_computation.5 | async-start | bytes 1146880
  4992.1 491.7 %reduce-scatter.12.cloned.1.call-start = ((), (), s32[]{:S(2)}) async-start(), calls=%async_computation.6 | async-start | bytes 2293760
  (333 other events, 10170.5 us)
Sparse Core Ops, SparseCore 0:
  218.8 54.6 all-reduce.769
  337.6 64.8 all-reduce.767
  442.3 81.7 all-reduce.765
  563.9 98.4 all-reduce.763
  691.2 115.1 all-reduce.761
  833.4 118.7 all-reduce.759
  975.7 90.2 all-reduce.757
  1070.6 86.3 all-reduce.755
  1177.7 117.9 all-reduce.753
  1329.1 133.2 all-reduce.751
  1503.0 99.5 all-reduce.749
  1611.4 154.4 all-reduce.747
  1806.0 201.5 all-reduce.745
  2055.0 211.4 all-reduce.743
  2275.5 154.4 all-reduce.741
  2469.9 201.5 all-reduce.739
  2719.2 211.1 all-reduce.737
  2938.9 154.2 all-reduce.735
  3145.6 190.7 all-reduce.733
  3421.6 166.7 all-reduce.731
  3595.2 154.9 all-reduce.729
  3805.1 154.5 all-reduce.727
  4042.3 166.9 all-reduce.725
  4219.2 52.9 all-reduce.723
  4315.8 78.8 all-reduce.721
  4478.9 144.1 all-reduce.719
  4633.1 53.3 all-reduce.717
  4738.3 51.8 all-reduce.715
  4871.6 50.9 all-reduce.713
  4931.9 53.8 all-reduce.711
  4988.7 42.3 all-reduce.707
  5034.8 26.0 reduce-scatter.13
  5063.4 352.5 all-reduce.709
  5419.8 27.0 reduce-scatter.9
  5450.8 33.0 reduce-scatter.11
where the time goes:
time: 5520 us; the launch traced here: 5490 us
  waiting for transfers between devices  4080 us (74%)
  loops' own time  531 us (10%)
  local copies, waits for them, and re-layouts  438 us (8%)
  other arithmetic  335 us (6%)
    psum x30, waiting for transfers between devices, on_device(): summed = lax.psum(moments, 'dp')  3580 us
    unnamed x40, waiting for transfers between devices  467 us
    another operation x28, loops' own time, on_device(): lax.switch(chooser, backward_fns[phase_id], (holding, accum, stored_now,...  418 us
    unnamed x1, other arithmetic  189 us
    another operation x28, loops' own time, on_device(): lax.switch(chooser, forward_fns[phase_id], (holding, received, images_now...  113 us
  transfers between devices with their start and end apart: 47, of which 46 were waited for; matrix products, arithmetic and copies ran while one was open for 3% of the time, Pallas kernels for 0%

commit v1 on v0

v1 whole, which is shorter than its diff:
```python
import functools

import jax
import jax.numpy as jnp
import numpy as np
from jax import lax
from jax.experimental import pallas as pl
from jax.experimental.pallas import tpu as pltpu
from jax.sharding import PartitionSpec as P

C_IN = 1024
C_MID = 512
C_OUT = 2048
EPS = 1e-05
W = 512
NQ = C_OUT // W
CH = 16
LANES = W // 128
HALF = W // 2
BF = jnp.bfloat16
F32 = jnp.float32
MESH = pl.DeviceIdType.MESH


def up16(n):
    return -(-n // 16) * 16


class Geometry:
    def __init__(self, crops, sides):
        self.crops, self.sides = crops, sides
        self.in_big = crops[0] * sides[0] ** 2
        self.in_all = self.in_big + crops[1] * sides[1] ** 2
        self.out_big = crops[0] * (sides[0] // 2) ** 2
        self.out_all = self.out_big + crops[1] * (sides[1] // 2) ** 2
        self.IN, self.OUT = up16(self.in_all), up16(self.out_all)

    def pixels(self, halves):
        index, table = 0, {}
        for group in (0, 1):
            side = self.sides[group] // 2 if halves else self.sides[group]
            for crop in range(self.crops[group]):
                for r in range(side):
                    for c in range(side):
                        table[group, crop, r, c] = index
                        index += 1
        return table

    def windows(self, stride):
        ins, outs = self.pixels(stride == 1), self.pixels(True)
        picks = np.zeros((9, self.OUT, self.OUT if stride == 1 else self.IN), np.float32)
        for (group, crop, r, c), row in outs.items():
            for tap in range(9):
                at = (group, crop, stride * r + tap // 3 - 1, stride * c + tap % 3 - 1)
                if at in ins:
                    picks[tap, row, ins[at]] = 1.0
        return picks.reshape(9 * self.OUT, -1)

    def every_second(self):
        ins, outs = self.pixels(False), self.pixels(True)
        picks = np.zeros((self.OUT, self.IN), np.float32)
        for (group, crop, r, c), row in outs.items():
            picks[row, ins[group, crop, 2 * r, 2 * c]] = 1.0
        return picks


def dot(a, b):
    return jnp.dot(a, b, preferred_element_type=F32)


def dot_nt(a, b):
    return lax.dot_general(a, b, (((1,), (1,)), ((), ())), preferred_element_type=F32)


def dot_tn(a, b):
    return lax.dot_general(a, b, (((0,), (0,)), ((), ())), preferred_element_type=F32)


def sigmoid(v):
    return 1.0 / (1.0 + jnp.exp(-v))


def slope_of(v):
    s = sigmoid(v)
    return s * (1.0 + v * (1.0 - s))


def runs_of(n_big, n_all, rows):
    runs = []
    for first in range(0, rows, CH):
        kind = (min(max(n_big - first, 0), CH), min(max(n_all - first, 0), CH))
        if runs and runs[-1][2:] == kind:
            runs[-1] = (runs[-1][0], runs[-1][1] + 1) + kind
        else:
            runs.append((first, 1) + kind)
    return runs


def row_ids():
    return lax.broadcasted_iota(jnp.int32, (CH, W), 0)


def part(v, low, high):
    if low >= high:
        return None
    if low == 0 and high == CH:
        return v
    r = row_ids()
    return jnp.where((r >= low) & (r < high), v, 0.0)


def pick(vb, vs, bc):
    if bc == CH:
        return vb
    if bc == 0:
        return vs
    return jnp.where(row_ids() < bc, vb, vs)


def each_step(blocks, runs, body, carry):
    def one_block(b, carry):
        for first, length, bc, vc in runs:
            if length == 1:
                carry = body(b, first, bc, vc, carry)
            else:
                carry = lax.fori_loop(
                    0,
                    length,
                    lambda i, c: body(b, pl.multiple_of(first + CH * i, CH), bc, vc, c),
                    carry,
                    unroll=min(length, 4) if length % min(length, 4) == 0 else 1,
                )
        return carry

    if blocks == 1:
        return one_block(0, carry)
    return lax.fori_loop(0, blocks, one_block, carry)


def reduce_rows(blocks, runs, fn, count):
    def body(b, first, bc, vc, carry):
        values = fn(b, first, bc, vc)
        new = []
        for i, v in enumerate(values):
            for g, piece in enumerate((part(v, 0, bc), part(v, bc, vc))):
                total = carry[g * count + i]
                new.append((g * count + i, total if piece is None else total + piece[:8] + piece[8:]))
        return tuple(v for _, v in sorted(new, key=lambda t: t[0]))

    zero = jnp.zeros((8, W), F32)
    totals = each_step(blocks, runs, body, (zero,) * (2 * count))
    return [jnp.sum(t, axis=0, keepdims=True) for t in totals]


def map_rows(blocks, runs, fn):
    def body(b, first, bc, vc, carry):
        fn(b, first, bc, vc)
        return carry

    each_step(blocks, runs, body, 0)


def make_kernel(geo, R, NP, MICRO, SR, PC):
    G = R // MICRO
    PR = SR // PC
    ADD = PR // 17 if PR % 17 == 0 else CH
    IN, OUT = geo.IN, geo.OUT
    ROWS = MICRO * OUT
    runs_in = runs_of(geo.in_big, geo.in_all, IN)
    runs_out = runs_of(geo.out_big, geo.out_all, OUT)
    count_in = (float(R * geo.in_big), float(R * (geo.in_all - geo.in_big)))
    count_out = (float(R * geo.out_big), float(R * (geo.out_all - geo.out_big)))

    def kernel(
        x_h, cot_h, gate_v, w4_h, w16_h, nt, keep, p2, p2t, pb, ps, pst,
        out_h, dx_o, dw_o, ng_o,
        wbuf, raw, xb, gateb, stage, rbig, ssm, rsm, fw, dwide, col, tgb, tmp, mrecv, srecv,
        dwl, pbuf, rv,
        own_a, rcv_a, own_b, rcv_b, par, cof, ngs, ngr,
        ld, raw_s, big_s, big_r, sm_s, sm_r, xs_s, xs_r, ct_s, ct_r, gt_s, gt_r,
        out_s, out_r, mn_s, mn_r, sb_s, sb_r, sta_s, sta_r, stb_s, stb_r, stn_s, stn_r,
        pa_s, pa_r, ch_s, ch_r,
    ):
        me_p, me_d = lax.axis_index("pipe"), lax.axis_index("dp")
        my_m, my_c = me_d // G, me_d % G

        def remote(src, dst, ss, rs, p, d):
            return pltpu.make_async_remote_copy(
                src_ref=src, dst_ref=dst, send_sem=ss, recv_sem=rs, device_id=(p, d), device_id_type=MESH
            )

        def push(src, dst, ss, rs, p, d):
            here = (me_p == p) & (me_d == d)

            @pl.when(here)
            def _():
                pltpu.make_async_copy(src, dst, rs).start()

            @pl.when(jnp.logical_not(here))
            def _():
                remote(src, dst, ss, rs, p, d).start()

        def pushed(src, dst, ss, rs, p, d):
            @pl.when(jnp.logical_not((me_p == p) & (me_d == d)))
            def _():
                remote(src, dst, ss, rs, p, d).wait_send()

        def arrived(dst, rs):
            remote(dst, dst, rs, rs, me_p, me_d).wait_recv()

        def sent(src, ss):
            remote(src, src, ss, ss, me_p, me_d).wait_send()

        def load(src, dst, i):
            return pltpu.make_async_copy(src, dst, ld.at[i])

        def send_a(slot):
            def one(k, c):
                remote(
                    own_a.at[slot], rcv_a.at[slot, k - 1], sta_s.at[slot], sta_r.at[slot],
                    me_p, lax.rem(me_d + k, R),
                ).start()
                return c

            lax.fori_loop(1, R, one, 0, unroll=R <= 8)

        def total_a(slot):
            arrived(rcv_a.at[slot], sta_r.at[slot])
            return lax.fori_loop(0, R - 1, lambda k, t: t + rcv_a[slot, k], own_a[slot], unroll=R <= 8)

        def send_b(slot):
            def one(k, c):
                remote(
                    own_b.at[slot], rcv_b.at[slot, k - 1], stb_s.at[slot], stb_r.at[slot],
                    me_p, my_m * G + lax.rem(my_c + k, G),
                ).start()
                return c

            lax.fori_loop(1, G, one, 0, unroll=G <= 8)

        def total_b(slot):
            arrived(rcv_b.at[slot], stb_r.at[slot])
            return lax.fori_loop(0, G - 1, lambda k, t: t + rcv_b[slot, k], own_b[slot], unroll=G <= 8)

        def put(ref, slot, sums):
            for i, s in enumerate(sums):
                ref[slot, pl.ds(i, 1), :] = s

        def finish_norm(total, slot, cb, counts):
            for g in (0, 1):
                mean = total[2 * g : 2 * g + 1] * (1.0 / counts[g])
                var = total[2 * g + 1 : 2 * g + 2] * (1.0 / counts[g]) - mean * mean
                rstd = lax.rsqrt(var + EPS)
                scale = rstd * nt[cb, 2 * g : 2 * g + 1, :]
                par[slot, pl.ds(4 * g, 1), :] = mean
                par[slot, pl.ds(4 * g + 1, 1), :] = rstd
                par[slot, pl.ds(4 * g + 2, 1), :] = scale
                par[slot, pl.ds(4 * g + 3, 1), :] = nt[cb, 2 * g + 1 : 2 * g + 2, :] - mean * scale

        def param(slot, i, bc):
            return pick(par[slot, pl.ds(i, 1), :], par[slot, pl.ds(4 + i, 1), :], bc)

        def normed(u, slot, bc):
            return u * param(slot, 2, bc) + param(slot, 3, bc)

        def centered(u, slot, bc):
            return (u - param(slot, 0, bc)) * param(slot, 1, bc)

        def finish_back(total, slot, counts, names):
            width = 1 + names
            for g in (0, 1):
                for i in range(width):
                    cof[slot, pl.ds(g * 4 + i, 1), :] = total[g * width + i : g * width + i + 1] * (1.0 / counts[g])

        def back(d, z, cslot, which, pslot, bc, vc):
            a = pick(cof[cslot, pl.ds(0, 1), :], cof[cslot, pl.ds(4, 1), :], bc)
            b = pick(cof[cslot, pl.ds(1 + which, 1), :], cof[cslot, pl.ds(5 + which, 1), :], bc)
            du = param(pslot, 2, bc) * (d - a - z * b)
            return (du if vc == CH else part(du, 0, vc) if vc else jnp.zeros_like(du)).astype(BF)

        def kept(v, m, bc):
            return v if bc == CH else v * pick(jnp.ones((1, W), F32), keep[m], bc)

        def rows(first, n=CH):
            return pl.ds(first, n)

        def at(b, first):
            return pl.ds(pl.multiple_of(b * OUT + first, CH), CH)

        n1 = C_IN
        n2 = 9 * C_MID
        n3 = C_MID + C_IN
        nab = C_OUT + 9 * C_MID

        def fetch(count, source, target):
            def copies(b, slot):
                return [
                    pltpu.make_async_copy(source(b, lane), raw.at[slot, lane], raw_s.at[slot, lane])
                    for lane in range(LANES)
                ]

            for copy in copies(0, 0):
                copy.start()

            def one(b, c):
                slot = lax.rem(b, 2)

                @pl.when(b + 1 < count)
                def _():
                    for copy in copies(b + 1, 1 - slot):
                        copy.start()

                for lane, copy in enumerate(copies(b, slot)):
                    copy.wait()
                    values = raw[slot, lane, :, 0, :].astype(F32).astype(BF)
                    wbuf[pl.ds(pl.multiple_of(target(b), W), W), pl.ds(lane * 128, 128)] = values
                return c

            lax.fori_loop(0, count, one, 0)

        def fetch_narrow(blocks):
            fetch(blocks, lambda b, lane: w4_h.at[pl.ds(b * W, W), lane], lambda b: b * W)

        def fetch_wide(first, blocks, target):
            fetch(
                NQ * blocks,
                lambda b, lane: w16_h.at[pl.ds(first + b // NQ * W, W), lax.rem(b, NQ) * LANES + lane],
                lambda b: target(lax.rem(b, NQ), b // NQ * W),
            )

        barrier = pltpu.get_barrier_semaphore()

        @pl.when((me_p == 0) | (me_p == 2))
        def _():
            load(x_h, xb.at[:, pl.ds(0, IN)], 0).start()

        def greet(i, c):
            p, d = i // R, lax.rem(i, R)

            @pl.when((p != me_p) | (d != me_d))
            def _():
                pl.semaphore_signal(barrier, inc=1, device_id=(p, d), device_id_type=MESH)

            return c

        lax.fori_loop(0, NP * R, greet, 0)

        def first_product(m):
            fw[m, pl.ds(0, IN), :] = dot(xb[2 * m, pl.ds(0, IN), :], wbuf[pl.ds(0, W), :]) + dot(
                xb[2 * m + 1, pl.ds(0, IN), :], wbuf[pl.ds(W, W), :]
            )

            def sums(b, f, bc, vc):
                u = fw[m, rows(f), :]
                return (u, u * u)

            put(own_a, m, reduce_rows(1, runs_in, sums, 2))

        @pl.when(me_p == 0)
        def _():
            fetch_narrow(n1 // W)
            load(x_h, xb.at[:, pl.ds(0, IN)], 0).wait()
            first_product(0)

        pl.semaphore_wait(barrier, NP * R - 1)

        ng_o[...] = jnp.zeros_like(ng_o)

        def keep_narrow(first, grad):
            for lane in range(LANES):
                tmp[pl.ds(lane, W, stride=LANES), :] = grad[:, lane * 128 : (lane + 1) * 128]
            start = pl.multiple_of(first * LANES, W)
            dwl[pl.ds(start, W * LANES), :] = tmp[pl.ds(0, W * LANES), :].astype(BF)

        def keep_wide(first, lhs, index):
            step = NQ * LANES
            for half in range(W // HALF):
                for q in range(NQ):
                    grad = dot_tn(lhs(pl.ds(half * HALF, HALF)), dwide[index + q, pl.ds(0, ROWS), :])
                    for lane in range(LANES):
                        part_of = grad[:, lane * 128 : (lane + 1) * 128]
                        tmp[pl.ds(q * LANES + lane, HALF, stride=step), :] = part_of
                dwl[pl.ds((first + half * HALF) * step, HALF * step), :] = tmp[...].astype(BF)

        def reduce_scatter(used_rows):
            n, i, core = R // 2, me_d // 2, lax.rem(me_d, 2)
            filled = -(-used_rows // PR) * PR
            if filled > used_rows:
                dwl[pl.ds(used_rows, filled - used_rows), :] = jnp.zeros((filled - used_rows, 128), BF)

            def start_of(t, side, pc):
                return pl.multiple_of((2 * t + side) * SR + pc * PR, CH)

            def used(t, side, pc):
                return (2 * t + side) * SR + pc * PR < used_rows

            def pair(t, pc):
                return remote(
                    dwl.at[pl.ds(start_of(t, 1 - core, pc), PR)], pbuf.at[t, pc],
                    pa_s.at[t, pc], pa_r.at[t, pc], me_p, me_d + 1 - 2 * core,
                )

            def rightward(t, pc):
                return remote(rv.at[t, pc], rv.at[t, pc], ch_s.at[t, pc], ch_r.at[t, pc], me_p, me_d + 2)

            def leftward(t, pc):
                slot = jnp.where(t == i - 1, n, t)
                return remote(rv.at[t, pc], rv.at[slot, pc], ch_s.at[t, pc], ch_r.at[slot, pc], me_p, me_d - 2)

            def pieces(fn):
                def one(j, c):
                    for pc in range(PC):
                        fn(j, pc)
                    return c

                lax.fori_loop(0, n, one, 0)

            def add(t, pc, others, store):
                first = start_of(t, core, pc)

                def one(s, c):
                    at_s = pl.ds(pl.multiple_of(s * ADD, CH), ADD)
                    v = dwl[pl.ds(pl.multiple_of(first + s * ADD, CH), ADD), :].astype(F32)
                    v += pbuf[t, pc, at_s, :].astype(F32)
                    for slot in others:
                        v += rv[slot, pc, at_s, :].astype(F32)
                    store(at_s, s, v)
                    return c

                lax.fori_loop(0, PR // ADD, one, 0)

            def send_pair(j, pc):
                t = jnp.where(lax.rem(j, 2) == 0, n - 1 - j // 2, j // 2)

                @pl.when(used(t, 1 - core, pc))
                def _():
                    pair(t, pc).start()

            def forward(t, pc, inside, more, copy):
                def store(at_s, s, v):
                    rv[t, pc, at_s, :] = v.astype(BF)

                @pl.when(inside & used(t, core, pc))
                def _():
                    pair(t, pc).wait_recv()

                    @pl.when(more)
                    def _():
                        arrived(rv.at[t, pc], ch_r.at[t, pc])
                        add(t, pc, (t,), store)

                    @pl.when(jnp.logical_not(more))
                    def _():
                        add(t, pc, (), store)

                    copy(t, pc).start()

            def both_ways(j, pc):
                right, left = n - 1 - j, j
                forward(right, pc, right > i, i > 0, rightward)
                forward(left, pc, left < i, i < n - 1, leftward)

            def finish(pc):
                def out_rows(s):
                    return pl.ds(pl.multiple_of(pc * PR + s * ADD, CH), ADD)

                def store(at_s, s, v):
                    dw_o[out_rows(s), :] = v

                @pl.when(jnp.logical_not(used(i, core, pc)))
                def _():
                    dw_o[pl.ds(pc * PR, PR), :] = jnp.zeros((PR, 128), F32)

                @pl.when(used(i, core, pc))
                def _():
                    pair(i, pc).wait_recv()
                    for low, high in ((True, True), (True, False), (False, True)):

                        @pl.when(((i > 0) == low) & ((i < n - 1) == high))
                        def _(low=low, high=high):
                            others = ()
                            if low:
                                arrived(rv.at[i, pc], ch_r.at[i, pc])
                                others += (i,)
                            if high:
                                arrived(rv.at[n, pc], ch_r.at[n, pc])
                                others += (n,)
                            add(i, pc, others, store)

            def sent_all(j, pc):
                @pl.when(used(j, 1 - core, pc))
                def _():
                    pair(j, pc).wait_send()

                @pl.when((j > i) & used(j, core, pc))
                def _():
                    rightward(j, pc).wait_send()

                @pl.when((j < i) & used(j, core, pc))
                def _():
                    leftward(j, pc).wait_send()

            pieces(send_pair)
            pieces(both_ways)
            for pc in range(PC):
                finish(pc)
            pieces(sent_all)

        def add_norm_grads(cb, total):
            for g in (0, 1):
                ng_o[cb, pl.ds(2 * g, 1), :] += total[2 * g + 1 : 2 * g + 2]
                ng_o[cb, pl.ds(2 * g + 1, 1), :] += total[2 * g : 2 * g + 1]

        @pl.when(me_p == 0)
        def _():
            send_a(0)

            def first(m, c):
                first_product(m)
                send_a(m)
                return c

            lax.fori_loop(1, MICRO, first, 0)

            def second(m, c):
                finish_norm(total_a(m), m, 0, count_in)

                def act(b, f, bc, vc):
                    n = normed(fw[m, rows(f), :], m, bc)
                    stage[m, rows(f), :] = kept(n * sigmoid(n), m, bc).astype(BF)

                map_rows(1, runs_in, act)
                push(stage.at[m, pl.ds(0, IN)], rbig.at[m, pl.ds(0, IN)], big_s.at[m], big_r.at[m], 1, me_d)
                return c

            lax.fori_loop(0, MICRO, second, 0)

            def main_copy(m):
                return (tgb.at[pl.ds(2 * m, 2), pl.ds(0, IN)], mrecv, mn_s.at[m], mn_r, m, me_d)

            def third(m, c):
                arrived(rbig.at[m, pl.ds(0, IN)], big_r.at[m])

                def sums(b, f, bc, vc):
                    u = fw[m, rows(f), :]
                    d = kept(rbig[m, rows(f), :].astype(F32) * slope_of(normed(u, m, bc)), m, bc)
                    fw[MICRO + m, rows(f), :] = d
                    return (d, d * centered(u, m, bc))

                put(own_a, MICRO + m, reduce_rows(1, runs_in, sums, 2))
                send_a(MICRO + m)
                total = total_a(MICRO + m)
                finish_back(total, 0, count_in, 1)
                add_norm_grads(0, total)

                def grad(b, f, bc, vc):
                    z = centered(fw[m, rows(f), :], m, bc)
                    dwide[m, rows(f), :] = back(fw[MICRO + m, rows(f), :], z, 0, 0, m, bc, vc)

                map_rows(1, runs_in, grad)
                for h in range(2):
                    piece = dot_nt(dwide[m, pl.ds(0, IN), :], wbuf[pl.ds(h * W, W), :])
                    tgb[2 * m + h, pl.ds(0, IN), :] = piece.astype(BF)
                push(*main_copy(m))
                return c

            lax.fori_loop(0, MICRO, third, 0)
            for h in range(2):
                total = dot_tn(xb[h, pl.ds(0, IN), :], dwide[0, pl.ds(0, IN), :])
                for m in range(1, MICRO):
                    total += dot_tn(xb[2 * m + h, pl.ds(0, IN), :], dwide[m, pl.ds(0, IN), :])
                keep_narrow(h * W, total)
            reduce_scatter(n1 * LANES)
            for m in range(MICRO):
                pushed(stage.at[m, pl.ds(0, IN)], rbig.at[m, pl.ds(0, IN)], big_s.at[m], big_r.at[m], 1, me_d)
                pushed(*main_copy(m))
            for slot in range(2 * MICRO):
                sent(rcv_a.at[slot], sta_s.at[slot])

        @pl.when(me_p == 1)
        def _():
            fetch_narrow(n2 // W)

            def first(m, c):
                arrived(rbig.at[m, pl.ds(0, IN)], big_r.at[m])
                col[:, m] = dot(p2[...], rbig[m, pl.ds(0, IN), :]).astype(BF).reshape(9, OUT, W)
                total = dot(col[0, m], wbuf[pl.ds(0, C_MID), :])
                for tap in range(1, 9):
                    total += dot(col[tap, m], wbuf[pl.ds(tap * C_MID, C_MID), :])
                fw[0, pl.ds(pl.multiple_of(m * OUT, CH), OUT), :] = total

                def sums(b, f, bc, vc):
                    u = fw[0, at(m, f), :]
                    return (u, u * u)

                put(own_a, m, reduce_rows(1, runs_out, sums, 2))
                send_a(m)
                finish_norm(total_a(m), m, 0, count_out)

                def act(b, f, bc, vc):
                    n = normed(fw[0, at(m, f), :], m, bc)
                    ssm[m, rows(f), :] = kept(n * sigmoid(n), m, bc).astype(BF)

                map_rows(1, runs_out, act)
                push(ssm.at[m], rsm.at[my_m], sm_s.at[m], sm_r.at[my_m], 2, m * G + my_c)
                return c

            lax.fori_loop(0, MICRO, first, 0)

            def second(m, c):
                arrived(rsm.at[m], sm_r.at[m])

                def sums(b, f, bc, vc):
                    u = fw[0, at(m, f), :]
                    d = kept(rsm[m, rows(f), :].astype(F32) * slope_of(normed(u, m, bc)), m, bc)
                    fw[1, at(m, f), :] = d
                    return (d, d * centered(u, m, bc))

                put(own_a, MICRO + m, reduce_rows(1, runs_out, sums, 2))
                send_a(MICRO + m)
                total = total_a(MICRO + m)
                finish_back(total, 0, count_out, 1)
                add_norm_grads(0, total)

                def grad(b, f, bc, vc):
                    z = centered(fw[0, at(m, f), :], m, bc)
                    dwide[0, at(m, f), :] = back(fw[1, at(m, f), :], z, 0, 0, m, bc, vc)

                map_rows(1, runs_out, grad)
                du = dwide[0, pl.ds(pl.multiple_of(m * OUT, CH), OUT), :]
                for tap in range(9):
                    tgb[tap, pl.ds(0, OUT), :] = dot_nt(du, wbuf[pl.ds(tap * C_MID, C_MID), :]).astype(BF)
                taps = tgb[:, pl.ds(0, OUT), :].reshape(9 * OUT, W)
                stage[m, pl.ds(0, IN), :] = dot(p2t[...], taps).astype(BF)
                push(stage.at[m, pl.ds(0, IN)], rbig.at[m, pl.ds(0, IN)], big_s.at[m], big_r.at[m], 0, me_d)
                return c

            lax.fori_loop(0, MICRO, second, 0)

            def weights(tap, c):
                grad = dot_tn(col[tap].reshape(ROWS, W), dwide[0, pl.ds(0, ROWS), :])
                keep_narrow(tap * C_MID, grad)
                return c

            lax.fori_loop(0, 9, weights, 0)
            reduce_scatter(n2 * LANES)
            for m in range(MICRO):
                pushed(stage.at[m, pl.ds(0, IN)], rbig.at[m, pl.ds(0, IN)], big_s.at[m], big_r.at[m], 0, me_d)
                pushed(ssm.at[m], rsm.at[my_m], sm_s.at[m], sm_r.at[my_m], 2, m * G + my_c)
            for slot in range(2 * MICRO):
                sent(rcv_a.at[slot], sta_s.at[slot])

        def share_norm_grads():
            ngs[...] = ng_o[...]
            for k in range(1, MICRO):
                remote(
                    ngs, ngr.at[k - 1], stn_s.at[k - 1], stn_r.at[k - 1], me_p, lax.rem(me_d + k * G, R)
                ).start()
            for k in range(1, MICRO):
                arrived(ngr.at[k - 1], stn_r.at[k - 1])
                ng_o[...] += ngr[k - 1]
            for k in range(1, MICRO):
                sent(ngs, stn_s.at[k - 1])

        def sub_copy(m):
            return (col.at[pl.ds(4, 2), m], col.at[pl.ds(0, 2), my_m], xs_s.at[m], xs_r.at[my_m], 2, m * G + my_c)

        def sub_back(k):
            return (col.at[pl.ds(6, 2), k], srecv, sb_s.at[k], sb_r, my_m, k * G + my_c)

        @pl.when(me_p == 2)
        def _():
            load(x_h, xb.at[:, pl.ds(0, IN)], 0).wait()

            def send_x(m, c):
                for h in range(2):
                    col[4 + h, m] = dot(ps[...], xb[2 * m + h, pl.ds(0, IN), :]).astype(BF)
                push(*sub_copy(m))
                return c

            lax.fori_loop(0, MICRO, send_x, 0)
            fetch_wide(0, n3 // W, lambda q, r: q * n3 + r)
            for k in range(MICRO):
                arrived(col.at[pl.ds(0, 2), k], xs_r.at[k])

            def w3(q):
                return wbuf[pl.ds(pl.multiple_of(q * n3, C_MID), C_MID), :]

            def wp(q, h):
                return wbuf[pl.ds(pl.multiple_of(q * n3 + C_MID + h * W, W), W), :]

            def xsub(h):
                return col[h].reshape(ROWS, W)

            def product(index, value, slot):
                fw[index, pl.ds(0, ROWS), :] = value

                def sums(b, f, bc, vc):
                    u = fw[index, at(b, f), :]
                    return (u, u * u)

                put(own_b, slot, reduce_rows(MICRO, runs_out, sums, 2))
                send_b(slot)

            def short(q, c):
                product(NQ + q, dot(xsub(0), wp(q, 0)) + dot(xsub(1), wp(q, 1)), NQ + q)
                return c

            lax.fori_loop(0, NQ, short, 0)
            for k in range(MICRO):
                arrived(rsm.at[k], sm_r.at[k])

            def main(q, c):
                product(q, dot(rsm[...].reshape(ROWS, W), w3(q)), q)
                return c

            lax.fori_loop(0, NQ, main, 0)

            def join(q, c):
                finish_norm(total_b(NQ + q), NQ + q, NQ + q, count_out)
                finish_norm(total_b(q), q, q, count_out)

                def act(b, f, bc, vc):
                    n = normed(fw[q, at(b, f), :], q, bc) + normed(fw[NQ + q, at(b, f), :], NQ + q, bc)
                    stage[q, at(b, f), :] = (n * sigmoid(n)).astype(BF)

                map_rows(MICRO, runs_out, act)
                push(stage.at[q, pl.ds(0, ROWS)], rbig.at[q, pl.ds(0, ROWS)], big_s.at[q], big_r.at[q], 3, me_d)
                return c

            lax.fori_loop(0, NQ, join, 0)

            def slopes(q, c):
                arrived(rbig.at[q, pl.ds(0, ROWS)], big_r.at[q])

                def sums(b, f, bc, vc):
                    um, us = fw[q, at(b, f), :], fw[NQ + q, at(b, f), :]
                    n = normed(um, q, bc) + normed(us, NQ + q, bc)
                    d = rbig[q, at(b, f), :].astype(F32) * slope_of(n)
                    fw[2 * NQ, at(b, f), :] = d
                    return (d, d * centered(um, q, bc), d * centered(us, NQ + q, bc))

                put(own_b, 2 * NQ + q, reduce_rows(MICRO, runs_out, sums, 3))
                send_b(2 * NQ + q)
                total = total_b(2 * NQ + q)
                finish_back(total, 0, count_out, 2)
                for g in (0, 1):
                    ng_o[q, pl.ds(2 * g, 1), :] = total[3 * g + 1 : 3 * g + 2]
                    ng_o[q, pl.ds(2 * g + 1, 1), :] = total[3 * g : 3 * g + 1]
                    ng_o[NQ + q, pl.ds(2 * g, 1), :] = total[3 * g + 2 : 3 * g + 3]
                    ng_o[NQ + q, pl.ds(2 * g + 1, 1), :] = total[3 * g : 3 * g + 1]

                def grad(b, f, bc, vc):
                    d = fw[2 * NQ, at(b, f), :]
                    zm = centered(fw[q, at(b, f), :], q, bc)
                    zs = centered(fw[NQ + q, at(b, f), :], NQ + q, bc)
                    dwide[q, at(b, f), :] = back(d, zm, 0, 0, q, bc, vc)
                    dwide[NQ + q, at(b, f), :] = back(d, zs, 0, 1, NQ + q, bc, vc)

                map_rows(MICRO, runs_out, grad)
                da = dot_nt(dwide[q, pl.ds(0, ROWS), :], w3(q))

                @pl.when(q == 0)
                def _():
                    fw[2 * NQ + 1, pl.ds(0, ROWS), :] = da

                @pl.when(q > 0)
                def _():
                    fw[2 * NQ + 1, pl.ds(0, ROWS), :] += da

                return c

            lax.fori_loop(0, NQ, slopes, 0)

            def back_a2(k, c):
                block = fw[2 * NQ + 1, pl.ds(pl.multiple_of(k * OUT, CH), OUT), :]
                ssm[k] = block.astype(BF)
                push(ssm.at[k], rsm_back(k), sm_s.at[k], sm_r.at[my_m], 1, k * G + my_c)
                return c

            def rsm_back(k):
                return rsm.at[my_m]

            lax.fori_loop(0, MICRO, back_a2, 0)

            for m in range(MICRO):
                pushed(*sub_copy(m))
            for h in range(C_IN // W):
                SUB = 2 * NQ + 2
                for q in range(NQ):
                    piece = dot_nt(dwide[NQ + q, pl.ds(0, ROWS), :], wp(q, h))
                    if q == 0:
                        fw[SUB, pl.ds(0, ROWS), :] = piece
                    else:
                        fw[SUB, pl.ds(0, ROWS), :] += piece
                for k in range(MICRO):
                    col[6 + h, k] = fw[SUB, pl.ds(k * OUT, OUT), :].astype(BF)
            for k in range(MICRO):
                push(*sub_back(k))

            keep_wide(0, lambda r: rsm[:, :, r].reshape(ROWS, HALF), 0)
            for h in range(2):
                keep_wide((h + 1) * W, lambda r, h=h: col[h, :, :, r].reshape(ROWS, HALF), NQ)
            share_norm_grads()
            reduce_scatter(n3 * NQ * LANES)
            for k in range(MICRO):
                pushed(ssm.at[k], rsm_back(k), sm_s.at[k], sm_r.at[my_m], 1, k * G + my_c)
                pushed(*sub_back(k))
            for q in range(NQ):
                pushed(stage.at[q, pl.ds(0, ROWS)], rbig.at[q, pl.ds(0, ROWS)], big_s.at[q], big_r.at[q], 3, me_d)
            for slot in range(3 * NQ):
                sent(rcv_b.at[slot], stb_s.at[slot])

        def block(k):
            return pl.ds(pl.multiple_of(k * OUT, CH), OUT)

        def cot_copy(m):
            return (cot_h.at[m], xb.at[pl.ds(0, NQ), block(my_m)], ct_s.at[m], ct_r.at[my_m], 3, m * G + my_c)

        def gate_copy(m):
            return (gate_v.at[m], gateb.at[my_m], gt_s.at[m], gt_r.at[my_m], 3, m * G + my_c)

        def out_copy(k):
            return (xb.at[pl.ds(NQ, NQ), block(k)], out_h, out_s.at[k], out_r, my_m, k * G + my_c)

        @pl.when(me_p == 3)
        def _():
            for m in range(MICRO):
                push(*gate_copy(m))
                push(*cot_copy(m))
            fetch_narrow(nab // W)
            fetch_wide(nab * W // C_OUT, 1, lambda q, r: nab + q * C_MID)
            A, B, T1, T2 = 2 * NQ, 2 * NQ + 1, 2 * NQ + 2, 2 * NQ + 3
            DB, DA, H1, H2 = NQ, NQ + 1, NQ + 2, NQ + 3
            full = pl.ds(0, ROWS)

            def wa(q):
                return wbuf[pl.ds(pl.multiple_of(q * W, W), W), :]

            def wb(tap):
                return wbuf[pl.ds(pl.multiple_of(C_OUT + tap * C_MID, C_MID), C_MID), :]

            def wc(q):
                return wbuf[pl.ds(pl.multiple_of(nab + q * C_MID, C_MID), C_MID), :]

            def accumulate(index, i, value):
                @pl.when(i == 0)
                def _():
                    fw[index, full, :] = value

                @pl.when(i > 0)
                def _():
                    fw[index, full, :] += value

            def begin(index, slot):
                def sums(b, f, bc, vc):
                    u = fw[index, at(b, f), :]
                    return (u, u * u)

                put(own_b, slot, reduce_rows(MICRO, runs_out, sums, 2))
                send_b(slot)

            def hidden(index, slot, target):
                def act(b, f, bc, vc):
                    n = normed(fw[index, at(b, f), :], slot, bc)
                    dwide[target, at(b, f), :] = kept(n * sigmoid(n), my_m, bc).astype(BF)

                map_rows(MICRO, runs_out, act)

            def gather(source, target):
                def one(k, c):
                    block = dwide[source, pl.ds(pl.multiple_of(k * OUT, CH), OUT), :]
                    target(k, dot(pb[...], block).astype(BF).reshape(9, OUT, W))
                    return c

                lax.fori_loop(0, MICRO, one, 0)

            def narrow(q, c):
                arrived(rbig.at[q, full], big_r.at[q])
                accumulate(A, q, dot(rbig[q, full, :], wa(q)))
                return c

            lax.fori_loop(0, NQ, narrow, 0)
            begin(A, 0)
            finish_norm(total_b(0), 0, 0, count_out)
            hidden(A, 0, H1)

            def to_col(k, v):
                col[:, k] = v

            gather(H1, to_col)

            def conv(tap, c):
                accumulate(B, tap, dot(col[tap].reshape(ROWS, W), wb(tap)))
                return c

            lax.fori_loop(0, 9, conv, 0)
            begin(B, 1)
            finish_norm(total_b(1), 1, 1, count_out)
            hidden(B, 1, H2)

            def widen(q, c):
                fw[q, full, :] = dot(dwide[H2, full, :], wc(q))
                begin(q, 2 + q)
                return c

            lax.fori_loop(0, NQ, widen, 0)
            for k in range(MICRO):
                arrived(gateb.at[k], gt_r.at[k])
                arrived(xb.at[pl.ds(0, NQ), block(k)], ct_r.at[k])

            def gate_at(b, f):
                g = gateb[b, rows(f), :]
                return jnp.concatenate([g] * (W // g.shape[1]), axis=1)

            def ends(q, c):
                finish_norm(total_b(2 + q), 2 + q, 2 + q, count_out)

                def sums(b, f, bc, vc):
                    u = fw[q, at(b, f), :]
                    g = gate_at(b, f)
                    v = rbig[q, at(b, f), :].astype(F32) + g * normed(u, 2 + q, bc)
                    sg = sigmoid(v)
                    xb[NQ + q, at(b, f), :] = (v * sg).astype(BF)
                    d = xb[q, at(b, f), :].astype(F32) * (sg * (1.0 + v * (1.0 - sg)))
                    fw[NQ + q, at(b, f), :] = d
                    d = g * d
                    return (d, d * centered(u, 2 + q, bc))

                put(own_b, 2 + NQ + q, reduce_rows(MICRO, runs_out, sums, 2))
                send_b(2 + NQ + q)
                return c

            lax.fori_loop(0, NQ, ends, 0)

            def ends_back(q, c):
                total = total_b(2 + NQ + q)
                finish_back(total, 0, count_out, 1)
                add_norm_grads(2 + q, total)

                def grad(b, f, bc, vc):
                    z = centered(fw[q, at(b, f), :], 2 + q, bc)
                    d = gate_at(b, f) * fw[NQ + q, at(b, f), :]
                    dwide[q, at(b, f), :] = back(d, z, 0, 0, 2 + q, bc, vc)

                map_rows(MICRO, runs_out, grad)
                accumulate(T1, q, dot_nt(dwide[q, full, :], wc(q)))
                return c

            lax.fori_loop(0, NQ, ends_back, 0)
            for k in range(MICRO):
                push(*out_copy(k))

            def middle(index, pslot, slot, target):
                def sums(b, f, bc, vc):
                    u = fw[index, at(b, f), :]
                    d = kept(fw[T1, at(b, f), :] * slope_of(normed(u, pslot, bc)), my_m, bc)
                    fw[T2, at(b, f), :] = d
                    return (d, d * centered(u, pslot, bc))

                put(own_b, slot, reduce_rows(MICRO, runs_out, sums, 2))
                send_b(slot)
                total = total_b(slot)
                finish_back(total, 0, count_out, 1)
                add_norm_grads(pslot, total)

                def grad(b, f, bc, vc):
                    z = centered(fw[index, at(b, f), :], pslot, bc)
                    dwide[target, at(b, f), :] = back(fw[T2, at(b, f), :], z, 0, 0, pslot, bc, vc)

                map_rows(MICRO, runs_out, grad)

            middle(B, 1, 2 + 2 * NQ, DB)

            def to_taps(k, v):
                tgb[:, pl.ds(pl.multiple_of(k * OUT, CH), OUT), :] = v

            gather(DB, to_taps)

            def conv_back(tap, c):
                accumulate(T1, tap, dot_nt(tgb[tap, full, :], wb(8 - tap)))
                return c

            lax.fori_loop(0, 9, conv_back, 0)
            middle(A, 0, 3 + 2 * NQ, DA)

            def to_y(q, c):
                grad = dot_nt(dwide[DA, full, :], wa(q)) + fw[NQ + q, full, :]
                stage[q, full, :] = grad.astype(BF)
                push(stage.at[q, full], rbig.at[q, full], big_s.at[q], big_r.at[q], 2, me_d)
                return c

            lax.fori_loop(0, NQ, to_y, 0)

            def weights_a(q, c):
                keep_narrow(q * W, dot_tn(rbig[q, full, :], dwide[DA, full, :]))
                return c

            def weights_b(tap, c):
                keep_narrow(C_OUT + tap * C_MID, dot_tn(col[tap].reshape(ROWS, W), dwide[DB, full, :]))
                return c

            lax.fori_loop(0, NQ, weights_a, 0)
            lax.fori_loop(0, 9, weights_b, 0)
            keep_wide(nab * W // C_OUT, lambda r: dwide[H2, full, r], 0)
            share_norm_grads()
            reduce_scatter((nab + NQ * C_MID) * LANES)
            for m in range(MICRO):
                pushed(*gate_copy(m))
                pushed(*cot_copy(m))
                pushed(*out_copy(m))
            for q in range(NQ):
                pushed(stage.at[q, full], rbig.at[q, full], big_s.at[q], big_r.at[q], 2, me_d)
            for slot in range(4 + 2 * NQ):
                sent(rcv_b.at[slot], stb_s.at[slot])

        arrived(srecv, sb_r)
        arrived(mrecv, mn_r)
        for h in range(2):
            dx_o[h] = (mrecv[h].astype(F32) + dot(pst[...], srecv[h])).astype(BF)
        arrived(out_h, out_r)

    return kernel


def solution(mesh):
    R, NP = mesh.shape["dp"], mesh.shape["pipe"]

    def on_device(x_big, x_small, cot_big, cot_small, section_weights, section_norms, gate_big, gate_small, width_step):
        MICRO = x_big.shape[0]
        G = R // MICRO
        geo = Geometry((x_big.shape[1], x_small.shape[1]), (x_big.shape[2], x_small.shape[2]))
        IN, OUT, ROWS = geo.IN, geo.OUT, MICRO * geo.OUT
        PW = section_weights.shape[1]
        NB = section_norms.shape[2] // W
        wide = max(IN, ROWS)

        def joined(big, small, width, length):
            parts = [v.reshape(MICRO, -1, width) for v in (big, small)]
            v = jnp.concatenate(parts, axis=1)
            return jnp.pad(v, ((0, 0), (0, length - v.shape[1]), (0, 0)))

        x = joined(x_big, x_small, C_IN, IN)
        x = x.reshape(MICRO, IN, 2, W).transpose(0, 2, 1, 3).reshape(2 * MICRO, IN, W)
        cot = joined(cot_big, cot_small, C_OUT, OUT).reshape(MICRO, OUT, NQ, W).transpose(0, 2, 1, 3)
        gates = [
            jnp.repeat(g.astype(F32), (v.shape[2]) ** 2, axis=1)
            for g, v in ((gate_big, cot_big), (gate_small, cot_small))
        ]
        gate = joined(gates[0][..., None], gates[1][..., None], 1, OUT)
        gate = jnp.broadcast_to(gate, (MICRO, OUT, 128))
        w4 = section_weights.reshape(PW // W, LANES, 1, 128)
        w16 = section_weights.reshape(PW // C_OUT, NQ * LANES, 1, 128)
        SR = PW // 128 // R
        PC = 4 if SR % (4 * CH) == 0 else 2 if SR % (2 * CH) == 0 else 1
        PR = SR // PC
        nt = section_norms[0].reshape(4, NB, W).transpose(1, 0, 2)
        keep = (jnp.arange(C_MID)[None] < C_MID * width_step[:, None] // 4).astype(F32)[:, None]
        p2 = geo.windows(2)
        sub = geo.every_second()
        consts = [p2, p2.T, geo.windows(1), sub, sub.T]
        consts = [jnp.asarray(c, BF) for c in consts]
        vmem, hbm = pl.BlockSpec(memory_space=pltpu.VMEM), pl.BlockSpec(memory_space=pl.ANY)
        V, D = pltpu.VMEM, pltpu.SemaphoreType.DMA
        out, dx, dw, ng = pl.pallas_call(
            make_kernel(geo, R, NP, MICRO, SR, PC),
            out_shape=(
                jax.ShapeDtypeStruct((NQ, OUT, W), BF),
                jax.ShapeDtypeStruct((2, IN, W), BF),
                jax.ShapeDtypeStruct((SR, 128), F32),
                jax.ShapeDtypeStruct((NB, 8, W), F32),
            ),
            in_specs=[hbm, hbm, vmem, hbm, hbm, vmem, vmem] + [vmem] * 5,
            out_specs=(hbm, vmem, vmem, vmem),
            scratch_shapes=[
                V((PW // W, W), BF),
                V((2, LANES, W, 1, 128), BF),
                V((2 * MICRO, wide, W), BF),
                V((MICRO, OUT, 128), F32),
                V((NQ, wide, W), BF),
                V((NQ, wide, W), BF),
                V((MICRO, OUT, W), BF),
                V((MICRO, OUT, W), BF),
                V((2 * NQ + 4, wide, W), F32),
                V((2 * NQ, wide, W), BF),
                V((9, MICRO, OUT, W), BF),
                V((9, wide, W), BF),
                V((HALF * NQ * LANES, 128), F32),
                V((2, IN, W), BF),
                V((2, OUT, W), BF),
                V((PW // 128, 128), BF),
                V((R // 2, PC, PR, 128), BF),
                V((R // 2 + 1, PC, PR, 128), BF),
                V((2 * MICRO, 4, W), F32),
                V((2 * MICRO, R - 1, 4, W), F32),
                V((3 * NQ, 8, W), F32),
                V((3 * NQ, G - 1, 8, W), F32),
                V((8, 8, W), F32),
                V((1, 8, W), F32),
                V((NB, 8, W), F32),
                V((MICRO - 1, NB, 8, W), F32),
                D((1,)),
                D((2, LANES)),
                D((4,)), D((4,)),
                D((4,)), D((4,)),
                D((4,)), D((4,)),
                D((4,)), D((4,)),
                D((4,)), D((4,)),
                D((4,)), D,
                D((4,)), D,
                D((4,)), D,
                D((2 * MICRO,)), D((2 * MICRO,)),
                D((3 * NQ,)), D((3 * NQ,)),
                D((MICRO - 1,)), D((MICRO - 1,)),
                D((R // 2, PC)), D((R // 2, PC)),
                D((R // 2, PC)), D((R // 2 + 1, PC)),
            ],
            compiler_params=pltpu.CompilerParams(
                collective_id=0, has_side_effects=True, vmem_limit_bytes=63 << 20
            ),
        )(x, cot, gate, w4, w16, nt, keep, *consts)

        def crops(v, width, side_of):
            nb, sb = geo.crops[0], side_of(geo.sides[0])
            ns, ss = geo.crops[1], side_of(geo.sides[1])
            cut = nb * sb * sb
            return (
                v[:cut].reshape(1, nb, sb, sb, width),
                v[cut : cut + ns * ss * ss].reshape(1, ns, ss, ss, width),
            )

        out_big, out_small = crops(out.transpose(1, 0, 2).reshape(OUT, C_OUT), C_OUT, lambda s: s // 2)
        grad_big, grad_small = crops(dx.transpose(1, 0, 2).reshape(IN, C_IN), C_IN, lambda s: s)
        weight = dw.reshape(1, PW // R)
        norm = ng[:, :4].transpose(1, 0, 2).reshape(1, 4, NB * W)
        return out_big, out_small, grad_big, grad_small, weight, norm

    images = P(None, "dp", None, None, None)
    ends = P("pipe", "dp", None, None, None)
    return jax.shard_map(
        on_device,
        mesh=mesh,
        in_specs=(images,) * 4 + (P("pipe", None), P("pipe", None, None), P(None, "dp"), P(None, "dp"), P()),
        out_specs=(ends,) * 4 + (P("pipe", "dp"), P("pipe", None, None)),
        check_vma=False,
    )
```

time: 5520 us -> 264 us (0.05)
  the two profiles are of different devices: /device:TPU:0 before, /device:TPU:20 now
where the time goes in v1:
time: 264 us
  Pallas kernels  242 us (92%)
  local copies, waits for them, and re-layouts  15.6 us (6%)
  other arithmetic  4.95 us (2%)
    pallas_call x1, Pallas kernels, on_device(): pl.pallas_call(make_kernel(geo, R, NP, MICRO, SR, PC), out_shape=(jax.Sha...  242 us
    unnamed x13, local copies, waits for them, and re-layouts  5.74 us

profile of v1, /device:TPU:20, one launch (start us, length us, event | category | flops | bytes accessed | tf_op | source)
XLA Modules:
  0.0 263.8 jit_solution(15300896834642319123)
XLA Ops:
  0.6 0.0 copy-start.2
  0.6 0.7 convert_bitcast_fusion
  1.4 0.7 and_select_fusion
  2.0 0.7 convert_element_type.26
  2.7 0.1 copy.29
  2.8 0.1 broadcast_in_dim_reshape.6
  2.9 0.1 broadcast_in_dim.6
  3.0 0.1 broadcast_in_dim_reshape.7
  3.0 0.1 fusion.6
  3.1 0.7 compare_convert_fusion.keep
  3.8 0.8 broadcast_in_dim.16.gate_v
  4.6 1.1 copy.25
  5.7 0.2 copy.27
  5.9 1.5 copy.22
  7.4 0.2 copy.24
  7.6 0.0 copy-done.2
  7.6 0.4 copy.26
  8.0 0.0 copy-start.1
  8.0 0.2 fusion.5
  8.3 1.2 copy.38
  9.5 0.2 copy-done.1
  9.7 0.5 copy.23
  10.2 0.4 fusion.4
  10.5 0.2 fusion.7
  10.7 1.5 pad_maximum_fusion
  12.2 242.5 %shard_map.181 = (bf16[4,80,512]{2,1,0:T(8,128)(2,1)}, bf16[2,272,512]{2,1,0:T(8,128)(2,1)}, f32[4352,128]{1,0:T(8,128)}, f32[8,8,512]{2,1,0:T(8,128)}) custom-call(bf16[8,272,512]{2,1,0:T(8,128)(2,1)} %bitcast.29, bf16[4,4,80,512]{3,2,1,0:T(8,128)(2,1)} %bitcast.30, f32[4,80,128]{2,1,0:T(8,128)} %broadcast_in_dim.16.gate_v, ...), custom_call_target="tpu_custom_call" | custom-call | tf_op jit(solution)/shard_map/pallas_call | solution.py:1065
  254.7 0.0 copy-start.3
  254.7 1.6 slice.31
  256.3 0.9 slice.35
  257.3 1.0 slice.34
  258.2 0.1 copy.30
  258.4 0.0 copy-start
  258.4 0.1 reshape.124
  258.5 0.7 copy.34
  259.2 0.8 reshape.123
  260.0 0.0 copy-done.3
  260.1 0.3 copy.32
  260.4 0.1 copy.33
  260.5 0.1 reshape.126
  260.6 0.8 copy.35
  261.4 1.0 reshape.125
  262.5 0.0 copy-done
  262.5 1.4 copy.40
  (3 shorter events, 0.1 us)
Async XLA Ops:
  0.6 6.9 %copy-start.2 = (bf16[4,1,7,7,2048]{4,0,3,2,1:T(4,128)(2,1)S(1)}, bf16[4,1,7,7,2048]{4,0,3,2,1:T(4,128)(2,1)}, u32[]{:S(2)}) copy-start(bf16[4,1,7,7,2048]{4,0,3,2,1:T(4,128)(2,1)} %param.16) | copy-start | bytes 2408452
  8.0 1.6 copy-start.1
  254.7 5.3 %copy-start.3 = (bf16[2,272,512]{2,1,0:T(8,128)(2,1)S(1)}, bf16[2,272,512]{2,1,0:T(8,128)(2,1)}, u32[]{:S(2)}) copy-start(bf16[2,272,512]{2,1,0:T(8,128)(2,1)} %get-tuple-element.11) | copy-start | bytes 1671172
  258.4 4.1 %copy-start = (f32[4352,128]{1,0:T(8,128)S(1)}, f32[4352,128]{1,0:T(8,128)}, u32[]{:S(2)}) copy-start(f32[4352,128]{1,0:T(8,128)} %get-tuple-element.12) | copy-start | bytes 6684676

commit v2 on v1

v2 whole, which is shorter than its diff:
```python
import functools

import jax
import jax.numpy as jnp
import numpy as np
from jax import lax
from jax.experimental import pallas as pl
from jax.experimental.pallas import tpu as pltpu
from jax.sharding import PartitionSpec as P

C_IN = 1024
C_MID = 512
C_OUT = 2048
EPS = 1e-05
W = 512
NQ = C_OUT // W
CH = 16
LANES = W // 128
HALF = W // 2
BF = jnp.bfloat16
F32 = jnp.float32
MESH = pl.DeviceIdType.MESH


def up16(n):
    return -(-n // 16) * 16


class Geometry:
    def __init__(self, crops, sides):
        self.crops, self.sides = crops, sides
        self.in_big = crops[0] * sides[0] ** 2
        self.in_all = self.in_big + crops[1] * sides[1] ** 2
        self.out_big = crops[0] * (sides[0] // 2) ** 2
        self.out_all = self.out_big + crops[1] * (sides[1] // 2) ** 2
        self.IN, self.OUT = up16(self.in_all), up16(self.out_all)

    def pixels(self, halves):
        index, table = 0, {}
        for group in (0, 1):
            side = self.sides[group] // 2 if halves else self.sides[group]
            crops, sides = range(self.crops[group]), range(side)
            if group == 0:
                places = [(crop, r, c) for crop in crops for r in sides for c in sides]
            else:
                places = [(crop, r, c) for r in sides for c in sides for crop in crops]
            for place in places:
                table[(group,) + place] = index
                index += 1
        return table

    def windows(self, stride):
        ins, outs = self.pixels(stride == 1), self.pixels(True)
        picks = np.zeros((9, self.OUT, self.OUT if stride == 1 else self.IN), np.float32)
        for (group, crop, r, c), row in outs.items():
            for tap in range(9):
                at = (group, crop, stride * r + tap // 3 - 1, stride * c + tap % 3 - 1)
                if at in ins:
                    picks[tap, row, ins[at]] = 1.0
        return picks.reshape(9 * self.OUT, -1)

    def every_second(self):
        ins, outs = self.pixels(False), self.pixels(True)
        picks = np.zeros((self.OUT, self.IN), np.float32)
        for (group, crop, r, c), row in outs.items():
            picks[row, ins[group, crop, 2 * r, 2 * c]] = 1.0
        return picks


def dot(a, b):
    return jnp.dot(a, b, preferred_element_type=F32)


def dot_nt(a, b):
    return lax.dot_general(a, b, (((1,), (1,)), ((), ())), preferred_element_type=F32)


def dot_tn(a, b):
    return lax.dot_general(a, b, (((0,), (0,)), ((), ())), preferred_element_type=F32)


def sigmoid(v):
    return 0.5 * jnp.tanh(0.5 * v) + 0.5


def slope_of(v):
    s = sigmoid(v)
    return s * (1.0 + v * (1.0 - s))


def runs_of(n_big, n_all, rows):
    runs = []
    for first in range(0, rows, CH):
        kind = (min(max(n_big - first, 0), CH), min(max(n_all - first, 0), CH))
        if runs and runs[-1][2:] == kind:
            runs[-1] = (runs[-1][0], runs[-1][1] + 1) + kind
        else:
            runs.append((first, 1) + kind)
    return runs


def row_ids():
    return lax.broadcasted_iota(jnp.int32, (CH, W), 0)


def part(v, low, high):
    if low >= high:
        return None
    if low == 0 and high == CH:
        return v
    r = row_ids()
    return jnp.where((r >= low) & (r < high), v, 0.0)


def pick(vb, vs, bc):
    if bc == CH:
        return vb
    if bc == 0:
        return vs
    return jnp.where(row_ids() < bc, vb, vs)


def each_step(blocks, runs, body, carry):
    def one_block(b, carry):
        for first, length, bc, vc in runs:
            if length == 1:
                carry = body(b, first, bc, vc, carry)
            else:
                carry = lax.fori_loop(
                    0,
                    length,
                    lambda i, c: body(b, pl.multiple_of(first + CH * i, CH), bc, vc, c),
                    carry,
                    unroll=min(length, 4) if length % min(length, 4) == 0 else 1,
                )
        return carry

    if blocks == 1:
        return one_block(0, carry)
    return lax.fori_loop(0, blocks, one_block, carry)


def reduce_rows(blocks, runs, fn, count):
    def body(b, first, bc, vc, carry):
        values = fn(b, first, bc, vc)
        new = []
        for i, v in enumerate(values):
            for g, piece in enumerate((part(v, 0, bc), part(v, bc, vc))):
                total = carry[g * count + i]
                new.append((g * count + i, total if piece is None else total + piece[:8] + piece[8:]))
        return tuple(v for _, v in sorted(new, key=lambda t: t[0]))

    zero = jnp.zeros((8, W), F32)
    totals = each_step(blocks, runs, body, (zero,) * (2 * count))
    return [jnp.sum(t, axis=0, keepdims=True) for t in totals]


def map_rows(blocks, runs, fn):
    def body(b, first, bc, vc, carry):
        fn(b, first, bc, vc)
        return carry

    each_step(blocks, runs, body, 0)


def make_kernel(geo, R, NP, MICRO, SR, PC):
    G = R // MICRO
    N = R // 2
    PR = SR // PC
    RW = SR // (NQ * LANES)
    PRQ = up16(RW * LANES)
    IN, OUT = geo.IN, geo.OUT
    ROWS = MICRO * OUT
    runs_in = runs_of(geo.in_big, geo.in_all, IN)
    runs_out = runs_of(geo.out_big, geo.out_all, OUT)
    count_in = (float(R * geo.in_big), float(R * (geo.in_all - geo.in_big)))
    count_out = (float(R * geo.out_big), float(R * (geo.out_all - geo.out_big)))
    RA, RB = radix(R, 8), radix(G, 4)
    n1 = C_IN
    n2 = 9 * C_MID
    n3 = C_MID + C_IN
    nab = C_OUT + 9 * C_MID
    nabc = nab + C_OUT
    S2 = -(-n3 // RW)

    def kernel(
        x_h, cot_h, gate_big, gate_small, width_step, w4_h, w16_h, nt, p2, pb, ps,
        ob_o, os_o, gb_o, gs_o, dw_o, ng_o,
        wbuf, raw, xb, gate_v, gateb, keep, stage, rbig, ssm, rsm, fw, dwide, col, tgb, tmp, mrecv, srecv, orecv,
        dwl, pbuf, rv, nt2,
        own_a, rcv_a, mid_a, out_a, own_b, rcv_b, mid_b, out_b, par, cof, ngs, ngr,
        ld, raw_s, big_s, big_r, sm_s, sm_t, sm_r, up_s, up_r, xs_s, xs_r, ct_s, ct_r, gt_s, gt_r, w_s, w_r, nt_s, nt_r,
        out_s, out_r, mn_s, mn_r, sb_s, sb_r, sta_s, sta_r, stc_s, stc_r, stb_s, stb_r, std_s, std_r, stn_s, stn_r,
        pa_s, pa_r, ch_s, ch_r,
    ):
        me_p, me_d = lax.axis_index("pipe"), lax.axis_index("dp")
        my_m, my_c = me_d // G, me_d % G
        core = lax.rem(me_d, 2)
        sibling = me_d + 1 - 2 * core
        full = pl.ds(0, ROWS)

        def remote(src, dst, ss, rs, p, d):
            return pltpu.make_async_remote_copy(
                src_ref=src, dst_ref=dst, send_sem=ss, recv_sem=rs, device_id=(p, d), device_id_type=MESH
            )

        def push(src, dst, ss, rs, p, d):
            here = (me_p == p) & (me_d == d)

            @pl.when(here)
            def _():
                pltpu.make_async_copy(src, dst, rs).start()

            @pl.when(jnp.logical_not(here))
            def _():
                remote(src, dst, ss, rs, p, d).start()

        def pushed(src, dst, ss, rs, p, d):
            @pl.when(jnp.logical_not((me_p == p) & (me_d == d)))
            def _():
                remote(src, dst, ss, rs, p, d).wait_send()

        def arrived(dst, rs):
            remote(dst, dst, rs, rs, me_p, me_d).wait_recv()

        def sent(src, ss):
            remote(src, src, ss, ss, me_p, me_d).wait_send()

        def spread_out(src, target, ss, rs, base, place, step, count):
            def one(k, c):
                peer = base + step * lax.rem(place + k, count)
                remote(src, target.at[k - 1], ss, rs, me_p, peer).start()
                return c

            lax.fori_loop(1, count, one, 0, unroll=count <= 8)

        def gather_up(first, received, count):
            return lax.fori_loop(0, count - 1, lambda k, t: t + received[k], first, unroll=count <= 8)

        def summer(own, rcv, mid, out, s1, r1, s2, r2, base, place, count, inner):
            low, high = lax.rem(place, inner), place // inner
            outer = count // inner

            def send(slot):
                spread_out(own.at[slot], rcv.at[slot], s1.at[slot], r1.at[slot], base + high * inner, low, 1, inner)

            def total(slot):
                arrived(rcv.at[slot], r1.at[slot])
                sums = gather_up(own[slot], rcv.at[slot], inner)
                if outer > 1:
                    mid[slot] = sums
                    spread_out(mid.at[slot], out.at[slot], s2.at[slot], r2.at[slot], base + low, high, inner, outer)
                    arrived(out.at[slot], r2.at[slot])
                    sums = gather_up(sums, out.at[slot], outer)
                return sums

            def drain(slot):
                sent(rcv.at[slot], s1.at[slot])
                if outer > 1:
                    sent(out.at[slot], s2.at[slot])

            return send, total, drain

        send_a, total_a, drain_a = summer(
            own_a, rcv_a, mid_a, out_a, sta_s, sta_r, stc_s, stc_r, 0, me_d, R, RA
        )
        send_b, total_b, drain_b = summer(
            own_b, rcv_b, mid_b, out_b, stb_s, stb_r, std_s, std_r, my_m * G, my_c, G, RB
        )

        def put(ref, slot, sums):
            for i, s in enumerate(sums):
                ref[slot, pl.ds(i, 1), :] = s

        def finish_norm(total, slot, table, cb, counts):
            for g in (0, 1):
                mean = total[2 * g : 2 * g + 1] * (1.0 / counts[g])
                var = total[2 * g + 1 : 2 * g + 2] * (1.0 / counts[g]) - mean * mean
                rstd = lax.rsqrt(var + EPS)
                scale = rstd * table[cb, 2 * g : 2 * g + 1, :]
                par[slot, pl.ds(4 * g, 1), :] = mean
                par[slot, pl.ds(4 * g + 1, 1), :] = rstd
                par[slot, pl.ds(4 * g + 2, 1), :] = scale
                par[slot, pl.ds(4 * g + 3, 1), :] = table[cb, 2 * g + 1 : 2 * g + 2, :] - mean * scale

        def param(slot, i, bc):
            return pick(par[slot, pl.ds(i, 1), :], par[slot, pl.ds(4 + i, 1), :], bc)

        def normed(u, slot, bc):
            return u * param(slot, 2, bc) + param(slot, 3, bc)

        def centered(u, slot, bc):
            return (u - param(slot, 0, bc)) * param(slot, 1, bc)

        def put_cof(slot, total, counts):
            for g in (0, 1):
                cof[slot, pl.ds(2 * g, 2), :] = total[2 * g : 2 * g + 2] * (1.0 / counts[g])

        def back(d, z, cslot, zslot, pslot, bc, vc):
            a = pick(cof[cslot, pl.ds(0, 1), :], cof[cslot, pl.ds(2, 1), :], bc)
            b = pick(cof[zslot, pl.ds(1, 1), :], cof[zslot, pl.ds(3, 1), :], bc)
            du = param(pslot, 2, bc) * (d - a - z * b)
            return (du if vc == CH else part(du, 0, vc) if vc else jnp.zeros_like(du)).astype(BF)

        def kept(v, m, bc):
            return v if bc == CH else v * pick(jnp.ones((1, W), F32), keep[m], bc)

        def rows(first, n=CH):
            return pl.ds(first, n)

        def at(b, first):
            return pl.ds(pl.multiple_of(b * OUT + first, CH), CH)

        def block(k):
            return pl.ds(pl.multiple_of(k * OUT, CH), OUT)

        def weight(first):
            return wbuf[pl.ds(pl.multiple_of(first, W), W), :]

        def squares(load):
            def sums(b, f, bc, vc):
                u = load(b, f)
                return (u, u * u)

            return sums

        def add_norm_grads(ref, cb, total):
            for g in (0, 1):
                ref[cb, pl.ds(2 * g, 1), :] += total[2 * g + 1 : 2 * g + 2]
                ref[cb, pl.ds(2 * g + 1, 1), :] += total[2 * g : 2 * g + 1]

        HW = raw.shape[2]

        def fetch(count, source, target):
            def copies(b, slot):
                return [
                    pltpu.make_async_copy(source(b, lane), raw.at[slot, lane], raw_s.at[slot, lane])
                    for lane in range(LANES)
                ]

            for copy in copies(0, 0):
                copy.start()

            def one(b, c):
                slot = lax.rem(b, 2)

                @pl.when(b + 1 < count)
                def _():
                    for copy in copies(b + 1, 1 - slot):
                        copy.start()

                for lane, copy in enumerate(copies(b, slot)):
                    copy.wait()
                    values = raw[slot, lane, :, 0, :].astype(F32).astype(BF)
                    wbuf[pl.ds(pl.multiple_of(target(b), HW), HW), pl.ds(lane * 128, 128)] = values
                return c

            lax.fori_loop(0, count, one, 0)

        def fetch_narrow(count):
            fetch(count // HW, lambda b, lane: w4_h.at[pl.ds(b * HW, HW), lane], lambda b: b * HW)

        def fetch_wide(first, count, target):
            per = count // HW
            fetch(
                NQ * per,
                lambda b, lane: w16_h.at[pl.ds(first + lax.rem(b, per) * HW, HW), b // per * LANES + lane],
                lambda b: target(b // per) + lax.rem(b, per) * HW,
            )

        def ship(source, target, q):
            return remote(wbuf.at[pl.ds(source(q), W)], wbuf.at[pl.ds(target(q), W)], w_s.at[q], w_r.at[q], me_p + 1, me_d)

        def ship_all(source, target, count, go):
            for i in range(count // 2):
                go(ship(source, target, core * (count // 2) + i))

        def pass_on(target, count, go):
            for i in range(count // 2):
                q = core * (count // 2) + i
                ref = wbuf.at[pl.ds(target(q), W)]
                go(ref, q, remote(ref, ref, w_s.at[q], w_r.at[q], me_p, sibling))

        def take(target, count):
            def first(ref, q, copy):
                arrived(ref, w_r.at[q])
                copy.start()

            pass_on(target, count, first)
            for i in range(count // 2):
                q = (1 - core) * (count // 2) + i
                arrived(wbuf.at[pl.ds(target(q), W)], w_r.at[q])

        def w1_at(q):
            return pl.multiple_of(n2 + q * W, W)

        def w3_at(q):
            return pl.multiple_of(nabc + q * W, W)

        def lay_narrow(first, grad):
            for lane in range(LANES):
                tmp[pl.ds(first + lane, W, stride=LANES), :] = grad[:, lane * 128 : (lane + 1) * 128]

        def keep_narrow(first, grad):
            lay_narrow(0, grad)
            start = pl.multiple_of(first * LANES, W)
            dwl[pl.ds(start, W * LANES), :] = tmp[pl.ds(0, W * LANES), :].astype(BF)

        def keep_wide(first, lhs, index):
            step = NQ * LANES
            for half in range(W // HALF):
                for q in range(NQ):
                    grad = dot_tn(lhs(pl.ds(half * HALF, HALF)), dwide[index + q, full, :])
                    for lane in range(LANES):
                        part_of = grad[:, lane * 128 : (lane + 1) * 128]
                        tmp[pl.ds(q * LANES + lane, HALF, stride=step), :] = part_of
                dwl[pl.ds((first + half * HALF) * step, HALF * step), :] = tmp[pl.ds(0, HALF * step), :].astype(BF)

        class Reduction:
            def __init__(self, pieces, rows_of, start, used):
                self.pieces, self.rows_of, self.start, self.used = pieces, rows_of, start, used
                self.step = next(a for a in (64, 48, 32, 16) if rows_of % a == 0)
                self.i = me_d // 2

            def at(self, pc):
                return pl.ds(pc * self.rows_of, self.rows_of)

            def pair(self, t, pc):
                src = dwl.at[pl.ds(pl.multiple_of(self.start(2 * t + 1 - core, pc), CH), self.rows_of)]
                return remote(src, pbuf.at[t, self.at(pc)], pa_s.at[t, pc], pa_r.at[t, pc], me_p, sibling)

            def rightward(self, t, pc):
                ref = rv.at[t, self.at(pc)]
                return remote(ref, ref, ch_s.at[t, pc], ch_r.at[t, pc], me_p, me_d + 2)

            def leftward(self, t, pc):
                slot = jnp.where(t == self.i - 1, N, t)
                src, dst = rv.at[t, self.at(pc)], rv.at[slot, self.at(pc)]
                return remote(src, dst, ch_s.at[t, pc], ch_r.at[slot, pc], me_p, me_d - 2)

            def add(self, t, pc, others, store):
                first, step = self.start(2 * t + core, pc), self.step

                def one(s, c):
                    at_s = pl.ds(pl.multiple_of(pc * self.rows_of + s * step, CH), step)
                    v = dwl[pl.ds(pl.multiple_of(first + s * step, CH), step), :].astype(F32)
                    v += pbuf[t, at_s, :].astype(F32)
                    for slot in others:
                        v += rv[slot, at_s, :].astype(F32)
                    store(at_s, s, v)
                    return c

                lax.fori_loop(0, self.rows_of // step, one, 0)

            def send_pairs(self, pcs, low=0, high=N):
                def one(j, c):
                    t = jnp.where(lax.rem(j, 2) == 0, high - 1 - j // 2, low + j // 2)
                    for pc in pcs:

                        @pl.when(self.used(2 * t + 1 - core, pc))
                        def _(pc=pc):
                            self.pair(t, pc).start()

                    return c

                lax.fori_loop(0, high - low, one, 0)

            def forward(self, t, pc, wanted, received, copy):
                def store(at_s, s, v):
                    rv[t, at_s, :] = v.astype(BF)

                @pl.when(wanted & self.used(2 * t + core, pc))
                def _():
                    self.pair(t, pc).wait_recv()
                    if received:
                        arrived(rv.at[t, self.at(pc)], ch_r.at[t, pc])
                    self.add(t, pc, (t,) if received else (), store)
                    copy(t, pc).start()

            def originate(self, pcs, low=0, high=N):
                def one(j, c):
                    right, left = high - 1 - j, low + j
                    for pc in pcs:
                        self.forward(right, pc, (self.i == 0) & (right > 0), False, self.rightward)
                        self.forward(left, pc, (self.i == N - 1) & (left < N - 1), False, self.leftward)
                    return c

                lax.fori_loop(0, high - low, one, 0)

            def relay(self, pcs, low=0, high=N):
                def one(j, c):
                    right, left = high - 1 - j, low + j
                    for pc in pcs:
                        self.forward(right, pc, (self.i > 0) & (right > self.i), True, self.rightward)
                        self.forward(left, pc, (self.i < N - 1) & (left < self.i), True, self.leftward)
                    return c

                lax.fori_loop(0, high - low, one, 0)

            def finish(self, pc, store):
                i = self.i

                @pl.when(self.used(2 * i + core, pc))
                def _():
                    self.pair(i, pc).wait_recv()
                    for low, high in ((True, True), (True, False), (False, True)):

                        @pl.when(((i > 0) == low) & ((i < N - 1) == high))
                        def _(low=low, high=high):
                            others = ()
                            if low:
                                arrived(rv.at[i, self.at(pc)], ch_r.at[i, pc])
                                others += (i,)
                            if high:
                                arrived(rv.at[N, self.at(pc)], ch_r.at[N, pc])
                                others += (N,)
                            self.add(i, pc, others, store)

            def drain(self):
                def one(j, c):
                    for pc in range(self.pieces):

                        @pl.when(self.used(2 * j + 1 - core, pc))
                        def _(pc=pc):
                            self.pair(j, pc).wait_send()

                        @pl.when((j > self.i) & self.used(2 * j + core, pc))
                        def _(pc=pc):
                            self.rightward(j, pc).wait_send()

                        @pl.when((j < self.i) & self.used(2 * j + core, pc))
                        def _(pc=pc):
                            self.leftward(j, pc).wait_send()

                    return c

                lax.fori_loop(0, N, one, 0)

        def weights_out():
            copy = pltpu.make_async_copy(tmp.at[pl.ds(0, SR)], dw_o, ld.at[1])
            copy.start()
            copy.wait()

        everything = range(PC)

        def flat(used_rows):
            filled = -(-used_rows // PR) * PR
            if filled > used_rows:
                dwl[pl.ds(used_rows, filled - used_rows), :] = jnp.zeros((filled - used_rows, 128), BF)
            return Reduction(PC, PR, lambda s, pc: s * SR + pc * PR, lambda s, pc: s * SR + pc * PR < used_rows)

        def launch(red, low=0, high=N):
            red.send_pairs(everything, low, high)
            red.originate(everything, low, high)

        def finish_flat(red):
            tmp[pl.ds(0, SR), :] = jnp.zeros((SR, 128), F32)
            for pc in everything:

                def store(at_s, s, v):
                    tmp[pl.ds(pl.multiple_of(pc * PR + s * red.step, CH), red.step), :] = v

                red.finish(pc, store)
            weights_out()
            red.drain()

        barrier = pltpu.get_barrier_semaphore()
        load_x = pltpu.make_async_copy(x_h, xb.at[:, pl.ds(0, IN)], ld.at[0])

        @pl.when(me_p < 3)
        def _():
            load_x.start()

        def greet(i, c):
            p, d = i // R, lax.rem(i, R)

            @pl.when((p != me_p) | (d != me_d))
            def _():
                pl.semaphore_signal(barrier, inc=1, device_id=(p, d), device_id_type=MESH)

            return c

        lax.fori_loop(0, NP * R, greet, 0)

        @pl.when(me_p == 0)
        def _():
            fetch_narrow(n1)

        @pl.when(me_p == 2)
        def _():
            fetch_wide(0, C_MID, lambda q: q * n3)

        ng_o[...] = jnp.zeros_like(ng_o)
        ngs[...] = jnp.zeros_like(ngs)
        for m in range(MICRO):
            lanes = lax.broadcasted_iota(jnp.int32, (1, W), 1)
            keep[m] = jnp.where(lanes < C_MID * width_step[m] // 4, 1.0, 0.0)

        pl.semaphore_wait(barrier, NP * R - 1)

        def lay_out(values, lanes, big_o, small_o, big_rows, side):
            fw[0, pl.ds(0, values.shape[0]), :] = values
            for r in range(big_rows // side):
                big_o[r, :, lanes] = fw[0, pl.ds(r * side, side), :].astype(BF)
            crops = geo.crops[1]
            for p in range(small_o.shape[0]):
                small_o[p, :, lanes] = fw[0, pl.ds(big_rows + p * crops, crops), :].astype(BF)

        def finals():
            arrived(orecv, out_r)
            for q in range(NQ):
                lay_out(orecv[q].astype(F32), pl.ds(q * W, W), ob_o, os_o, geo.out_big, geo.sides[0] // 2)
            arrived(srecv, sb_r)
            arrived(mrecv, mn_r)
            for h in range(2):
                total = mrecv[h].astype(F32) + dot_tn(ps[...], srecv[h])
                lay_out(total, pl.ds(h * W, W), gb_o, gs_o, geo.in_big, geo.sides[0])

        def sub_hop(k):
            ref = col.at[pl.ds(6, 2), k]
            return remote(ref, ref, xs_s.at[k], xs_r.at[k], 0, me_d)

        def sub_back(k):
            return (col.at[pl.ds(6, 2), k], srecv, sb_s.at[k], sb_r, my_m, k * G + my_c)

        def nt_copy(count):
            return remote(nt.at[pl.ds(0, count)], nt2.at[pl.ds(0, count)], nt_s, nt_r, me_p + 1, me_d)

        def main_copy(m):
            return (tgb.at[pl.ds(2 * m, 2), pl.ds(0, IN)], mrecv, mn_s.at[m], mn_r, m, me_d)

        def w1_here(q):
            return pl.multiple_of(q * W, W)

        def ng_copy():
            return remote(ngs.at[0], ngr.at[0, 0], stn_s.at[0], stn_r.at[0], 0, me_d)

        @pl.when(me_p == 0)
        def _():
            ship_all(w1_here, w1_at, 2, lambda copy: copy.start())
            nt_copy(1).start()
            load_x.wait()

            def dx(m, c):
                arrived(rbig.at[m, pl.ds(0, IN)], big_r.at[m])
                for h in range(2):
                    tgb[2 * m + h, pl.ds(0, IN), :] = dot_nt(rbig[m, pl.ds(0, IN), :], weight(h * W)).astype(BF)
                push(*main_copy(m))
                return c

            lax.fori_loop(0, MICRO, dx, 0)
            for h in range(2):
                total = dot_tn(xb[h, pl.ds(0, IN), :], rbig[0, pl.ds(0, IN), :])
                for m in range(1, MICRO):
                    total += dot_tn(xb[2 * m + h, pl.ds(0, IN), :], rbig[m, pl.ds(0, IN), :])
                keep_narrow(h * W, total)
            red = flat(n1 * LANES)
            launch(red)
            for k in range(MICRO):
                arrived(col.at[pl.ds(6, 2), k], xs_r.at[k])
                push(*sub_back(k))
            red.relay(everything)
            finish_flat(red)
            finals()
            arrived(ngr.at[0, 0], stn_r.at[0])
            ng_o[0] = ngr[0, 0]
            ship_all(w1_here, w1_at, 2, lambda copy: copy.wait_send())
            nt_copy(1).wait_send()
            for m in range(MICRO):
                pushed(*main_copy(m))
                pushed(*sub_back(m))

        @pl.when(me_p == 1)
        def _():
            A2, D2, D1 = MICRO, MICRO + 1, MICRO + 2
            fetch_narrow(n2)
            load_x.wait()
            take(w1_at, 2)
            arrived(nt2.at[pl.ds(0, 1)], nt_r)

            def first(m, c):
                fw[m, pl.ds(0, IN), :] = dot(xb[2 * m, pl.ds(0, IN), :], weight(n2)) + dot(
                    xb[2 * m + 1, pl.ds(0, IN), :], weight(n2 + W)
                )
                put(own_a, m, reduce_rows(1, runs_in, squares(lambda b, f: fw[m, rows(f), :]), 2))
                send_a(m)
                return c

            lax.fori_loop(0, MICRO, first, 0)

            def conv(m):
                finish_norm(total_a(m), m, nt2, 0, count_in)

                def act(b, f, bc, vc):
                    n = normed(fw[m, rows(f), :], m, bc)
                    stage[m, rows(f), :] = kept(n * sigmoid(n), m, bc).astype(BF)

                map_rows(1, runs_in, act)
                col[:, m] = dot(p2[...], stage[m, pl.ds(0, IN), :]).astype(BF).reshape(9, OUT, W)
                total = dot(col[0, m], weight(0))
                for tap in range(1, 9):
                    total += dot(col[tap, m], weight(tap * C_MID))
                fw[A2, block(m), :] = total
                put(own_a, MICRO + m, reduce_rows(1, runs_out, squares(lambda b, f: fw[A2, at(m, f), :]), 2))
                send_a(MICRO + m)

            def a2_copy(m, p):
                sems = sm_s if p == 2 else sm_t
                return (ssm.at[m], rsm.at[my_m], sems.at[m], sm_r.at[my_m], p, m * G + my_c)

            def give(m):
                slot = MICRO + m
                finish_norm(total_a(slot), slot, nt, 0, count_out)

                def act(b, f, bc, vc):
                    n = normed(fw[A2, at(m, f), :], slot, bc)
                    ssm[m, rows(f), :] = kept(n * sigmoid(n), m, bc).astype(BF)

                map_rows(1, runs_out, act)
                push(*a2_copy(m, 3))
                push(*a2_copy(m, 2))

            def forward(step, c):
                @pl.when(step < MICRO)
                def _():
                    conv(step)

                @pl.when(step > 0)
                def _():
                    give(step - 1)

                return c

            lax.fori_loop(0, MICRO + 1, forward, 0)

            def back_two(m):
                arrived(rsm.at[m], sm_r.at[m])
                slot = MICRO + m

                def sums(b, f, bc, vc):
                    u = fw[A2, at(m, f), :]
                    d = kept(rsm[m, rows(f), :].astype(F32) * slope_of(normed(u, slot, bc)), m, bc)
                    fw[D2, at(m, f), :] = d
                    return (d, d * centered(u, slot, bc))

                put(own_a, 2 * MICRO + m, reduce_rows(1, runs_out, sums, 2))
                send_a(2 * MICRO + m)

            def back_mid(m):
                total = total_a(2 * MICRO + m)
                slot = MICRO + m
                put_cof(0, total, count_out)
                add_norm_grads(ng_o, 0, total)

                def grad(b, f, bc, vc):
                    z = centered(fw[A2, at(m, f), :], slot, bc)
                    dwide[0, at(m, f), :] = back(fw[D2, at(m, f), :], z, 0, 0, slot, bc, vc)

                map_rows(1, runs_out, grad)

            def back_one(m):
                du = dwide[0, block(m), :]
                for tap in range(9):
                    tgb[tap, pl.ds(0, OUT), :] = dot_nt(du, weight(tap * C_MID)).astype(BF)
                taps = tgb[:, pl.ds(0, OUT), :].reshape(9 * OUT, W)
                stage[m, pl.ds(0, IN), :] = dot_tn(p2[...], taps).astype(BF)

                def sums(b, f, bc, vc):
                    u = fw[m, rows(f), :]
                    d = kept(stage[m, rows(f), :].astype(F32) * slope_of(normed(u, m, bc)), m, bc)
                    fw[D1 + m, rows(f), :] = d
                    return (d, d * centered(u, m, bc))

                put(own_a, 3 * MICRO + m, reduce_rows(1, runs_in, sums, 2))
                send_a(3 * MICRO + m)

            def du1_copy(m):
                ref = pl.ds(0, IN)
                return remote(stage.at[m, ref], rbig.at[m, ref], big_s.at[m], big_r.at[m], 0, me_d)

            def back_out(m):
                total = total_a(3 * MICRO + m)
                put_cof(0, total, count_in)
                add_norm_grads(ngs, 0, total)

                def grad(b, f, bc, vc):
                    z = centered(fw[m, rows(f), :], m, bc)
                    stage[m, rows(f), :] = back(fw[D1 + m, rows(f), :], z, 0, 0, m, bc, vc)

                map_rows(1, runs_in, grad)
                du1_copy(m).start()

            def backward(step, c):
                @pl.when(step < MICRO)
                def _():
                    back_two(step)

                @pl.when((step > 0) & (step <= MICRO))
                def _():
                    back_mid(step - 1)
                    back_one(step - 1)

                @pl.when(step > 1)
                def _():
                    back_out(step - 2)

                return c

            def weights(tap, c):
                keep_narrow(tap * C_MID, dot_tn(col[tap].reshape(ROWS, W), dwide[0, full, :]))
                return c

            lax.fori_loop(0, MICRO + 2, backward, 0)
            ng_copy().start()
            lax.fori_loop(0, 9, weights, 0)
            red = flat(n2 * LANES)
            launch(red)
            red.relay(everything)
            finals()
            finish_flat(red)
            pass_on(w1_at, 2, lambda ref, q, copy: copy.wait_send())
            ng_copy().wait_send()
            for m in range(MICRO):
                du1_copy(m).wait_send()
                pushed(*a2_copy(m, 2))
                pushed(*a2_copy(m, 3))
            for slot in range(4 * MICRO):
                drain_a(slot)

        def share_copy(k):
            return remote(ngs, ngr.at[k - 1], stn_s.at[k - 1], stn_r.at[k - 1], me_p, lax.rem(me_d + k * G, R))

        def share_norm_grads():
            ngs[...] = ng_o[...]
            for k in range(1, MICRO):
                share_copy(k).start()

        def take_norm_grads():
            for k in range(1, MICRO):
                arrived(ngr.at[k - 1], stn_r.at[k - 1])
                ng_o[...] += ngr[k - 1]
            for k in range(1, MICRO):
                share_copy(k).wait_send()

        def sub_copy(m):
            return (col.at[pl.ds(4, 2), m], col.at[pl.ds(0, 2), my_m], xs_s.at[m], xs_r.at[my_m], 2, m * G + my_c)

        def w3_here(q):
            return pl.multiple_of(q * n3, W)

        @pl.when(me_p == 2)
        def _():
            ship_all(w3_here, w3_at, NQ, lambda copy: copy.start())
            nt_copy(NQ).start()
            load_x.wait()

            def send_x(m, c):
                for h in range(2):
                    col[4 + h, m] = dot(ps[...], xb[2 * m + h, pl.ds(0, IN), :]).astype(BF)
                push(*sub_copy(m))
                return c

            lax.fori_loop(0, MICRO, send_x, 0)
            fetch_wide(C_MID, C_IN, lambda q: q * n3 + C_MID)
            for k in range(MICRO):
                arrived(col.at[pl.ds(0, 2), k], xs_r.at[k])

            def w3(q):
                return weight(q * n3)

            def wp(q, h):
                return weight(q * n3 + C_MID + h * W)

            def xsub(h):
                return col[h].reshape(ROWS, W)

            def product(index, value, slot):
                fw[index, full, :] = value
                put(own_b, slot, reduce_rows(MICRO, runs_out, squares(lambda b, f: fw[index, at(b, f), :]), 2))
                send_b(slot)

            def up_copy(q):
                return remote(stage.at[q, full], stage.at[q, full], up_s.at[q], up_r.at[q], 3, me_d)

            def short(q):
                product(NQ + q, dot(xsub(0), wp(q, 0)) + dot(xsub(1), wp(q, 1)), NQ + q)

            def short_out(q):
                finish_norm(total_b(NQ + q), NQ + q, nt, NQ + q, count_out)

                def act(b, f, bc, vc):
                    stage[q, at(b, f), :] = normed(fw[NQ + q, at(b, f), :], NQ + q, bc).astype(BF)

                map_rows(MICRO, runs_out, act)
                up_copy(q).start()

            def shorts(step, c):
                @pl.when(step < NQ)
                def _():
                    short(step)

                @pl.when(step > 0)
                def _():
                    short_out(step - 1)

                return c

            lax.fori_loop(0, NQ + 1, shorts, 0)
            for k in range(MICRO):
                arrived(rsm.at[k], sm_r.at[k])

            def main(q, c):
                product(q, dot(rsm[...].reshape(ROWS, W), w3(q)), q)
                return c

            lax.fori_loop(0, NQ, main, 0)

            def main_norm(q, c):
                finish_norm(total_b(q), q, nt, q, count_out)
                return c

            lax.fori_loop(0, NQ, main_norm, 0)
            tmp[...] = jnp.zeros_like(tmp)
            red = Reduction(
                NQ, PRQ, lambda s, pc: (pc * S2 + s) * PRQ, lambda s, pc: s < S2
            )
            D, SUB = 2 * NQ, 2 * NQ + 1

            def lay_part(s, q):
                start = pl.multiple_of((q * S2 + s) * PRQ, CH)
                at_s = pl.multiple_of(s * RW * LANES, 8)
                dwl[pl.ds(start, RW * LANES), :] = tmp[pl.ds(at_s, RW * LANES), :].astype(BF)

            for q in range(NQ):
                arrived(rbig.at[q, full], big_r.at[q])

                def sums(b, f, bc, vc):
                    um, us = fw[q, at(b, f), :], fw[NQ + q, at(b, f), :]
                    n = normed(um, q, bc) + normed(us, NQ + q, bc)
                    d = rbig[q, at(b, f), :].astype(F32) * slope_of(n)
                    fw[D, at(b, f), :] = d
                    return (d, d * centered(um, q, bc), d * centered(us, NQ + q, bc))

                db, mb, sb, ds, ms, ss = reduce_rows(MICRO, runs_out, sums, 3)
                put(own_b, 2 * NQ + q, (db, mb, ds, ms))
                put(own_b, 3 * NQ + q, (db, sb, ds, ss))
                send_b(2 * NQ + q)
                send_b(3 * NQ + q)
                for i, cb in ((0, q), (1, NQ + q)):
                    total = total_b((2 + i) * NQ + q)
                    put_cof(i, total, count_out)
                    add_norm_grads(ng_o, cb, total)

                def grad(b, f, bc, vc):
                    d = fw[D, at(b, f), :]
                    zm = centered(fw[q, at(b, f), :], q, bc)
                    zs = centered(fw[NQ + q, at(b, f), :], NQ + q, bc)
                    dwide[q, at(b, f), :] = back(d, zm, 0, 0, q, bc, vc)
                    dwide[NQ + q, at(b, f), :] = back(d, zs, 1, 1, NQ + q, bc, vc)

                map_rows(MICRO, runs_out, grad)
                lay_narrow(0, dot_tn(rsm[...].reshape(ROWS, W), dwide[q, full, :]))
                for h in range(2):
                    lay_narrow((1 + h) * W * LANES, dot_tn(xsub(h), dwide[NQ + q, full, :]))

                def lay(s, c):
                    lay_part(s, q)
                    return c

                lax.fori_loop(0, S2, lay, 0)
                red.send_pairs((q,))
                for h in range(2):
                    piece = dot_nt(dwide[NQ + q, full, :], wp(q, h))
                    fw[SUB + h, full, :] = piece if q == 0 else fw[SUB + h, full, :] + piece
                red.originate((q,))

            share_norm_grads()
            for h in range(2):
                for k in range(MICRO):
                    col[6 + h, k] = fw[SUB + h, block(k), :].astype(BF)
            for m in range(MICRO):
                pushed(*sub_copy(m))
            for k in range(MICRO):
                sub_hop(k).start()
            for q in range(NQ):
                red.relay((q,))
            finals()
            take_norm_grads()
            for q in range(NQ):

                def store(at_s, s, v):
                    tmp[pl.ds(pl.multiple_of(SR + s * red.step, CH), red.step), :] = v

                red.finish(q, store)

                @pl.when(red.used(me_d, q))
                def _():
                    for lane in range(LANES):
                        values = tmp[pl.ds(SR + lane, RW, stride=LANES), :]
                        tmp[pl.ds(q * LANES + lane, RW, stride=NQ * LANES), :] = values

            @pl.when(jnp.logical_not(red.used(me_d, 0)))
            def _():
                tmp[pl.ds(0, SR), :] = jnp.zeros((SR, 128), F32)

            weights_out()
            red.drain()
            ship_all(w3_here, w3_at, NQ, lambda copy: copy.wait_send())
            nt_copy(NQ).wait_send()
            for k in range(MICRO):
                sub_hop(k).wait_send()
            for q in range(NQ):
                up_copy(q).wait_send()
            for slot in range(4 * NQ):
                drain_b(slot)

        def cot_copy(m):
            return (cot_h.at[m], xb.at[pl.ds(0, NQ), block(my_m)], ct_s.at[m], ct_r.at[my_m], 3, m * G + my_c)

        def gate_copy(m):
            return (gate_v.at[m], gateb.at[my_m], gt_s.at[m], gt_r.at[my_m], 3, m * G + my_c)

        def out_copy(k):
            return (xb.at[pl.ds(NQ, NQ), block(k)], orecv, out_s.at[k], out_r, my_m, k * G + my_c)

        @pl.when(me_p == 3)
        def _():
            r = lax.broadcasted_iota(jnp.int32, (OUT, 128), 0)
            small = r - geo.out_big
            for m in range(MICRO):
                g = jnp.zeros((OUT, 128), F32)
                for i in range(geo.crops[0]):
                    area = geo.out_big // geo.crops[0]
                    g = jnp.where((r >= i * area) & (r < (i + 1) * area), gate_big[i, m].astype(F32), g)
                for i in range(geo.crops[1]):
                    mine = (small >= 0) & (lax.rem(small + geo.crops[1] * OUT, geo.crops[1]) == i)
                    g = jnp.where(mine, gate_small[i, m].astype(F32), g)
                gate_v[m] = g
            for m in range(MICRO):
                push(*gate_copy(m))
                push(*cot_copy(m))
            fetch_narrow(nab)
            fetch_wide(nab * W // C_OUT, C_MID, lambda q: nab + q * C_MID)
            take(w3_at, NQ)
            arrived(nt2, nt_r)
            A, B, T1, T2, U3 = 2 * NQ, 2 * NQ + 1, 2 * NQ + 2, 2 * NQ + 3, 2 * NQ + 4
            DB, DA, H1, H2 = NQ, NQ + 1, NQ + 2, NQ + 3
            S3, PM = 4 + 2 * NQ, 2 + NQ

            def wa(q):
                return weight(q * W)

            def wb(tap):
                return weight(C_OUT + tap * C_MID)

            def wc(q):
                return weight(nab + q * C_MID)

            def w3(q):
                return weight(nabc + q * C_MID)

            def accumulate(index, i, value):
                @pl.when(i == 0)
                def _():
                    fw[index, full, :] = value

                @pl.when(i > 0)
                def _():
                    fw[index, full, :] += value

            def begin(index, slot):
                put(own_b, slot, reduce_rows(MICRO, runs_out, squares(lambda b, f: fw[index, at(b, f), :]), 2))
                send_b(slot)

            def hidden(index, slot, target):
                def act(b, f, bc, vc):
                    n = normed(fw[index, at(b, f), :], slot, bc)
                    dwide[target, at(b, f), :] = kept(n * sigmoid(n), my_m, bc).astype(BF)

                map_rows(MICRO, runs_out, act)

            def gather(source, target):
                def one(k, c):
                    target(k, dot(pb[...], dwide[source, block(k), :]).astype(BF).reshape(9, OUT, W))
                    return c

                lax.fori_loop(0, MICRO, one, 0)

            for k in range(MICRO):
                arrived(rsm.at[k], sm_r.at[k])

            def main(q, c):
                fw[U3 + q, full, :] = dot(rsm[...].reshape(ROWS, W), w3(q))
                begin(U3 + q, S3 + q)
                return c

            lax.fori_loop(0, NQ, main, 0)

            def join(q, c):
                finish_norm(total_b(S3 + q), PM + q, nt2, q, count_out)
                arrived(stage.at[q, full], up_r.at[q])

                def act(b, f, bc, vc):
                    n = normed(fw[U3 + q, at(b, f), :], PM + q, bc) + stage[q, at(b, f), :].astype(F32)
                    rbig[q, at(b, f), :] = (n * sigmoid(n)).astype(BF)

                map_rows(MICRO, runs_out, act)
                accumulate(A, q, dot(rbig[q, full, :], wa(q)))
                return c

            lax.fori_loop(0, NQ, join, 0)
            begin(A, 0)
            finish_norm(total_b(0), 0, nt, 0, count_out)
            hidden(A, 0, H1)

            def to_col(k, v):
                col[:, k] = v

            gather(H1, to_col)

            def conv(tap, c):
                accumulate(B, tap, dot(col[tap].reshape(ROWS, W), wb(tap)))
                return c

            lax.fori_loop(0, 9, conv, 0)
            begin(B, 1)
            finish_norm(total_b(1), 1, nt, 1, count_out)
            hidden(B, 1, H2)

            def widen(q, c):
                fw[q, full, :] = dot(dwide[H2, full, :], wc(q))
                begin(q, 2 + q)
                return c

            lax.fori_loop(0, NQ, widen, 0)
            for k in range(MICRO):
                arrived(gateb.at[k], gt_r.at[k])
                arrived(xb.at[pl.ds(0, NQ), block(k)], ct_r.at[k])

            def gate_at(b, f):
                g = gateb[b, rows(f), :]
                return jnp.concatenate([g] * LANES, axis=1)

            def ends(q, c):
                finish_norm(total_b(2 + q), 2 + q, nt, 2 + q, count_out)

                def sums(b, f, bc, vc):
                    u = fw[q, at(b, f), :]
                    g = gate_at(b, f)
                    v = rbig[q, at(b, f), :].astype(F32) + g * normed(u, 2 + q, bc)
                    sg = sigmoid(v)
                    xb[NQ + q, at(b, f), :] = (v * sg).astype(BF)
                    d = xb[q, at(b, f), :].astype(F32) * (sg * (1.0 + v * (1.0 - sg)))
                    fw[NQ + q, at(b, f), :] = d
                    d = g * d
                    return (d, d * centered(u, 2 + q, bc))

                put(own_b, 2 + NQ + q, reduce_rows(MICRO, runs_out, sums, 2))
                send_b(2 + NQ + q)
                return c

            lax.fori_loop(0, NQ, ends, 0)

            def ends_back(q, c):
                total = total_b(2 + NQ + q)
                put_cof(0, total, count_out)
                add_norm_grads(ng_o, 2 + q, total)

                def grad(b, f, bc, vc):
                    z = centered(fw[q, at(b, f), :], 2 + q, bc)
                    d = gate_at(b, f) * fw[NQ + q, at(b, f), :]
                    dwide[q, at(b, f), :] = back(d, z, 0, 0, 2 + q, bc, vc)

                map_rows(MICRO, runs_out, grad)
                accumulate(T1, q, dot_nt(dwide[q, full, :], wc(q)))
                return c

            lax.fori_loop(0, NQ, ends_back, 0)
            for k in range(MICRO):
                push(*out_copy(k))

            def middle(index, pslot, slot, target):
                def sums(b, f, bc, vc):
                    u = fw[index, at(b, f), :]
                    d = kept(fw[T1, at(b, f), :] * slope_of(normed(u, pslot, bc)), my_m, bc)
                    fw[T2, at(b, f), :] = d
                    return (d, d * centered(u, pslot, bc))

                put(own_b, slot, reduce_rows(MICRO, runs_out, sums, 2))
                send_b(slot)
                total = total_b(slot)
                put_cof(0, total, count_out)
                add_norm_grads(ng_o, pslot, total)

                def grad(b, f, bc, vc):
                    z = centered(fw[index, at(b, f), :], pslot, bc)
                    dwide[target, at(b, f), :] = back(fw[T2, at(b, f), :], z, 0, 0, pslot, bc, vc)

                map_rows(MICRO, runs_out, grad)

            middle(B, 1, 2 + 2 * NQ, DB)

            def to_taps(k, v):
                tgb[:, block(k), :] = v

            gather(DB, to_taps)

            def conv_back(tap, c):
                accumulate(T1, tap, dot_nt(tgb[tap, full, :], wb(8 - tap)))
                return c

            lax.fori_loop(0, 9, conv_back, 0)
            middle(A, 0, 3 + 2 * NQ, DA)

            def dy_copy(q):
                return remote(stage.at[q, full], rbig.at[q, full], big_s.at[q], big_r.at[q], 2, me_d)

            def to_y(q, c):
                fw[T2, full, :] = dot_nt(dwide[DA, full, :], wa(q))

                def sums(b, f, bc, vc):
                    dy = (fw[T2, at(b, f), :] + fw[NQ + q, at(b, f), :]).astype(BF)
                    u = fw[U3 + q, at(b, f), :]
                    n = normed(u, PM + q, bc) + stage[q, at(b, f), :].astype(F32)
                    stage[q, at(b, f), :] = dy
                    d = dy.astype(F32) * slope_of(n)
                    fw[q, at(b, f), :] = d
                    return (d, d * centered(u, PM + q, bc))

                put(own_b, S3 + NQ + q, reduce_rows(MICRO, runs_out, sums, 2))
                send_b(S3 + NQ + q)
                dy_copy(q).start()
                return c

            lax.fori_loop(0, NQ, to_y, 0)

            def through_w3(q, c):
                put_cof(0, total_b(S3 + NQ + q), count_out)

                def grad(b, f, bc, vc):
                    z = centered(fw[U3 + q, at(b, f), :], PM + q, bc)
                    xb[q, at(b, f), :] = back(fw[q, at(b, f), :], z, 0, 0, PM + q, bc, vc)

                map_rows(MICRO, runs_out, grad)
                accumulate(T1, q, dot_nt(xb[q, full, :], w3(q)))
                return c

            lax.fori_loop(0, NQ, through_w3, 0)

            def da2_copy(k):
                return remote(ssm.at[k], rsm.at[my_m], sm_s.at[k], sm_r.at[my_m], 1, k * G + my_c)

            def back_a2(k, c):
                ssm[k] = fw[T1, block(k), :].astype(BF)
                da2_copy(k).start()
                return c

            lax.fori_loop(0, MICRO, back_a2, 0)

            def weights_a(q, c):
                keep_narrow(q * W, dot_tn(rbig[q, full, :], dwide[DA, full, :]))
                return c

            def weights_b(tap, c):
                keep_narrow(C_OUT + tap * C_MID, dot_tn(col[tap].reshape(ROWS, W), dwide[DB, full, :]))
                return c

            share_norm_grads()
            red = flat(nabc * LANES)
            t1, t2 = (C_OUT + C_MID) * LANES // (2 * SR), -(-(nab - C_MID) * LANES // (2 * SR))
            order = ((t2, N), (0, t1), (t1, t2))
            keep_wide(nab * W // C_OUT, lambda r: dwide[H2, full, r], 0)
            weights_b(8, 0)
            launch(red, *order[0])
            lax.fori_loop(0, NQ, weights_a, 0)
            weights_b(0, 0)
            launch(red, *order[1])
            lax.fori_loop(1, 8, weights_b, 0)
            launch(red, *order[2])
            for low, high in order:
                red.relay(everything, low, high)
            finals()
            take_norm_grads()
            finish_flat(red)
            pass_on(w3_at, NQ, lambda ref, q, copy: copy.wait_send())
            for m in range(MICRO):
                pushed(*gate_copy(m))
                pushed(*cot_copy(m))
                pushed(*out_copy(m))
                da2_copy(m).wait_send()
            for q in range(NQ):
                dy_copy(q).wait_send()
            for slot in range(S3 + 2 * NQ):
                drain_b(slot)

    return kernel


def radix(count, most):
    if count <= most:
        return count
    return next(r for r in range(most, 0, -1) if count % r == 0)


def handed_on(arrays):
    count = len(arrays)

    def kernel(*refs):
        for i in range(count):
            refs[count + i][...] = refs[i][...]

    vmem = pl.BlockSpec(memory_space=pltpu.VMEM)
    return pl.pallas_call(
        kernel,
        out_shape=tuple(jax.ShapeDtypeStruct(a.shape, a.dtype) for a in arrays),
        in_specs=[vmem] * count,
        out_specs=(vmem,) * count,
    )(*arrays)


def solution(mesh):
    R, NP = mesh.shape["dp"], mesh.shape["pipe"]

    def on_device(x_big, x_small, cot_big, cot_small, section_weights, section_norms, gate_big, gate_small, width_step):
        MICRO = x_big.shape[0]
        G = R // MICRO
        geo = Geometry((x_big.shape[1], x_small.shape[1]), (x_big.shape[2], x_small.shape[2]))
        IN, OUT, ROWS = geo.IN, geo.OUT, MICRO * geo.OUT
        PW = section_weights.shape[1]
        NB = section_norms.shape[2] // W
        wide = max(IN, ROWS)

        def joined(big, small, width, length):
            parts = [big.reshape(MICRO, -1, width), small.transpose(0, 2, 3, 1, 4).reshape(MICRO, -1, width)]
            v = jnp.concatenate(parts, axis=1)
            return jnp.pad(v, ((0, 0), (0, length - v.shape[1]), (0, 0)))

        x = joined(x_big, x_small, C_IN, IN)
        x = x.reshape(MICRO, IN, 2, W).transpose(0, 2, 1, 3).reshape(2 * MICRO, IN, W)
        cot = joined(cot_big, cot_small, C_OUT, OUT).reshape(MICRO, OUT, NQ, W).transpose(0, 2, 1, 3)
        w4 = section_weights.reshape(PW // W, LANES, 1, 128)
        w16 = section_weights.reshape(PW // C_OUT, NQ * LANES, 1, 128)
        SR = PW // 128 // R
        PC = 4 if SR % (4 * CH) == 0 else 2 if SR % (2 * CH) == 0 else 1
        RW = SR // (NQ * LANES)
        SRP = max(SR, NQ * up16(RW * LANES))
        tmp_rows = max(HALF * NQ * LANES, -(-(C_MID + C_IN) // RW) * RW * LANES, SR + up16(RW * LANES))
        nt = section_norms[0].reshape(4, NB, W).transpose(1, 0, 2)
        p2 = geo.windows(2)
        sub = geo.every_second()
        consts = [p2, geo.windows(1), sub]
        consts = [jnp.asarray(c, BF) for c in consts]
        vmem, hbm = pl.BlockSpec(memory_space=pltpu.VMEM), pl.BlockSpec(memory_space=pl.ANY)
        smem = pl.BlockSpec(memory_space=pltpu.SMEM)
        V, D = pltpu.VMEM, pltpu.SemaphoreType.DMA
        RA, RB = radix(R, 8), radix(G, 4)
        nb, sb, ns, ss = geo.crops[0], geo.sides[0], geo.crops[1], geo.sides[1]
        SA, SB = 4 * MICRO, 4 + 4 * NQ

        def sums(slots, first, all_of):
            later = max(all_of // first - 1, 1)
            kept_slots = slots if all_of > first else 1
            return [
                V((slots, 4, W), F32),
                V((slots, max(first - 1, 1), 4, W), F32),
                V((kept_slots, 4, W), F32),
                V((kept_slots, later, 4, W), F32),
            ]

        results = pl.pallas_call(
            make_kernel(geo, R, NP, MICRO, SR, PC),
            out_shape=(
                jax.ShapeDtypeStruct((nb * sb // 2, sb // 2, C_OUT), BF),
                jax.ShapeDtypeStruct((ss * ss // 4, ns, C_OUT), BF),
                jax.ShapeDtypeStruct((nb * sb, sb, C_IN), BF),
                jax.ShapeDtypeStruct((ss * ss, ns, C_IN), BF),
                jax.ShapeDtypeStruct((SR, 128), F32),
                jax.ShapeDtypeStruct((NB, 4, W), F32),
            ),
            in_specs=[hbm, hbm, smem, smem, smem, hbm, hbm, vmem] + [vmem] * 3,
            out_specs=(vmem, vmem, vmem, vmem, hbm, vmem),
            scratch_shapes=[
                V((PW // W + C_OUT, W), BF),
                V((2, LANES, 128, 1, 128), BF),
                V((2 * MICRO, wide, W), BF),
                V((MICRO, OUT, 128), F32),
                V((MICRO, OUT, 128), F32),
                V((MICRO, 1, W), F32),
                V((NQ, wide, W), BF),
                V((NQ, wide, W), BF),
                V((MICRO, OUT, W), BF),
                V((MICRO, OUT, W), BF),
                V((3 * NQ + 4, wide, W), F32),
                V((2 * NQ, wide, W), BF),
                V((9, MICRO, OUT, W), BF),
                V((9, wide, W), BF),
                V((tmp_rows, 128), F32),
                V((2, IN, W), BF),
                V((2, OUT, W), BF),
                V((NQ, OUT, W), BF),
                V((PW // 128, 128), BF),
                V((R // 2, SRP, 128), BF),
                V((R // 2 + 1, SRP, 128), BF),
                V((NQ, 4, W), F32),
                *sums(SA, RA, R),
                *sums(SB, RB, G),
                V((max(2 * MICRO, 2 + 2 * NQ), 8, W), F32),
                V((2, 4, W), F32),
                V((NB, 4, W), F32),
                V((MICRO - 1, NB, 4, W), F32),
                D((2,)),
                D((2, LANES)),
                D((4,)), D((4,)),
                D((4,)), D((4,)), D((4,)),
                D((4,)), D((4,)),
                D((4,)), D((4,)),
                D((4,)), D((4,)),
                D((4,)), D((4,)),
                D((4,)), D((4,)),
                D, D,
                D((4,)), D,
                D((4,)), D,
                D((4,)), D,
                D((SA,)), D((SA,)), D((SA,)), D((SA,)),
                D((SB,)), D((SB,)), D((SB,)), D((SB,)),
                D((MICRO - 1,)), D((MICRO - 1,)),
                D((R // 2, 4)), D((R // 2, 4)),
                D((R // 2, 4)), D((R // 2 + 1, 4)),
            ],
            compiler_params=pltpu.CompilerParams(
                collective_id=0, has_side_effects=True, vmem_limit_bytes=63 << 20
            ),
        )(x, cot, gate_big.T, gate_small.T, width_step, w4, w16, nt, *consts)

        ob, os, gb, gs, dw, ng = handed_on(results)

        def small(v, side, width):
            return v.reshape(side, side, ns, width).transpose(2, 0, 1, 3)[None]

        return (
            ob.reshape(1, nb, sb // 2, sb // 2, C_OUT),
            small(os, ss // 2, C_OUT),
            gb.reshape(1, nb, sb, sb, C_IN),
            small(gs, ss, C_IN),
            dw.reshape(1, PW // R),
            ng.transpose(1, 0, 2).reshape(1, 4, NB * W),
        )

    images = P(None, "dp", None, None, None)
    ends = P("pipe", "dp", None, None, None)
    return jax.shard_map(
        on_device,
        mesh=mesh,
        in_specs=(images,) * 4 + (P("pipe", None), P("pipe", None, None), P(None, "dp"), P(None, "dp"), P()),
        out_specs=(ends,) * 4 + (P("pipe", "dp"), P("pipe", None, None)),
        check_vma=False,
    )
```

time: 264 us -> 222 us (0.84)
  the two profiles are of different devices: /device:TPU:20 before, /device:TPU:10 now
where the time goes in v2:
time: 222 us; the launch traced here: 219 us
  Pallas kernels  211 us (95%)
  local copies, waits for them, and re-layouts  5.82 us (3%)
    pallas_call x1, Pallas kernels, on_device(): pl.pallas_call(make_kernel(geo, R, NP, MICRO, SR, PC), out_shape=(jax.Sha...  207 us

profile of v2, /device:TPU:10, one launch (start us, length us, event | category | flops | bytes accessed | tf_op | source)
XLA Modules:
  0.0 219.5 jit_solution(5197645162717002840)
XLA Ops:
  0.6 0.0 copy-start.1
  0.6 1.2 copy.21
  1.8 0.2 copy.23
  2.0 2.0 reshape.56
  4.0 0.0 copy-done.1
  4.0 0.4 copy.22
  4.5 0.0 copy-start
  4.5 0.2 fusion.5
  4.7 1.2 copy.27
  5.9 0.2 copy-done
  6.1 0.5 copy.20
  6.6 0.4 fusion.4
  7.0 0.2 fusion.6
  7.1 1.5 pad_maximum_fusion
  8.7 207.1 %shard_map.163 = (bf16[7,7,2048]{2,1,0:T(8,128)(2,1)}, bf16[9,2,2048]{2,1,0:T(2,128)(2,1)}, bf16[14,14,1024]{2,1,0:T(8,128)(2,1)}, bf16[36,2,1024]{2,1,0:T(2,128...) custom-call(bf16[8,272,512]{2,1,0:T(8,128)(2,1)} %bitcast.38, bf16[4,4,80,512]{3,2,1,0:T(8,128)(2,1)} %bitcast.39, ...), custom_call_target="tpu_custom_call" | custom-call | tf_op jit(solution)/shard_map/pallas_call | solution.py:1370
  215.8 3.7 %shard_map.164 = (bf16[7,7,2048]{2,1,0:T(8,128)(2,1)}, bf16[9,2,2048]{2,1,0:T(2,128)(2,1)}, bf16[14,14,1024]{2,1,0:T(8,128)(2,1)}, bf16[36,2,1024]{2,1,0:T(2,128...) custom-call(bf16[7,7,2048]{2,1,0:T(8,128)(2,1)} %get-tuple-element.18.refs_0_, ...), custom_call_target="tpu_custom_call" | custom-call | tf_op jit(solution)/shard_map/pallas_call | solution.py:1313
Async XLA Ops:
  0.6 3.4 %copy-start.1 = (bf16[4,1,7,7,2048]{4,0,3,2,1:T(4,128)(2,1)S(1)}, bf16[4,1,7,7,2048]{4,0,3,2,1:T(4,128)(2,1)}, u32[]{:S(2)}) copy-start(bf16[4,1,7,7,2048]{4,0,3,2,1:T(4,128)(2,1)} %param.14) | copy-start | bytes 2408452
  4.5 1.6 copy-start

commit v3 on v2

--- a/solution.py
+++ b/solution.py
@@ -329,7 +329,7 @@
                 ref[cb, pl.ds(2 * g, 1), :] += total[2 * g + 1 : 2 * g + 2]
                 ref[cb, pl.ds(2 * g + 1, 1), :] += total[2 * g : 2 * g + 1]
 
-        HW = raw.shape[2]
+        SLOTS, HW = raw.shape[0], raw.shape[2]
 
         def fetch(count, source, target):
             def copies(b, slot):
@@ -338,15 +338,16 @@
                     for lane in range(LANES)
                 ]
 
-            for copy in copies(0, 0):
-                copy.start()
+            for ahead in range(min(SLOTS - 1, count)):
+                for copy in copies(ahead, ahead):
+                    copy.start()
 
             def one(b, c):
-                slot = lax.rem(b, 2)
-
-                @pl.when(b + 1 < count)
+                slot = lax.rem(b, SLOTS)
+
+                @pl.when(b + SLOTS - 1 < count)
                 def _():
-                    for copy in copies(b + 1, 1 - slot):
+                    for copy in copies(b + SLOTS - 1, lax.rem(b + SLOTS - 1, SLOTS)):
                         copy.start()
 
                 for lane, copy in enumerate(copies(b, slot)):
@@ -368,16 +369,14 @@
                 lambda b: target(b // per) + lax.rem(b, per) * HW,
             )
 
-        def ship(source, target, q):
-            return remote(wbuf.at[pl.ds(source(q), W)], wbuf.at[pl.ds(target(q), W)], w_s.at[q], w_r.at[q], me_p + 1, me_d)
-
-        def ship_all(source, target, count, go):
-            for i in range(count // 2):
-                go(ship(source, target, core * (count // 2) + i))
+        def halves(count):
+            return [core * (count // 2) + i for i in range(count // 2)]
+
+        def ship(source, target, q, ss, p):
+            return remote(wbuf.at[pl.ds(source(q), W)], wbuf.at[pl.ds(target(q), W)], ss.at[q], w_r.at[q], p, me_d)
 
         def pass_on(target, count, go):
-            for i in range(count // 2):
-                q = core * (count // 2) + i
+            for q in halves(count):
                 ref = wbuf.at[pl.ds(target(q), W)]
                 go(ref, q, remote(ref, ref, w_s.at[q], w_r.at[q], me_p, sibling))
 
@@ -396,6 +395,9 @@
 
         def w3_at(q):
             return pl.multiple_of(nabc + q * W, W)
+
+        def w3_between(q):
+            return pl.multiple_of(n1 + q * W, W)
 
         def lay_narrow(first, grad):
             for lane in range(LANES):
@@ -423,7 +425,18 @@
                 self.i = me_d // 2
 
             def at(self, pc):
-                return pl.ds(pc * self.rows_of, self.rows_of)
+                return pl.ds(pl.multiple_of(pc * self.rows_of, CH), self.rows_of)
+
+            def each(self, pcs, fn):
+                if len(pcs) == 1:
+                    fn(pcs[0])
+                    return
+
+                def one(pc, c):
+                    fn(pc)
+                    return c
+
+                lax.fori_loop(pcs[0], pcs[-1] + 1, one, 0)
 
             def pair(self, t, pc):
                 src = dwl.at[pl.ds(pl.multiple_of(self.start(2 * t + 1 - core, pc), CH), self.rows_of)]
@@ -455,12 +468,13 @@
             def send_pairs(self, pcs, low=0, high=N):
                 def one(j, c):
                     t = jnp.where(lax.rem(j, 2) == 0, high - 1 - j // 2, low + j // 2)
-                    for pc in pcs:
-
+
+                    def send(pc):
                         @pl.when(self.used(2 * t + 1 - core, pc))
-                        def _(pc=pc):
+                        def _():
                             self.pair(t, pc).start()
 
+                    self.each(pcs, send)
                     return c
 
                 lax.fori_loop(0, high - low, one, 0)
@@ -480,9 +494,12 @@
             def originate(self, pcs, low=0, high=N):
                 def one(j, c):
                     right, left = high - 1 - j, low + j
-                    for pc in pcs:
+
+                    def both(pc):
                         self.forward(right, pc, (self.i == 0) & (right > 0), False, self.rightward)
                         self.forward(left, pc, (self.i == N - 1) & (left < N - 1), False, self.leftward)
+
+                    self.each(pcs, both)
                     return c
 
                 lax.fori_loop(0, high - low, one, 0)
@@ -490,9 +507,12 @@
             def relay(self, pcs, low=0, high=N):
                 def one(j, c):
                     right, left = high - 1 - j, low + j
-                    for pc in pcs:
+
+                    def both(pc):
                         self.forward(right, pc, (self.i > 0) & (right > self.i), True, self.rightward)
                         self.forward(left, pc, (self.i < N - 1) & (left < self.i), True, self.leftward)
+
+                    self.each(pcs, both)
                     return c
 
                 lax.fori_loop(0, high - low, one, 0)
@@ -518,20 +538,20 @@
 
             def drain(self):
                 def one(j, c):
-                    for pc in range(self.pieces):
-
+                    def waits(pc):
                         @pl.when(self.used(2 * j + 1 - core, pc))
-                        def _(pc=pc):
+                        def _():
                             self.pair(j, pc).wait_send()
 
                         @pl.when((j > self.i) & self.used(2 * j + core, pc))
-                        def _(pc=pc):
+                        def _():
                             self.rightward(j, pc).wait_send()
 
                         @pl.when((j < self.i) & self.used(2 * j + core, pc))
-                        def _(pc=pc):
+                        def _():
                             self.leftward(j, pc).wait_send()
 
+                    self.each(range(self.pieces), waits)
                     return c
 
                 lax.fori_loop(0, N, one, 0)
@@ -555,12 +575,14 @@
 
         def finish_flat(red):
             tmp[pl.ds(0, SR), :] = jnp.zeros((SR, 128), F32)
-            for pc in everything:
-
+
+            def finish(pc):
                 def store(at_s, s, v):
                     tmp[pl.ds(pl.multiple_of(pc * PR + s * red.step, CH), red.step), :] = v
 
                 red.finish(pc, store)
+
+            red.each(everything, finish)
             weights_out()
             red.drain()
 
@@ -632,27 +654,73 @@
         def w1_here(q):
             return pl.multiple_of(q * W, W)
 
-        def ng_copy():
-            return remote(ngs.at[0], ngr.at[0, 0], stn_s.at[0], stn_r.at[0], 0, me_d)
+        def section_0(m, first):
+            fw[m, pl.ds(0, IN), :] = dot(xb[2 * m, pl.ds(0, IN), :], weight(first)) + dot(
+                xb[2 * m + 1, pl.ds(0, IN), :], weight(first + W)
+            )
+            put(own_a, m, reduce_rows(1, runs_in, squares(lambda b, f: fw[m, rows(f), :]), 2))
+            send_a(m)
 
         @pl.when(me_p == 0)
         def _():
-            ship_all(w1_here, w1_at, 2, lambda copy: copy.start())
+            for q in halves(2):
+                ship(w1_here, w1_at, q, w_s, 1).start()
             nt_copy(1).start()
+            for q in halves(NQ):
+                arrived(wbuf.at[pl.ds(w3_between(q), W)], w_r.at[q])
+                ship(w3_between, w3_at, q, big_s, 3).start()
             load_x.wait()
 
-            def dx(m, c):
+            def first(m, c):
+                section_0(m, 0)
+                return c
+
+            lax.fori_loop(0, MICRO, first, 0)
+            for m in range(MICRO):
+                finish_norm(total_a(m), m, nt, 0, count_in)
+
+            def back_sums(m):
                 arrived(rbig.at[m, pl.ds(0, IN)], big_r.at[m])
+
+                def sums(b, f, bc, vc):
+                    u = fw[m, rows(f), :]
+                    d = kept(rbig[m, rows(f), :].astype(F32) * slope_of(normed(u, m, bc)), m, bc)
+                    fw[MICRO + m, rows(f), :] = d
+                    return (d, d * centered(u, m, bc))
+
+                put(own_a, MICRO + m, reduce_rows(1, runs_in, sums, 2))
+                send_a(MICRO + m)
+
+            def dx(m):
+                total = total_a(MICRO + m)
+                put_cof(0, total, count_in)
+                add_norm_grads(ng_o, 0, total)
+
+                def grad(b, f, bc, vc):
+                    z = centered(fw[m, rows(f), :], m, bc)
+                    dwide[m, rows(f), :] = back(fw[MICRO + m, rows(f), :], z, 0, 0, m, bc, vc)
+
+                map_rows(1, runs_in, grad)
                 for h in range(2):
-                    tgb[2 * m + h, pl.ds(0, IN), :] = dot_nt(rbig[m, pl.ds(0, IN), :], weight(h * W)).astype(BF)
+                    tgb[2 * m + h, pl.ds(0, IN), :] = dot_nt(dwide[m, pl.ds(0, IN), :], weight(h * W)).astype(BF)
                 push(*main_copy(m))
-                return c
-
-            lax.fori_loop(0, MICRO, dx, 0)
+
+            def backward(step, c):
+                @pl.when(step < MICRO)
+                def _():
+                    back_sums(step)
+
+                @pl.when(step > 0)
+                def _():
+                    dx(step - 1)
+
+                return c
+
+            lax.fori_loop(0, MICRO + 1, backward, 0)
             for h in range(2):
-                total = dot_tn(xb[h, pl.ds(0, IN), :], rbig[0, pl.ds(0, IN), :])
+                total = dot_tn(xb[h, pl.ds(0, IN), :], dwide[0, pl.ds(0, IN), :])
                 for m in range(1, MICRO):
-                    total += dot_tn(xb[2 * m + h, pl.ds(0, IN), :], rbig[m, pl.ds(0, IN), :])
+                    total += dot_tn(xb[2 * m + h, pl.ds(0, IN), :], dwide[m, pl.ds(0, IN), :])
                 keep_narrow(h * W, total)
             red = flat(n1 * LANES)
             launch(red)
@@ -662,9 +730,12 @@
             red.relay(everything)
             finish_flat(red)
             finals()
-            arrived(ngr.at[0, 0], stn_r.at[0])
-            ng_o[0] = ngr[0, 0]
-            ship_all(w1_here, w1_at, 2, lambda copy: copy.wait_send())
+            for slot in range(2 * MICRO):
+                drain_a(slot)
+            for q in halves(2):
+                ship(w1_here, w1_at, q, w_s, 1).wait_send()
+            for q in halves(NQ):
+                ship(w3_between, w3_at, q, big_s, 3).wait_send()
             nt_copy(1).wait_send()
             for m in range(MICRO):
                 pushed(*main_copy(m))
@@ -672,23 +743,19 @@
 
         @pl.when(me_p == 1)
         def _():
-            A2, D2, D1 = MICRO, MICRO + 1, MICRO + 2
+            A2, D2 = MICRO, MICRO + 1
             fetch_narrow(n2)
             load_x.wait()
             take(w1_at, 2)
             arrived(nt2.at[pl.ds(0, 1)], nt_r)
 
             def first(m, c):
-                fw[m, pl.ds(0, IN), :] = dot(xb[2 * m, pl.ds(0, IN), :], weight(n2)) + dot(
-                    xb[2 * m + 1, pl.ds(0, IN), :], weight(n2 + W)
-                )
-                put(own_a, m, reduce_rows(1, runs_in, squares(lambda b, f: fw[m, rows(f), :]), 2))
-                send_a(m)
+                section_0(m, n2)
                 return c
 
             lax.fori_loop(0, MICRO, first, 0)
 
-            def conv(m):
+            def windows(m, c):
                 finish_norm(total_a(m), m, nt2, 0, count_in)
 
                 def act(b, f, bc, vc):
@@ -697,18 +764,21 @@
 
                 map_rows(1, runs_in, act)
                 col[:, m] = dot(p2[...], stage[m, pl.ds(0, IN), :]).astype(BF).reshape(9, OUT, W)
-                total = dot(col[0, m], weight(0))
-                for tap in range(1, 9):
-                    total += dot(col[tap, m], weight(tap * C_MID))
-                fw[A2, block(m), :] = total
+                return c
+
+            def conv(tap, c):
+                fw[A2, full, :] += dot(col[tap].reshape(ROWS, W), weight(tap * C_MID))
+                return c
+
+            def conv_sums(m, c):
                 put(own_a, MICRO + m, reduce_rows(1, runs_out, squares(lambda b, f: fw[A2, at(m, f), :]), 2))
                 send_a(MICRO + m)
-
-            def a2_copy(m, p):
-                sems = sm_s if p == 2 else sm_t
-                return (ssm.at[m], rsm.at[my_m], sems.at[m], sm_r.at[my_m], p, m * G + my_c)
-
-            def give(m):
+                return c
+
+            def a2_copy(m):
+                return remote(ssm.at[m], rsm.at[my_m], sm_s.at[m], sm_r.at[my_m], 3, m * G + my_c)
+
+            def give(m, c):
                 slot = MICRO + m
                 finish_norm(total_a(slot), slot, nt, 0, count_out)
 
@@ -717,21 +787,14 @@
                     ssm[m, rows(f), :] = kept(n * sigmoid(n), m, bc).astype(BF)
 
                 map_rows(1, runs_out, act)
-                push(*a2_copy(m, 3))
-                push(*a2_copy(m, 2))
-
-            def forward(step, c):
-                @pl.when(step < MICRO)
-                def _():
-                    conv(step)
-
-                @pl.when(step > 0)
-                def _():
-                    give(step - 1)
-
-                return c
-
-            lax.fori_loop(0, MICRO + 1, forward, 0)
+                a2_copy(m).start()
+                return c
+
+            lax.fori_loop(0, MICRO, windows, 0)
+            fw[A2, full, :] = dot(col[0].reshape(ROWS, W), weight(0))
+            lax.fori_loop(1, 9, conv, 0)
+            lax.fori_loop(0, MICRO, conv_sums, 0)
+            lax.fori_loop(0, MICRO, give, 0)
 
             def back_two(m):
                 arrived(rsm.at[m], sm_r.at[m])
@@ -758,51 +821,28 @@
 
                 map_rows(1, runs_out, grad)
 
-            def back_one(m):
-                du = dwide[0, block(m), :]
-                for tap in range(9):
-                    tgb[tap, pl.ds(0, OUT), :] = dot_nt(du, weight(tap * C_MID)).astype(BF)
-                taps = tgb[:, pl.ds(0, OUT), :].reshape(9 * OUT, W)
+            def back_taps(tap, c):
+                tgb[tap, full, :] = dot_nt(dwide[0, full, :], weight(tap * C_MID)).astype(BF)
+                return c
+
+            def back_one(m, c):
+                taps = tgb[:, block(m), :].reshape(9 * OUT, W)
                 stage[m, pl.ds(0, IN), :] = dot_tn(p2[...], taps).astype(BF)
-
-                def sums(b, f, bc, vc):
-                    u = fw[m, rows(f), :]
-                    d = kept(stage[m, rows(f), :].astype(F32) * slope_of(normed(u, m, bc)), m, bc)
-                    fw[D1 + m, rows(f), :] = d
-                    return (d, d * centered(u, m, bc))
-
-                put(own_a, 3 * MICRO + m, reduce_rows(1, runs_in, sums, 2))
-                send_a(3 * MICRO + m)
-
-            def du1_copy(m):
+                da1_copy(m).start()
+                return c
+
+            def da1_copy(m):
                 ref = pl.ds(0, IN)
                 return remote(stage.at[m, ref], rbig.at[m, ref], big_s.at[m], big_r.at[m], 0, me_d)
-
-            def back_out(m):
-                total = total_a(3 * MICRO + m)
-                put_cof(0, total, count_in)
-                add_norm_grads(ngs, 0, total)
-
-                def grad(b, f, bc, vc):
-                    z = centered(fw[m, rows(f), :], m, bc)
-                    stage[m, rows(f), :] = back(fw[D1 + m, rows(f), :], z, 0, 0, m, bc, vc)
-
-                map_rows(1, runs_in, grad)
-                du1_copy(m).start()
 
             def backward(step, c):
                 @pl.when(step < MICRO)
                 def _():
                     back_two(step)
 
-                @pl.when((step > 0) & (step <= MICRO))
+                @pl.when(step > 0)
                 def _():
                     back_mid(step - 1)
-                    back_one(step - 1)
-
-                @pl.when(step > 1)
-                def _():
-                    back_out(step - 2)
 
                 return c
 
@@ -810,21 +850,21 @@
                 keep_narrow(tap * C_MID, dot_tn(col[tap].reshape(ROWS, W), dwide[0, full, :]))
                 return c
 
-            lax.fori_loop(0, MICRO + 2, backward, 0)
-            ng_copy().start()
+            lax.fori_loop(0, MICRO + 1, backward, 0)
+            lax.fori_loop(0, 9, back_taps, 0)
+            lax.fori_loop(0, MICRO, back_one, 0)
             lax.fori_loop(0, 9, weights, 0)
             red = flat(n2 * LANES)
-            launch(red)
+            red.send_pairs(everything)
+            red.originate(everything)
             red.relay(everything)
             finals()
             finish_flat(red)
             pass_on(w1_at, 2, lambda ref, q, copy: copy.wait_send())
-            ng_copy().wait_send()
             for m in range(MICRO):
-                du1_copy(m).wait_send()
-                pushed(*a2_copy(m, 2))
-                pushed(*a2_copy(m, 3))
-            for slot in range(4 * MICRO):
+                da1_copy(m).wait_send()
+                a2_copy(m).wait_send()
+            for slot in range(3 * MICRO):
                 drain_a(slot)
 
         def share_copy(k):
@@ -850,7 +890,8 @@
 
         @pl.when(me_p == 2)
         def _():
-            ship_all(w3_here, w3_at, NQ, lambda copy: copy.start())
+            for q in halves(NQ):
+                ship(w3_here, w3_between, q, w_s, 0).start()
             nt_copy(NQ).start()
             load_x.wait()
 
@@ -1005,7 +1046,8 @@
 
             weights_out()
             red.drain()
-            ship_all(w3_here, w3_at, NQ, lambda copy: copy.wait_send())
+            for q in halves(NQ):
+                ship(w3_here, w3_between, q, w_s, 0).wait_send()
             nt_copy(NQ).wait_send()
             for k in range(MICRO):
                 sub_hop(k).wait_send()
@@ -1059,15 +1101,6 @@
             def w3(q):
                 return weight(nabc + q * C_MID)
 
-            def accumulate(index, i, value):
-                @pl.when(i == 0)
-                def _():
-                    fw[index, full, :] = value
-
-                @pl.when(i > 0)
-                def _():
-                    fw[index, full, :] += value
-
             def begin(index, slot):
                 put(own_b, slot, reduce_rows(MICRO, runs_out, squares(lambda b, f: fw[index, at(b, f), :]), 2))
                 send_b(slot)
@@ -1086,8 +1119,12 @@
 
                 lax.fori_loop(0, MICRO, one, 0)
 
+            def a2_on(k):
+                return remote(rsm.at[k], rsm.at[k], sm_t.at[k], sm_r.at[k], 2, me_d)
+
             for k in range(MICRO):
                 arrived(rsm.at[k], sm_r.at[k])
+                a2_on(k).start()
 
             def main(q, c):
                 fw[U3 + q, full, :] = dot(rsm[...].reshape(ROWS, W), w3(q))
@@ -1105,10 +1142,10 @@
                     rbig[q, at(b, f), :] = (n * sigmoid(n)).astype(BF)
 
                 map_rows(MICRO, runs_out, act)
-                accumulate(A, q, dot(rbig[q, full, :], wa(q)))
                 return c
 
             lax.fori_loop(0, NQ, join, 0)
+            fw[A, full, :] = sum(dot(rbig[q, full, :], wa(q)) for q in range(NQ))
             begin(A, 0)
             finish_norm(total_b(0), 0, nt, 0, count_out)
             hidden(A, 0, H1)
@@ -1118,11 +1155,7 @@
 
             gather(H1, to_col)
 
-            def conv(tap, c):
-                accumulate(B, tap, dot(col[tap].reshape(ROWS, W), wb(tap)))
-                return c
-
-            lax.fori_loop(0, 9, conv, 0)
+            fw[B, full, :] = sum(dot(col[tap].reshape(ROWS, W), wb(tap)) for tap in range(9))
             begin(B, 1)
             finish_norm(total_b(1), 1, nt, 1, count_out)
             hidden(B, 1, H2)
@@ -1172,10 +1205,10 @@
                     dwide[q, at(b, f), :] = back(d, z, 0, 0, 2 + q, bc, vc)
 
                 map_rows(MICRO, runs_out, grad)
-                accumulate(T1, q, dot_nt(dwide[q, full, :], wc(q)))
                 return c
 
             lax.fori_loop(0, NQ, ends_back, 0)
+            fw[T1, full, :] = sum(dot_nt(dwide[q, full, :], wc(q)) for q in range(NQ))
             for k in range(MICRO):
                 push(*out_copy(k))
 
@@ -1205,11 +1238,7 @@
 
             gather(DB, to_taps)
 
-            def conv_back(tap, c):
-                accumulate(T1, tap, dot_nt(tgb[tap, full, :], wb(8 - tap)))
-                return c
-
-            lax.fori_loop(0, 9, conv_back, 0)
+            fw[T1, full, :] = sum(dot_nt(tgb[tap, full, :], wb(8 - tap)) for tap in range(9))
             middle(A, 0, 3 + 2 * NQ, DA)
 
             def dy_copy(q):
@@ -1242,10 +1271,10 @@
                     xb[q, at(b, f), :] = back(fw[q, at(b, f), :], z, 0, 0, PM + q, bc, vc)
 
                 map_rows(MICRO, runs_out, grad)
-                accumulate(T1, q, dot_nt(xb[q, full, :], w3(q)))
                 return c
 
             lax.fori_loop(0, NQ, through_w3, 0)
+            fw[T1, full, :] = sum(dot_nt(xb[q, full, :], w3(q)) for q in range(NQ))
 
             def da2_copy(k):
                 return remote(ssm.at[k], rsm.at[my_m], sm_s.at[k], sm_r.at[my_m], 1, k * G + my_c)
@@ -1288,6 +1317,7 @@
                 pushed(*cot_copy(m))
                 pushed(*out_copy(m))
                 da2_copy(m).wait_send()
+                a2_on(m).wait_send()
             for q in range(NQ):
                 dy_copy(q).wait_send()
             for slot in range(S3 + 2 * NQ):
@@ -1355,7 +1385,7 @@
         V, D = pltpu.VMEM, pltpu.SemaphoreType.DMA
         RA, RB = radix(R, 8), radix(G, 4)
         nb, sb, ns, ss = geo.crops[0], geo.sides[0], geo.crops[1], geo.sides[1]
-        SA, SB = 4 * MICRO, 4 + 4 * NQ
+        SA, SB = 3 * MICRO, 4 + 4 * NQ
 
         def sums(slots, first, all_of):
             later = max(all_of // first - 1, 1)
@@ -1381,7 +1411,7 @@
             out_specs=(vmem, vmem, vmem, vmem, hbm, vmem),
             scratch_shapes=[
                 V((PW // W + C_OUT, W), BF),
-                V((2, LANES, 128, 1, 128), BF),
+                V((4, LANES, 128, 1, 128), BF),
                 V((2 * MICRO, wide, W), BF),
                 V((MICRO, OUT, 128), F32),
                 V((MICRO, OUT, 128), F32),
@@ -1409,7 +1439,7 @@
                 V((NB, 4, W), F32),
                 V((MICRO - 1, NB, 4, W), F32),
                 D((2,)),
-                D((2, LANES)),
+                D((4, LANES)),
                 D((4,)), D((4,)),
                 D((4,)), D((4,)), D((4,)),
                 D((4,)), D((4,)),

time: 222 us -> 211 us (0.950)
  the two profiles are of different devices: /device:TPU:10 before, /device:TPU:0 now
where the time goes in v3:
time: 211 us; the launch traced here: 210 us
  Pallas kernels  201 us (95%)
  local copies, waits for them, and re-layouts  5.82 us (3%)
  other arithmetic  2.13 us (1%)
    pallas_call x1, Pallas kernels, on_device(): pl.pallas_call(make_kernel(geo, R, NP, MICRO, SR, PC), out_shape=(jax.Sha...  197 us

profile of v3, /device:TPU:0, one launch (start us, length us, event | category | flops | bytes accessed | tf_op | source)
XLA Modules:
  0.0 209.7 jit_solution(9987007984576462552)
XLA Ops:
  0.6 0.0 copy-start.1
  0.6 1.2 copy.21
  1.8 0.2 copy.23
  2.0 2.0 reshape.56
  4.0 0.0 copy-done.1
  4.0 0.4 copy.22
  4.5 0.0 copy-start
  4.5 0.2 fusion.5
  4.7 1.2 copy.27
  5.9 0.2 copy-done
  6.1 0.5 copy.20
  6.6 0.4 fusion.4
  7.0 0.2 fusion.6
  7.1 1.5 pad_maximum_fusion
  8.7 197.3 %shard_map.163 = (bf16[7,7,2048]{2,1,0:T(8,128)(2,1)}, bf16[9,2,2048]{2,1,0:T(2,128)(2,1)}, bf16[14,14,1024]{2,1,0:T(8,128)(2,1)}, bf16[36,2,1024]{2,1,0:T(2,128...) custom-call(bf16[8,272,512]{2,1,0:T(8,128)(2,1)} %bitcast.38, bf16[4,4,80,512]{3,2,1,0:T(8,128)(2,1)} %bitcast.39, ...), custom_call_target="tpu_custom_call" | custom-call | tf_op jit(solution)/shard_map/pallas_call | solution.py:1400
  206.0 3.7 %shard_map.164 = (bf16[7,7,2048]{2,1,0:T(8,128)(2,1)}, bf16[9,2,2048]{2,1,0:T(2,128)(2,1)}, bf16[14,14,1024]{2,1,0:T(8,128)(2,1)}, bf16[36,2,1024]{2,1,0:T(2,128...) custom-call(bf16[7,7,2048]{2,1,0:T(8,128)(2,1)} %get-tuple-element.18.refs_0_, ...), custom_call_target="tpu_custom_call" | custom-call | tf_op jit(solution)/shard_map/pallas_call | solution.py:1343
Async XLA Ops:
  0.6 3.4 %copy-start.1 = (bf16[4,1,7,7,2048]{4,0,3,2,1:T(4,128)(2,1)S(1)}, bf16[4,1,7,7,2048]{4,0,3,2,1:T(4,128)(2,1)}, u32[]{:S(2)}) copy-start(bf16[4,1,7,7,2048]{4,0,3,2,1:T(4,128)(2,1)} %param.14) | copy-start | bytes 2408452
  4.5 1.6 copy-start

commit v4 on v3

--- a/solution.py
+++ b/solution.py
@@ -563,35 +563,43 @@
 
         everything = range(PC)
 
-        def flat(used_rows):
+        def flat(used_rows, pieces=PC):
+            PR = SR // pieces
             filled = -(-used_rows // PR) * PR
             if filled > used_rows:
                 dwl[pl.ds(used_rows, filled - used_rows), :] = jnp.zeros((filled - used_rows, 128), BF)
-            return Reduction(PC, PR, lambda s, pc: s * SR + pc * PR, lambda s, pc: s * SR + pc * PR < used_rows)
+            return Reduction(pieces, PR, lambda s, pc: s * SR + pc * PR, lambda s, pc: s * SR + pc * PR < used_rows)
 
         def launch(red, low=0, high=N):
-            red.send_pairs(everything, low, high)
-            red.originate(everything, low, high)
+            red.send_pairs(range(red.pieces), low, high)
+            red.originate(range(red.pieces), low, high)
 
         def finish_flat(red):
             tmp[pl.ds(0, SR), :] = jnp.zeros((SR, 128), F32)
 
             def finish(pc):
                 def store(at_s, s, v):
-                    tmp[pl.ds(pl.multiple_of(pc * PR + s * red.step, CH), red.step), :] = v
+                    first = pc * red.rows_of + s * red.step
+                    tmp[pl.ds(pl.multiple_of(first, CH), red.step), :] = v
 
                 red.finish(pc, store)
 
-            red.each(everything, finish)
+            red.each(range(red.pieces), finish)
             weights_out()
             red.drain()
 
         barrier = pltpu.get_barrier_semaphore()
-        load_x = pltpu.make_async_copy(x_h, xb.at[:, pl.ds(0, IN)], ld.at[0])
+        loads_x = [
+            pltpu.make_async_copy(
+                x_h.at[:, :, pl.ds(h * W, W)], xb.at[pl.ds(h * MICRO, MICRO), pl.ds(0, IN)], ld.at[2 * h]
+            )
+            for h in range(2)
+        ]
 
         @pl.when(me_p < 3)
         def _():
-            load_x.start()
+            for copy in loads_x:
+                copy.start()
 
         def greet(i, c):
             p, d = i // R, lax.rem(i, R)
@@ -655,8 +663,8 @@
             return pl.multiple_of(q * W, W)
 
         def section_0(m, first):
-            fw[m, pl.ds(0, IN), :] = dot(xb[2 * m, pl.ds(0, IN), :], weight(first)) + dot(
-                xb[2 * m + 1, pl.ds(0, IN), :], weight(first + W)
+            fw[m, pl.ds(0, IN), :] = dot(xb[m, pl.ds(0, IN), :], weight(first)) + dot(
+                xb[MICRO + m, pl.ds(0, IN), :], weight(first + W)
             )
             put(own_a, m, reduce_rows(1, runs_in, squares(lambda b, f: fw[m, rows(f), :]), 2))
             send_a(m)
@@ -669,7 +677,8 @@
             for q in halves(NQ):
                 arrived(wbuf.at[pl.ds(w3_between(q), W)], w_r.at[q])
                 ship(w3_between, w3_at, q, big_s, 3).start()
-            load_x.wait()
+            for copy in loads_x:
+                copy.wait()
 
             def first(m, c):
                 section_0(m, 0)
@@ -678,6 +687,8 @@
             lax.fori_loop(0, MICRO, first, 0)
             for m in range(MICRO):
                 finish_norm(total_a(m), m, nt, 0, count_in)
+
+            tmp[pl.ds(0, n1 * LANES), :] = jnp.zeros((n1 * LANES, 128), F32)
 
             def back_sums(m):
                 arrived(rbig.at[m, pl.ds(0, IN)], big_r.at[m])
@@ -704,6 +715,11 @@
                 for h in range(2):
                     tgb[2 * m + h, pl.ds(0, IN), :] = dot_nt(dwide[m, pl.ds(0, IN), :], weight(h * W)).astype(BF)
                 push(*main_copy(m))
+                for h in range(2):
+                    grad = dot_tn(xb[h * MICRO + m, pl.ds(0, IN), :], dwide[m, pl.ds(0, IN), :])
+                    for lane in range(LANES):
+                        at_l = pl.ds(h * W * LANES + lane, W, stride=LANES)
+                        tmp[at_l, :] += grad[:, lane * 128 : (lane + 1) * 128]
 
             def backward(step, c):
                 @pl.when(step < MICRO)
@@ -717,17 +733,13 @@
                 return c
 
             lax.fori_loop(0, MICRO + 1, backward, 0)
-            for h in range(2):
-                total = dot_tn(xb[h, pl.ds(0, IN), :], dwide[0, pl.ds(0, IN), :])
-                for m in range(1, MICRO):
-                    total += dot_tn(xb[2 * m + h, pl.ds(0, IN), :], dwide[m, pl.ds(0, IN), :])
-                keep_narrow(h * W, total)
-            red = flat(n1 * LANES)
+            dwl[pl.ds(0, n1 * LANES), :] = tmp[pl.ds(0, n1 * LANES), :].astype(BF)
+            red = flat(n1 * LANES, 2 * PC if PR % (2 * CH) == 0 else PC)
             launch(red)
             for k in range(MICRO):
                 arrived(col.at[pl.ds(6, 2), k], xs_r.at[k])
                 push(*sub_back(k))
-            red.relay(everything)
+            red.relay(range(red.pieces))
             finish_flat(red)
             finals()
             for slot in range(2 * MICRO):
@@ -745,7 +757,8 @@
         def _():
             A2, D2 = MICRO, MICRO + 1
             fetch_narrow(n2)
-            load_x.wait()
+            for copy in loads_x:
+                copy.wait()
             take(w1_at, 2)
             arrived(nt2.at[pl.ds(0, 1)], nt_r)
 
@@ -851,9 +864,11 @@
                 return c
 
             lax.fori_loop(0, MICRO + 1, backward, 0)
-            lax.fori_loop(0, 9, back_taps, 0)
+            for tap in range(9):
+                back_taps(tap, 0)
             lax.fori_loop(0, MICRO, back_one, 0)
-            lax.fori_loop(0, 9, weights, 0)
+            for tap in range(9):
+                weights(tap, 0)
             red = flat(n2 * LANES)
             red.send_pairs(everything)
             red.originate(everything)
@@ -893,11 +908,12 @@
             for q in halves(NQ):
                 ship(w3_here, w3_between, q, w_s, 0).start()
             nt_copy(NQ).start()
-            load_x.wait()
+            for copy in loads_x:
+                copy.wait()
 
             def send_x(m, c):
                 for h in range(2):
-                    col[4 + h, m] = dot(ps[...], xb[2 * m + h, pl.ds(0, IN), :]).astype(BF)
+                    col[4 + h, m] = dot(ps[...], xb[h * MICRO + m, pl.ds(0, IN), :]).astype(BF)
                 push(*sub_copy(m))
                 return c
 
@@ -1056,8 +1072,12 @@
             for slot in range(4 * NQ):
                 drain_b(slot)
 
-        def cot_copy(m):
-            return (cot_h.at[m], xb.at[pl.ds(0, NQ), block(my_m)], ct_s.at[m], ct_r.at[my_m], 3, m * G + my_c)
+        def cot_copy(m, q):
+            src, dst = cot_h.at[m, :, pl.ds(q * W, W)], xb.at[q, block(my_m)]
+            return (src, dst, ct_s.at[m], ct_r.at[my_m], 3, m * G + my_c)
+
+        def cot_all(m):
+            return (cot_h.at[m], cot_h.at[m], ct_s.at[m], ct_r.at[my_m], 3, m * G + my_c)
 
         def gate_copy(m):
             return (gate_v.at[m], gateb.at[my_m], gt_s.at[m], gt_r.at[my_m], 3, m * G + my_c)
@@ -1080,7 +1100,8 @@
                 gate_v[m] = g
             for m in range(MICRO):
                 push(*gate_copy(m))
-                push(*cot_copy(m))
+                for q in range(NQ):
+                    push(*cot_copy(m, q))
             fetch_narrow(nab)
             fetch_wide(nab * W // C_OUT, C_MID, lambda q: nab + q * C_MID)
             take(w3_at, NQ)
@@ -1160,8 +1181,10 @@
             finish_norm(total_b(1), 1, nt, 1, count_out)
             hidden(B, 1, H2)
 
+            for q in range(NQ):
+                fw[q, full, :] = dot(dwide[H2, full, :], wc(q))
+
             def widen(q, c):
-                fw[q, full, :] = dot(dwide[H2, full, :], wc(q))
                 begin(q, 2 + q)
                 return c
 
@@ -1244,11 +1267,12 @@
             def dy_copy(q):
                 return remote(stage.at[q, full], rbig.at[q, full], big_s.at[q], big_r.at[q], 2, me_d)
 
+            for q in range(NQ):
+                fw[NQ + q, full, :] += dot_nt(dwide[DA, full, :], wa(q))
+
             def to_y(q, c):
-                fw[T2, full, :] = dot_nt(dwide[DA, full, :], wa(q))
-
                 def sums(b, f, bc, vc):
-                    dy = (fw[T2, at(b, f), :] + fw[NQ + q, at(b, f), :]).astype(BF)
+                    dy = fw[NQ + q, at(b, f), :].astype(BF)
                     u = fw[U3 + q, at(b, f), :]
                     n = normed(u, PM + q, bc) + stage[q, at(b, f), :].astype(F32)
                     stage[q, at(b, f), :] = dy
@@ -1314,7 +1338,7 @@
             pass_on(w3_at, NQ, lambda ref, q, copy: copy.wait_send())
             for m in range(MICRO):
                 pushed(*gate_copy(m))
-                pushed(*cot_copy(m))
+                pushed(*cot_all(m))
                 pushed(*out_copy(m))
                 da2_copy(m).wait_send()
                 a2_on(m).wait_send()
@@ -1366,8 +1390,7 @@
             return jnp.pad(v, ((0, 0), (0, length - v.shape[1]), (0, 0)))
 
         x = joined(x_big, x_small, C_IN, IN)
-        x = x.reshape(MICRO, IN, 2, W).transpose(0, 2, 1, 3).reshape(2 * MICRO, IN, W)
-        cot = joined(cot_big, cot_small, C_OUT, OUT).reshape(MICRO, OUT, NQ, W).transpose(0, 2, 1, 3)
+        cot = joined(cot_big, cot_small, C_OUT, OUT)
         w4 = section_weights.reshape(PW // W, LANES, 1, 128)
         w16 = section_weights.reshape(PW // C_OUT, NQ * LANES, 1, 128)
         SR = PW // 128 // R
@@ -1438,7 +1461,7 @@
                 V((2, 4, W), F32),
                 V((NB, 4, W), F32),
                 V((MICRO - 1, NB, 4, W), F32),
-                D((2,)),
+                D((3,)),
                 D((4, LANES)),
                 D((4,)), D((4,)),
                 D((4,)), D((4,)), D((4,)),
@@ -1454,8 +1477,8 @@
                 D((SA,)), D((SA,)), D((SA,)), D((SA,)),
                 D((SB,)), D((SB,)), D((SB,)), D((SB,)),
                 D((MICRO - 1,)), D((MICRO - 1,)),
-                D((R // 2, 4)), D((R // 2, 4)),
-                D((R // 2, 4)), D((R // 2 + 1, 4)),
+                D((R // 2, 8)), D((R // 2, 8)),
+                D((R // 2, 8)), D((R // 2 + 1, 8)),
             ],
             compiler_params=pltpu.CompilerParams(
                 collective_id=0, has_side_effects=True, vmem_limit_bytes=63 << 20

time: 211 us -> 207 us (0.981)
  Pallas kernels: 201 us -> 198 us
    pallas_call x1, Pallas kernels: 197 us -> 194 us  [on_device(): pl.pallas_call(make_kernel(geo, R, NP, MICRO, SR, PC), out_shape=(jax.Sha...]
    concatenate x2, other arithmetic: 0.59 us -> 3.01 us  [joined(): v = jnp.concatenate(parts, axis=1)]
where the time goes in v4:
time: 207 us; the launch traced here: 206 us
  Pallas kernels  198 us (96%)
  local copies, waits for them, and re-layouts  4.27 us (2%)
  other arithmetic  3.01 us (1%)
    pallas_call x1, Pallas kernels, on_device(): pl.pallas_call(make_kernel(geo, R, NP, MICRO, SR, PC), out_shape=(jax.Sha...  194 us

profile of v4, /device:TPU:0, one launch (start us, length us, event | category | flops | bytes accessed | tf_op | source)
XLA Modules:
  0.0 205.9 jit_solution(7218761034827200111)
XLA Ops:
  0.6 0.0 copy-start.1
  0.6 1.2 copy.21
  1.8 0.2 copy.23
  2.0 2.0 reshape.49
  4.0 0.0 copy-done.1
  4.0 0.0 copy-start
  4.0 0.4 copy.22
  4.5 1.3 fusion.5.cot_h
  5.7 0.0 copy-done
  5.7 0.5 copy.20
  6.2 1.8 fusion.4.x_h
  8.0 194.2 %shard_map.163 = (bf16[7,7,2048]{2,1,0:T(8,128)(2,1)}, bf16[9,2,2048]{2,1,0:T(2,128)(2,1)}, bf16[14,14,1024]{2,1,0:T(8,128)(2,1)}, bf16[36,2,1024]{2,1,0:T(2,128...) custom-call(bf16[4,272,1024]{2,1,0:T(8,128)(2,1)} %fusion.4.x_h, bf16[4,80,2048]{2,1,0:T(8,128)(2,1)} %fusion.5.cot_h, ...), custom_call_target="tpu_custom_call" | custom-call | tf_op jit(solution)/shard_map/pallas_call | solution.py:1423
  202.2 3.7 %shard_map.164 = (bf16[7,7,2048]{2,1,0:T(8,128)(2,1)}, bf16[9,2,2048]{2,1,0:T(2,128)(2,1)}, bf16[14,14,1024]{2,1,0:T(8,128)(2,1)}, bf16[36,2,1024]{2,1,0:T(2,128...) custom-call(bf16[7,7,2048]{2,1,0:T(8,128)(2,1)} %get-tuple-element.18.refs_0_, ...), custom_call_target="tpu_custom_call" | custom-call | tf_op jit(solution)/shard_map/pallas_call | solution.py:1367
Async XLA Ops:
  0.6 3.4 %copy-start.1 = (bf16[4,1,7,7,2048]{4,0,3,2,1:T(4,128)(2,1)S(1)}, bf16[4,1,7,7,2048]{4,0,3,2,1:T(4,128)(2,1)}, u32[]{:S(2)}) copy-start(bf16[4,1,7,7,2048]{4,0,3,2,1:T(4,128)(2,1)} %param.14) | copy-start | bytes 2408452
  4.0 1.7 copy-start

commit v5 on v4

--- a/solution.py
+++ b/solution.py
@@ -713,13 +713,13 @@
 
                 map_rows(1, runs_in, grad)
                 for h in range(2):
+                    piece = dot_tn(xb[h * MICRO + m, pl.ds(0, IN), :], dwide[m, pl.ds(0, IN), :])
+                    for lane in range(LANES):
+                        at_l = pl.ds(h * W * LANES + lane, W, stride=LANES)
+                        tmp[at_l, :] += piece[:, lane * 128 : (lane + 1) * 128]
+                for h in range(2):
                     tgb[2 * m + h, pl.ds(0, IN), :] = dot_nt(dwide[m, pl.ds(0, IN), :], weight(h * W)).astype(BF)
                 push(*main_copy(m))
-                for h in range(2):
-                    grad = dot_tn(xb[h * MICRO + m, pl.ds(0, IN), :], dwide[m, pl.ds(0, IN), :])
-                    for lane in range(LANES):
-                        at_l = pl.ds(h * W * LANES + lane, W, stride=LANES)
-                        tmp[at_l, :] += grad[:, lane * 128 : (lane + 1) * 128]
 
             def backward(step, c):
                 @pl.when(step < MICRO)
@@ -867,12 +867,16 @@
             for tap in range(9):
                 back_taps(tap, 0)
             lax.fori_loop(0, MICRO, back_one, 0)
-            for tap in range(9):
+            red = flat(n2 * LANES)
+            cut = 5 * C_MID * LANES // (2 * SR)
+            for tap in range(5):
                 weights(tap, 0)
-            red = flat(n2 * LANES)
-            red.send_pairs(everything)
-            red.originate(everything)
-            red.relay(everything)
+            launch(red, 0, cut)
+            for tap in range(5, 9):
+                weights(tap, 0)
+            launch(red, cut, N)
+            red.relay(everything, 0, cut)
+            red.relay(everything, cut, N)
             finals()
             finish_flat(red)
             pass_on(w1_at, 2, lambda ref, q, copy: copy.wait_send())
@@ -1358,17 +1362,34 @@
 
 def handed_on(arrays):
     count = len(arrays)
+    jobs = []
+    for i, a in enumerate(arrays):
+        parts = 4 if a.ndim == 2 and a.shape[0] % 32 == 0 else 1
+        jobs += [(i, k * (a.shape[0] // parts), a.shape[0] // parts) for k in range(parts)]
 
     def kernel(*refs):
-        for i in range(count):
-            refs[count + i][...] = refs[i][...]
-
-    vmem = pl.BlockSpec(memory_space=pltpu.VMEM)
+        held, sems = refs[2 * count : 3 * count], refs[-1]
+
+        def move(n, src, dst):
+            i, first, length = jobs[n]
+            part_of = pl.ds(first, length)
+            return pltpu.make_async_copy(src[i].at[part_of], dst[i].at[part_of], sems.at[n])
+
+        for n in range(len(jobs)):
+            move(n, refs[:count], held).start()
+        for n in range(len(jobs)):
+            move(n, refs[:count], held).wait()
+            move(n, held, refs[count : 2 * count]).start()
+        for n in range(len(jobs)):
+            move(n, held, refs[count : 2 * count]).wait()
+
+    hbm = pl.BlockSpec(memory_space=pl.ANY)
     return pl.pallas_call(
         kernel,
         out_shape=tuple(jax.ShapeDtypeStruct(a.shape, a.dtype) for a in arrays),
-        in_specs=[vmem] * count,
-        out_specs=(vmem,) * count,
+        in_specs=[hbm] * count,
+        out_specs=(hbm,) * count,
+        scratch_shapes=[pltpu.VMEM(a.shape, a.dtype) for a in arrays] + [pltpu.SemaphoreType.DMA((len(jobs),))],
     )(*arrays)
 
 

time: 207 us -> 206 us (level)
  no operation moved by 1% of the time
where the time goes in v5:
time: 206 us; the launch traced here: 205 us
  Pallas kernels  197 us (96%)
  local copies, waits for them, and re-layouts  4.27 us (2%)
  other arithmetic  3.01 us (1%)
    pallas_call x1, Pallas kernels, on_device(): pl.pallas_call(make_kernel(geo, R, NP, MICRO, SR, PC), out_shape=(jax.Sha...  194 us

profile of v5, /device:TPU:0, one launch (start us, length us, event | category | flops | bytes accessed | tf_op | source)
XLA Modules:
  0.0 205.1 jit_solution(11190250677595876784)
XLA Ops:
  0.6 0.0 copy-start.1
  0.6 1.2 copy.21
  1.8 0.2 copy.23
  2.0 2.0 reshape.49
  4.0 0.0 copy-done.1
  4.0 0.0 copy-start
  4.0 0.4 copy.22
  4.5 1.3 fusion.5.cot_h
  5.7 0.0 copy-done
  5.7 0.5 copy.20
  6.2 1.8 fusion.4.x_h
  8.0 194.0 %shard_map.163 = (bf16[7,7,2048]{2,1,0:T(8,128)(2,1)}, bf16[9,2,2048]{2,1,0:T(2,128)(2,1)}, bf16[14,14,1024]{2,1,0:T(8,128)(2,1)}, bf16[36,2,1024]{2,1,0:T(2,128...) custom-call(bf16[4,272,1024]{2,1,0:T(8,128)(2,1)} %fusion.4.x_h, bf16[4,80,2048]{2,1,0:T(8,128)(2,1)} %fusion.5.cot_h, ...), custom_call_target="tpu_custom_call" | custom-call | tf_op jit(solution)/shard_map/pallas_call | solution.py:1444
  202.0 2.9 %shard_map.164 = (bf16[7,7,2048]{2,1,0:T(8,128)(2,1)}, bf16[9,2,2048]{2,1,0:T(2,128)(2,1)}, bf16[14,14,1024]{2,1,0:T(8,128)(2,1)}, bf16[36,2,1024]{2,1,0:T(2,128...) custom-call(bf16[7,7,2048]{2,1,0:T(8,128)(2,1)} %get-tuple-element.18.refs_0_, ...), custom_call_target="tpu_custom_call" | custom-call | tf_op jit(solution)/shard_map/pallas_call | solution.py:1387
Async XLA Ops:
  0.6 3.4 %copy-start.1 = (bf16[4,1,7,7,2048]{4,0,3,2,1:T(4,128)(2,1)S(1)}, bf16[4,1,7,7,2048]{4,0,3,2,1:T(4,128)(2,1)}, u32[]{:S(2)}) copy-start(bf16[4,1,7,7,2048]{4,0,3,2,1:T(4,128)(2,1)} %param.14) | copy-start | bytes 2408452
  4.0 1.7 copy-start
